TPU v7x, 32 devices: a whole 2x2x4 slice. The times are simulated.
32 devices in a mesh: gx: 4 (over y, core), gy: 8 (over z, x).
Axes of the slice: x: 2, y: 2, z: 4, core: 2. Of those that a mesh axis runs over, the one named last changes fastest.
Arguments:
- tensor: float32 [2048, 1024, 32], P('gx', 'gy'), may hold values from -6 to 6
- factor_two: float32 [1024, 64], P('gy', 'gx'), may hold values from -0.1875 to 0.1875
- factor_three: float32 [32, 64], replicated, may hold values from -1 to 1
Outputs:
- factor_one: float32 [2048, 64], P(('gx', 'gy'))
All inputs are finite; a program needn't handle non-finite values.
Results may differ from a plain program's by a relative error of at most 0.000098.
Values sent between devices are 32-bit elements; how exact they have to be, the bound alone decides.
No kernel may reach another device: no remote copies, remote signals or barrier semaphores. Data moves between devices by JAX's collectives and lax.ppermute only.
A program may use at most 64 MiB of HBM per device.

v0:
```python
import jax
import jax.numpy as jnp
from jax import lax
from jax.sharding import PartitionSpec as P


def factorize(normal):
    order = normal.shape[0]
    places = jnp.arange(order, dtype=jnp.int32)

    def column_step(index, lower):
        target = lax.dynamic_slice_in_dim(normal, index, 1, 1)[:, 0]
        lower_row = lax.dynamic_slice_in_dim(lower, index, 1, 0)[0]
        remain = target - jnp.dot(lower, lower_row, precision=lax.Precision.HIGHEST)
        pivot = jnp.sqrt(jnp.sum(jnp.where(places == index, remain, 0.0)))
        column = jnp.where(places >= index, remain / pivot, 0.0)
        return lax.dynamic_update_slice_in_dim(lower, column[:, None], index, 1)

    return lax.fori_loop(0, order, column_step, jnp.zeros_like(normal))


def solve_lower(lower, right):
    order = lower.shape[0]

    def row_step(index, result):
        lower_row = lax.dynamic_slice_in_dim(lower, index, 1, 0)
        pivot = lax.dynamic_slice(lower, (index, index), (1, 1))
        target = lax.dynamic_slice_in_dim(right, index, 1, 0)
        value = (target - jnp.dot(lower_row, result, precision=lax.Precision.HIGHEST)) / pivot
        return lax.dynamic_update_slice_in_dim(result, value, index, 0)

    return lax.fori_loop(0, order, row_step, jnp.zeros_like(right))


def solve_upper(lower, right):
    order = lower.shape[0]

    def row_step(count, result):
        index = order - 1 - count
        lower_col = lax.dynamic_slice_in_dim(lower, index, 1, 1)[:, 0]
        pivot = lax.dynamic_slice(lower, (index, index), (1, 1))
        target = lax.dynamic_slice_in_dim(right, index, 1, 0)
        value = (
            target - jnp.dot(lower_col[None, :], result, precision=lax.Precision.HIGHEST)
        ) / pivot
        return lax.dynamic_update_slice_in_dim(result, value, index, 0)

    return lax.fori_loop(0, order, row_step, jnp.zeros_like(right))


def body(tensor, factor_two, factor_three):
    rows, width, depth = tensor.shape
    full_two = lax.all_gather(factor_two, "gx", axis=1, tiled=True)
    rank = full_two.shape[1]
    khatri = (full_two[:, None, :] * factor_three[None, :, :]).reshape(width * depth, rank)
    partial_value = jnp.dot(
        tensor.reshape(rows, width * depth), khatri, precision=lax.Precision.HIGHEST
    )
    local_gram = jnp.dot(full_two.T, full_two, precision=lax.Precision.HIGHEST)
    gram_three = jnp.dot(factor_three.T, factor_three, precision=lax.Precision.HIGHEST)
    owned = lax.psum_scatter(partial_value, "gy", scatter_dimension=0, tiled=True)
    gram_two = lax.psum(local_gram, "gy")
    normal = gram_two * gram_three
    lower = factorize(normal)
    inner = solve_lower(lower, owned.T)
    return solve_upper(lower, inner).T


def solution(mesh):
    in_specs = (P("gx", "gy", None), P("gy", "gx"), P())
    out_specs = P(("gx", "gy"), None)
    return jax.shard_map(body, mesh=mesh, in_specs=in_specs, out_specs=out_specs, check_vma=False)
```

profile of v0, /device:TPU:0, one launch (start us, length us, event | category | flops | bytes accessed | tf_op | source)
XLA Modules:
  0.0 379.6 jit_solution(7282303145562202032)
XLA Ops:
  6.5 6.5 %all_gather.3 = f32[128,64]{0,1:T(8,128)S(1)} all-gather(f32[128,16]{0,1:T(8,128)} %param.10), channel_id=1, replica_groups=mesh['gx'=4,'gy'=8] {'gx'}, dimensions={1}, use_global_device_ids=true | all-gather | bytes 40960 | tf_op jit(solution)/shard_map/all_gather | solution.py:53
  13.1 14.6 %fusion.17 = f32[512,64]{0,1:T(8,128)S(1)} fusion(f32[512,128,32]{1,2,0:T(8,128)} %param.9, f32[32,64]{1,0:T(8,128)} %param.11, f32[128,64]{0,1:T(8,128)S(1)} %all_gather.3), kind=kOutput, calls=%fused_computation.21 | convolution fusion | flops 1610874880 | bytes 8560640 | tf_op jit(solution)/shard_map/dot_general | solution.py:56
  27.6 0.8 copy.14
  28.7 37.9 %psum.7 = f32[64,64]{1,0:T(8,128)S(1)} all-reduce(f32[64,64]{1,0:T(8,128)S(1)} %fusion.23), channel_id=1, replica_groups=mesh['gx'=4,'gy'=8] {'gy'}, use_global_device_ids=true, to_apply=%region_0.0 | all-reduce | flops 4096 | bytes 32768 | tf_op jit(solution)/shard_map/psum | solution.py:62
  66.9 107.2 %while.45 = (s32[]{:T(128)}, f32[64,64]{1,0:T(8,128)S(1)}, f32[64,64]{0,1:T(8,128)S(1)}, s32[]{:T(128)}, s32[]{:T(128)}) while((s32[]{:T(128)}, f32[64,64]{1,0:T(8,128)S(1)}, f32[64,64]{0,1:T(8,128)S(1)}, s32[]{:T(128)}, s32[]{:T(128)}) %tuple.95), condition=%wide.region_3.0_spmd.clone.clone, body=%wide.region_1.3_spmd.clone.clone.sunk | while | flops 49601 | bytes 37205 | solution.py:19
  174.2 0.8 copy.15
  175.0 98.3 %while.43 = (s32[]{:T(128)}, f32[64,64]{1,0:T(8,128)S(1)}, f32[64,64]{1,0:T(8,128)S(1)}, f32[64,64]{1,0:T(8,128)S(1)}, s32[]{:T(128)}, /*index=5*/s32[]{:T(128)}) while((s32[]{:T(128)}, f32[64,64]{1,0:T(8,128)S(1)}, f32[64,64]{1,0:T(8,128)S(1)}, f32[64,64]{1,0:T(8,128)S(1)}, s32[]{:T(128)}, /*index=5*/s32[]{:T(128)}) %tuple.106), condition=%wide.region_6.7_spmd, body=%wide.region_5.6_spmd.sunk | while | flops 49282 | bytes 36181 | solution.py:32
  175.7 0.8 fusion.42
  178.8 0.8 fusion.42
  181.8 0.8 fusion.42
  183.4 0.8 fusion.42
  184.9 0.8 fusion.42
  186.4 0.8 fusion.42
  188.0 0.8 fusion.42
  189.5 0.8 fusion.42
  191.0 0.8 fusion.42
  192.6 0.8 fusion.42
  194.1 0.8 fusion.42
  195.7 0.8 fusion.42
  197.2 0.8 fusion.42
  198.7 0.8 fusion.42
  200.3 0.8 fusion.42
  201.8 0.8 fusion.42
  204.9 0.8 fusion.42
  207.9 0.8 fusion.42
  211.0 0.8 fusion.42
  212.5 0.8 fusion.42
  214.1 0.8 fusion.42
  215.6 0.8 fusion.42
  217.2 0.8 fusion.42
  218.7 0.8 fusion.42
  220.2 0.8 fusion.42
  221.8 0.8 fusion.42
  223.3 0.8 fusion.42
  224.8 0.8 fusion.42
  226.4 0.8 fusion.42
  227.9 0.8 fusion.42
  229.4 0.8 fusion.42
  231.0 0.8 fusion.42
  234.0 0.8 fusion.42
  237.1 0.8 fusion.42
  240.2 0.8 fusion.42
  241.7 0.8 fusion.42
  243.3 0.8 fusion.42
  244.8 0.8 fusion.42
  246.3 0.8 fusion.42
  247.9 0.8 fusion.42
  249.4 0.8 fusion.42
  250.9 0.8 fusion.42
  252.5 0.8 fusion.42
  254.0 0.8 fusion.42
  255.6 0.8 fusion.42
  257.1 0.8 fusion.42
  258.6 0.8 fusion.42
  260.2 0.8 fusion.42
  263.2 0.8 fusion.42
  266.3 0.8 fusion.42
  269.4 0.8 fusion.42
  270.9 0.8 fusion.42
  272.4 0.8 fusion.42
  273.3 98.7 %while.44 = (s32[]{:T(128)}, f32[64,64]{1,0:T(8,128)S(1)}, f32[64,64]{1,0:T(8,128)S(1)}, f32[64,64]{0,1:T(8,128)S(1)}, s32[]{:T(128)}, /*index=5*/s32[]{:T(128)}, s32[]{:T(128)}, s32[]{:T(128)}) while((s32[]{:T(128)}, f32[64,64]{1,0:T(8,128)S(1)}, f32[64,64]{1,0:T(8,128)S(1)}, f32[64,64]{0,1:T(8,128)S(1)}, s32[]{:T(128)}, ...), condition=%wide.region_8.9_spmd, body=%wide.region_7.8_spmd.sunk | while | flops 49286 | bytes 35735 | solution.py:48
  274.0 0.8 fusion.45
  275.5 0.8 fusion.45
  277.1 0.8 fusion.45
  (597 shorter events, 216.8 us)
Async XLA Ops:
  6.5 60.0 %copy-start = (f32[32,64]{1,0:T(8,128)S(1)}, f32[32,64]{1,0:T(8,128)}, u32[]{:S(2)}) copy-start(f32[32,64]{1,0:T(8,128)} %param.11) | copy-start | bytes 24580
  6.5 167.6 %reduce-scatter.4.cloned.1.call-start = ((), (), s32[]{:S(2)}) async-start(), calls=%async_computation.1 | async-start | bytes 294912
Sparse Core Ops, SparseCore 0:
  28.6 63.6 reduce-scatter.3
where the time goes:
time: 382 us; the launch traced here: 380 us
  matrix products  168 us (44%)
  local copies, waits for them, and re-layouts  111 us (29%)
  blocking collectives  44.4 us (12%)
  loops' own time  42.5 us (11%)
  between operations  13.5 us (4%)
    dynamic_slice x128, local copies, waits for them, and re-layouts, row_step(): pivot = lax.dynamic_slice(lower, (index, index), (1, 1))  85.5 us
    dot_general x64, matrix products, row_step(): jnp.dot(lower_col[None, :], result, precision=lax.Precision.HIGHEST)  52.8 us
    dot_general x64, matrix products, row_step(): jnp.dot(lower_row, result, precision=lax.Precision.HIGHEST)  52.8 us
    dot_general x64, matrix products, column_step(): remain = target - jnp.dot(lower, lower_row, precision=lax.Precision.HIGHEST)  47.4 us
    another operation x1, loops' own time, factorize(): return lax.fori_loop(0, order, column_step, jnp.zeros_like(normal))  39.9 us
    psum x1, blocking collectives, body(): gram_two = lax.psum(local_gram, 'gy')  37.9 us
    dot_general x1, matrix products, body(): jnp.dot(tensor.reshape(rows, width * depth), khatri, precision=lax.Precis...  14.6 us
    dynamic_update_slice x64, local copies, waits for them, and re-layouts, column_step(): return lax.dynamic_update_slice_in_dim(lower, column[:, None], index, 1)  13.3 us
  transfers between devices with their start and end apart: 1, of which 0 were waited for; matrix products, arithmetic and copies ran while one was open for 18% of the time, Pallas kernels for 0%

commit v1 on v0

v1 whole, which is shorter than its diff:
```python
import functools
import math

import jax
import jax.numpy as jnp
from jax import lax
from jax.experimental import pallas as pl
from jax.experimental.pallas import tpu as pltpu
from jax.sharding import PartitionSpec as P

HIGHEST = lax.Precision.HIGHEST
WHOLE = pl.BlockSpec(memory_space=pltpu.VMEM)


def dot_of(left, right, dims):
    return lax.dot_general(
        left, right, ((dims[:1], dims[1:]), ((), ())), precision=HIGHEST, preferred_element_type=jnp.float32
    )


def pack(values):
    half = values.shape[0] // 2
    return jnp.concatenate([values[:half], values[half:]], axis=1)


def rounds_of(size):
    if size == 4:
        return [(2, 3, 1, 0), (3, 2, 0, 1), (1, 0, 3, 2)]
    return [tuple(place ^ distance for place in range(size)) for distance in range(size - 1, 0, -1)]


def pick(table, place):
    value = table[0]
    for index, entry in enumerate(table):
        value = jnp.where(place == index, entry, value)
    return value


def load(tensor_ref, held_ref, sems, firsts):
    rows = held_ref.shape[0] // len(firsts)
    piece = held_ref.shape[0] // sems.shape[0]
    copies = []
    for place, first in enumerate(firsts):
        for start in range(0, rows, piece):
            copies.append(
                pltpu.make_async_copy(
                    tensor_ref.at[pl.ds(first * rows + start, piece)],
                    held_ref.at[pl.ds(place * rows + start, piece)],
                    sems.at[len(copies)],
                )
            )
    for copy in copies:
        copy.start()
    return copies


def halves(values):
    values = values.reshape(values.shape[0] * values.shape[1], values.shape[2])
    high = values.astype(jnp.bfloat16)
    low = (values - high.astype(jnp.float32)).astype(jnp.bfloat16)
    return jnp.concatenate([high, low], axis=1)


def split_kernel(rounds, chunk, tensor_ref, out_ref, held_ref, sems):
    me = lax.axis_index("gy") >> 1
    copies = load(tensor_ref, held_ref, sems, [pick(table, me) for table in rounds])
    depth = held_ref.shape[1]
    piece = held_ref.shape[0] // len(copies)
    for index, copy in enumerate(copies):
        copy.wait()
        for start in range(index * piece, (index + 1) * piece, chunk):
            out_ref[start * depth : (start + chunk) * depth, :] = halves(held_ref[start : start + chunk])


def gram_kernel(*refs):
    *shares, three_ref, gram_ref, three_gram_ref, weight_ref, two_ref = refs
    me = lax.axis_index("gx")
    share = shares[0].shape[0]
    for distance, ref in enumerate(shares):
        two_ref[pl.ds(pl.multiple_of((me ^ distance) * share, share), share), :] = ref[...]
    two = two_ref[...]
    gram_ref[...] = pack(dot_of(two, two, (1, 1)))
    three = three_ref[...]
    three_gram_ref[...] = pack(dot_of(three, three, (0, 0)))
    two = two.T
    high = two.astype(jnp.bfloat16)
    low = (two - high.astype(jnp.float32)).astype(jnp.bfloat16)
    both = jnp.concatenate([high, low], axis=1)
    weight_ref[...] = jnp.concatenate([both, both], axis=0)


def multiply(count, chunk, take, weight_ref, three_ref, outs, sum_ref):
    depth, rank = three_ref.shape
    rows = sum_ref.shape[0]
    half = rows // 2
    three = three_ref[...]
    three = jnp.concatenate([three, three], axis=1)[None]
    lower_half = lax.broadcasted_iota(jnp.int32, (half, 2 * rank), 1) < rank
    for block in range(count):
        for start in range(0, rows, chunk):
            product = jnp.dot(take(block * rows + start), weight_ref[...], preferred_element_type=jnp.float32)
            sum_ref[start : start + chunk, :] = jnp.sum(product.reshape(chunk, depth, 2 * rank) * three, axis=1)
        total = sum_ref[...]
        total = total + pltpu.roll(total, rank, 1)
        place = block % 2 * half
        outs[block // 2][place : place + half, :] = jnp.where(lower_half, total[:half], total[half:])


def sent_kernel(chunk, split_ref, weight_ref, three_ref, gram_ref, *refs):
    *outs, sum_ref = refs
    depth = three_ref.shape[0]

    def take(start):
        return split_ref[start * depth : (start + chunk) * depth, :]

    multiply(2 * len(outs), chunk, take, weight_ref, three_ref, outs, sum_ref)
    for out_ref in outs:
        out_ref[sum_ref.shape[0] :, :] = gram_ref[...]


def kept_kernel(chunk, tensor_ref, weight_ref, three_ref, gram_ref, out_ref, sum_ref, held_ref, sems):
    copies = load(tensor_ref, held_ref, sems, [lax.axis_index("gy") >> 1])
    piece = held_ref.shape[0] // len(copies)

    def take(start):
        if start % piece == 0:
            copies[start // piece].wait()
        return halves(held_ref[start : start + chunk])

    multiply(2, chunk, take, weight_ref, three_ref, [out_ref], sum_ref)
    out_ref[sum_ref.shape[0] :, :] = gram_ref[...]


def add_kernel(left_ref, right_ref, out_ref):
    out_ref[...] = left_ref[...] + right_ref[...]


def combine_kernel(half, left_ref, right_ref, sent_ref, kept_ref):
    bit = lax.rem(lax.axis_index("gy"), 2)
    for out_ref, place in ((sent_ref, 1 - bit), (kept_ref, bit)):
        rows = pl.ds(pl.multiple_of(place * half, half), half)
        out_ref[:half, :] = left_ref[rows, :] + right_ref[rows, :]
        out_ref[half:, :] = left_ref[2 * half :, :] + right_ref[2 * half :, :]


def solve_kernel(left_ref, right_ref, three_gram_ref, out_ref):
    total = left_ref[...] + right_ref[...]
    half, (place, lanes) = out_ref.shape[0] // 2, three_gram_ref.shape
    gram = total[half:] * three_gram_ref[...]
    order = lanes // 2
    rows = lax.broadcasted_iota(jnp.int32, (order, lanes), 0)
    lane_ids = lax.broadcasted_iota(jnp.int32, (order, lanes), 1)
    joined = jnp.concatenate([pltpu.roll(gram, order, 1), gram], axis=0)
    joined = jnp.where(lane_ids < order, jnp.where(rows == lane_ids, 1.0, 0.0), joined)
    right = jnp.concatenate([total[:half], pltpu.roll(total[:half], order, 1)], axis=0)
    right = jnp.where(lax.broadcasted_iota(jnp.int32, right.shape, 1) < order, right, 0.0)

    tile = (8, lanes)
    bands = [joined[8 * g : 8 * g + 8] for g in range(order // 8)]
    places = lax.broadcasted_iota(jnp.int32, tile, 0)

    def lane(value, index):
        return jnp.broadcast_to(value[:, order + index : order + index + 1], tile)

    for own in range(len(bands)):
        base, later = 8 * own, range(own + 1, len(bands))
        line = [jnp.broadcast_to(bands[own][q : q + 1], tile) for q in range(8)]
        entry = [[lane(line[q], base + p) if p >= q else None for p in range(8)] for q in range(8)]
        column = {h: [lane(bands[h], base + q) for q in range(8)] for h in later}
        band = None
        for q in range(8):
            pivot = entry[q][q]
            inverse = pltpu.reciprocal(pivot, approx=True)
            row = line[q] * lax.rsqrt(pivot)
            band = row if band is None else jnp.where(places == q, row, band)
            factor = [entry[q][p] * inverse if p > q else None for p in range(8)]
            for p in range(q + 1, 8):
                entry[p][p] = entry[p][p] - (entry[q][p] * entry[q][p]) * inverse
                for s in range(p + 1, 8):
                    entry[p][s] = entry[p][s] - factor[p] * entry[q][s]
                line[p] = line[p] - factor[p] * line[q]
            for h in later:
                scale = column[h][q] * inverse
                bands[h] = bands[h] - scale * line[q]
                for p in range(q + 1, 8):
                    column[h][p] = column[h][p] - scale * entry[q][p]
        bands[own] = band
    lower = jnp.concatenate(bands, axis=0)
    solved = dot_of(right, lower, (1, 1))
    out_ref[...] = dot_of(solved, lower, (1, 0))[:, :order]


def call(kernel, out_shape, args, flops, limit, scratch=(), specs=None):
    many = isinstance(out_shape, tuple)
    moved = sum(4 * a.size for a in args) + sum(4 * math.prod(o.shape) for o in (out_shape if many else (out_shape,)))
    return pl.pallas_call(
        kernel,
        out_shape=out_shape,
        in_specs=specs or [WHOLE] * len(args),
        out_specs=(WHOLE,) * len(out_shape) if many else WHOLE,
        scratch_shapes=scratch,
        compiler_params=pltpu.CompilerParams(vmem_limit_bytes=limit * 1024 * 1024),
        cost_estimate=pl.CostEstimate(flops=flops, bytes_accessed=moved, transcendentals=0),
    )(*args)


def body(tensor, factor_two, factor_three):
    groups, blocks = lax.axis_size("gx"), lax.axis_size("gy")
    rows, width, depth = tensor.shape
    rank = factor_three.shape[1]
    owned = rows // blocks
    half = owned // 2
    chunk = min(16, half)
    rounds = rounds_of(blocks // 2)
    f32 = functools.partial(pltpu.VMEM, dtype=jnp.float32)
    packed = f32((rank // 2, 2 * rank))
    pair = f32((owned + rank // 2, 2 * rank))
    single = f32((half + rank // 2, 2 * rank))
    sums = f32((owned, 2 * rank))
    hbm = pl.BlockSpec(memory_space=pltpu.HBM)

    def held(size, pieces):
        return [f32((size * 2 * owned, depth, width)), pltpu.SemaphoreType.DMA((size * pieces,))]

    mine = factor_two.T
    shares = [
        lax.ppermute(mine, "gx", [(i, i ^ distance) for i in range(groups)]) for distance in range(groups - 1, 0, -1)
    ]
    shares = [mine] + shares[::-1]
    tensor = pltpu.with_memory_space_constraint(jnp.transpose(tensor, (0, 2, 1)), pltpu.HBM)
    split = call(
        functools.partial(split_kernel, rounds, chunk),
        pltpu.VMEM((len(rounds) * 2 * owned * depth, 2 * width), jnp.bfloat16),
        (tensor,),
        10**9,
        12,
        held(len(rounds), 4),
        [hbm],
    )
    gram, three_gram, weight = call(
        gram_kernel,
        (packed, packed, pltpu.VMEM((2 * width, 2 * rank), jnp.bfloat16)),
        (*shares, factor_three),
        10**8,
        12,
        [f32((rank, width))],
    )
    sent = call(
        functools.partial(sent_kernel, chunk),
        (pair,) * len(rounds),
        (split, weight, factor_three, gram),
        2 * 10**9,
        12,
        [sums],
    )
    arrived = [
        lax.ppermute(
            value, "gy", [(2 * i + bit, 2 * j + bit) for i, j in enumerate(table) for bit in range(2)]
        )
        for value, table in zip(sent, rounds)
    ]
    total = call(
        functools.partial(kept_kernel, chunk),
        pair,
        (tensor, weight, factor_three, gram),
        2 * 10**9,
        12,
        [sums, *held(1, 4)],
        [hbm, WHOLE, WHOLE, WHOLE],
    )
    for part in arrived[:-1]:
        total = call(add_kernel, pair, (total, part), 10**6, 12)
    sent, kept = call(
        functools.partial(combine_kernel, half), (single, single), (total, arrived[-1]), 10**6, 12
    )
    last = lax.ppermute(sent, "gy", [(i, i ^ 1) for i in range(blocks)])
    return call(
        solve_kernel, jax.ShapeDtypeStruct((owned, rank), jnp.float32), (kept, last, three_gram), 10**8, 12
    )


def solution(mesh):
    in_specs = (P("gx", "gy", None), P("gy", "gx"), P())
    out_specs = P(("gx", "gy"), None)
    return jax.shard_map(body, mesh=mesh, in_specs=in_specs, out_specs=out_specs, check_vma=False)
```

time: 382 us -> 23.8 us (0.06)
  matrix products: 168 us -> 0 us
  local copies, waits for them, and re-layouts: 111 us -> 0.01 us
  blocking collectives: 44.4 us -> 0 us
  loops' own time: 42.5 us -> 0 us
  between operations: 13.5 us -> 0.06 us
  Pallas kernels: 0 us -> 10.5 us
  starting transfers between devices: 0.01 us -> 8.84 us
  waiting for transfers between devices: 0.03 us -> 4.23 us
    dot_general x195 -> x0, matrix products: 168 us -> none  [the longest x64 52.8 us: row_step(): jnp.dot(lower_col[None, :], result, precision=lax.Precision.HIGHEST)]
    dynamic_slice x128 -> x0, local copies, waits for them, and re-layouts: 85.5 us -> none  [row_step(): pivot = lax.dynamic_slice(lower, (index, index), (1, 1))]
    another operation x3 -> x0, loops' own time: 42.5 us -> none  [the longest x1 39.9 us: factorize(): return lax.fori_loop(0, order, column_step, jnp.zeros_like(normal))]
    psum x1 -> x0, blocking collectives: 37.9 us -> none  [body(): gram_two = lax.psum(local_gram, 'gy')]
    dynamic_update_slice x192 -> x0, local copies, waits for them, and re-layouts: 16.6 us -> none  [the longest x64 13.3 us: column_step(): return lax.dynamic_update_slice_in_dim(lower, column[:, None], index, 1)]
    pallas_call x0 -> x8, Pallas kernels: none -> 10.5 us  [call(): pl.pallas_call(kernel, out_shape=out_shape, in_specs=specs or [WHOLE] * l...]
    ppermute x0 -> x7, starting transfers between devices: none -> 8.84 us  [the longest x3 4.17 us: body(): lax.ppermute(value, 'gy', [(2 * i + bit, 2 * j + bit) for i, j in enumera...]
    all_gather x1 -> x0, blocking collectives: 6.53 us -> none  [body(): full_two = lax.all_gather(factor_two, 'gx', axis=1, tiled=True)]
  transfers between devices with their start and end apart: 1 -> 7, of which waited for: 0 -> 3; matrix products, arithmetic and copies ran while one was open for 18% -> 0% of each run, Pallas kernels for 0% -> 23%
where the time goes in v1:
time: 23.8 us; the launch traced here: 23.7 us
  Pallas kernels  10.5 us (44%)
  starting transfers between devices  8.84 us (37%)
  waiting for transfers between devices  4.23 us (18%)
    pallas_call x8, Pallas kernels, call(): pl.pallas_call(kernel, out_shape=out_shape, in_specs=specs or [WHOLE] * l...  10.5 us
    ppermute x3, starting transfers between devices, body(): lax.ppermute(value, 'gy', [(2 * i + bit, 2 * j + bit) for i, j in enumera...  4.17 us
    ppermute x3, starting transfers between devices, body(): lax.ppermute(mine, 'gx', [(i, i ^ distance) for i in range(groups)])  3.11 us
    ppermute x1, waiting for transfers between devices, body(): last = lax.ppermute(sent, 'gy', [(i, i ^ 1) for i in range(blocks)])  2.42 us
    ppermute x3, waiting for transfers between devices, body(): lax.ppermute(value, 'gy', [(2 * i + bit, 2 * j + bit) for i, j in enumera...  1.56 us
    ppermute x1, starting transfers between devices, body(): last = lax.ppermute(sent, 'gy', [(i, i ^ 1) for i in range(blocks)])  1.56 us
  transfers between devices with their start and end apart: 7, of which 3 were waited for; matrix products, arithmetic and copies ran while one was open for 0% of the time, Pallas kernels for 23%

profile of v1, /device:TPU:0, one launch (start us, length us, event | category | flops | bytes accessed | tf_op | source)
XLA Modules:
  0.0 23.7 jit_solution(18326475322894838600)
XLA Ops:
  0.0 0.0 copy-start.1
  0.0 0.0 copy-start
  0.0 0.5 %collective-permute-start = (f32[16,128]{1,0:T(8,128)}, f32[16,128]{1,0:T(8,128)S(1)}, u32[]{:S(2)}, u32[]{:S(2)}) collective-permute-start(f32[16,128]{1,0:T(8,128)} %bitcast.2), channel_id=1, source_target_pairs={{0,8},{8,0},{16,24},{24,16},{1,9},{9,1},{17,25},{25,17},{2,10},{10... | collective-permute-start | bytes 24584 | tf_op jit(solution)/shard_map/ppermute | solution.py:227
  0.5 2.6 %collective-permute-start.1 = (f32[16,128]{1,0:T(8,128)}, f32[16,128]{1,0:T(8,128)S(1)}, u32[]{:S(2)}, u32[]{:S(2)}) collective-permute-start(f32[16,128]{1,0:T(8,128)} %bitcast.3), channel_id=1, source_target_pairs={{0,16},{8,24},{16,0},{24,8},{1,17},{9,25},{17,1},{25,9},{2,18},{10... | collective-permute-start | bytes 24584 | tf_op jit(solution)/shard_map/ppermute | solution.py:227
  3.0 0.1 collective-permute-start.2
  3.1 2.9 %shard_map.39.split_ref = bf16[12288,256]{1,0:T(8,128)(2,1)S(1)} custom-call(f32[512,32,128]{2,1,0:T(8,128)} %bitcast.6), custom_call_target="tpu_custom_call" | custom-call | flops 1000000000 | bytes 20971520 | tf_op jit(solution)/shard_map/pallas_call | solution.py:196
  6.1 0.0 collective-permute-done.refs_1_
  6.1 0.0 collective-permute-done.1.refs_2_
  6.1 0.2 %collective-permute-done.2.refs_3_ = f32[16,128]{1,0:T(8,128)S(1)} collective-permute-done((f32[16,128]{1,0:T(8,128)}, f32[16,128]{1,0:T(8,128)S(1)}, u32[]{:S(2)}, u32[]{:S(2)}) %collective-permute-start.2) | collective-permute-done | bytes 8224 | tf_op jit(solution)/shard_map/ppermute | solution.py:227
  6.3 0.0 copy-done.1
  6.3 0.0 copy-done
  6.3 0.3 %shard_map.37 = (f32[32,128]{1,0:T(8,128)S(1)}, f32[32,128]{1,0:T(8,128)S(1)}, bf16[256,128]{1,0:T(8,128)(2,1)S(1)}) custom-call(f32[16,128]{1,0:T(8,128)S(1)} %bitcast.5, f32[16,128]{1,0:T(8,128)S(1)} %collective-permute-done.refs_1_, f32[16,128]{1,0:T(8,128)S(1)} %collective-permute-done.1.refs_2_, f32[16,128]{1,0:T(8,128)S(1)} %collective-permute-done.2.refs_3_, ...), custom_call_target="tpu_custom_call" | custom-call | flops 100000000 | bytes 204800 | tf_op jit(solution)/shard_map/pallas_call | solution.py:196
  6.6 1.9 %shard_map.40 = (f32[96,128]{1,0:T(8,128)S(1)}, f32[96,128]{1,0:T(8,128)S(1)}, f32[96,128]{1,0:T(8,128)S(1)}) custom-call(bf16[12288,256]{1,0:T(8,128)(2,1)S(1)} %shard_map.39.split_ref, bf16[256,128]{1,0:T(8,128)(2,1)S(1)} %get-tuple-element.13.weight_ref, f32[32,64]{1,0:T(8,128)S(1)} %copy-done, f32[32,128]{1,0:T(8,128)S(1)} %get-tuple-element.14.gram_ref), custom_call_target="tpu_custom_call" | custom-call | flops 2000000000 | bytes 12886016 | tf_op jit(solution)/shard_map/pallas_call | solution.py:196
  8.5 2.6 %collective-permute-start.3 = (f32[96,128]{1,0:T(8,128)S(1)}, f32[96,128]{1,0:T(8,128)S(1)}, u32[]{:S(2)}, u32[]{:S(2)}) collective-permute-start(f32[96,128]{1,0:T(8,128)S(1)} %get-tuple-element.15), channel_id=1, source_target_pairs={{0,4},{1,5},{2,6},{3,7},{4,2},{5,3},{6,0},{7,1},{8,12},{9,13},{10,... | collective-permute-start | bytes 147464 | tf_op jit(solution)/shard_map/ppermute | solution.py:257
  11.1 1.2 %collective-permute-start.4 = (f32[96,128]{1,0:T(8,128)S(1)}, f32[96,128]{1,0:T(8,128)S(1)}, u32[]{:S(2)}, u32[]{:S(2)}) collective-permute-start(f32[96,128]{1,0:T(8,128)S(1)} %get-tuple-element.16), channel_id=1, source_target_pairs={{0,6},{1,7},{2,4},{3,5},{4,0},{5,1},{6,2},{7,3},{8,14},{9,15},{10,... | collective-permute-start | bytes 147464 | tf_op jit(solution)/shard_map/ppermute | solution.py:257
  12.4 0.3 %collective-permute-start.5 = (f32[96,128]{1,0:T(8,128)S(1)}, f32[96,128]{1,0:T(8,128)S(1)}, u32[]{:S(2)}, u32[]{:S(2)}) collective-permute-start(f32[96,128]{1,0:T(8,128)S(1)} %get-tuple-element.17), channel_id=1, source_target_pairs={{0,2},{1,3},{2,0},{3,1},{4,6},{5,7},{6,4},{7,5},{8,10},{9,11},{10,... | collective-permute-start | bytes 147464 | tf_op jit(solution)/shard_map/ppermute | solution.py:257
  12.7 2.5 %shard_map.38.left_ref = f32[96,128]{1,0:T(8,128)S(1)} custom-call(f32[512,32,128]{2,1,0:T(8,128)} %bitcast.7, bf16[256,128]{1,0:T(8,128)(2,1)S(1)} %get-tuple-element.13.weight_ref, f32[32,64]{1,0:T(8,128)S(1)} %copy-done, f32[32,128]{1,0:T(8,128)S(1)} %get-tuple-element.14.gram_ref), custom_call_target="tpu_custom_call" | custom-call | flops 2000000000 | bytes 8593408 | tf_op jit(solution)/shard_map/pallas_call | solution.py:196
  15.2 0.0 collective-permute-done.3.right_ref
  15.2 1.5 %collective-permute-done.4.right_ref = f32[96,128]{1,0:T(8,128)S(1)} collective-permute-done((f32[96,128]{1,0:T(8,128)S(1)}, f32[96,128]{1,0:T(8,128)S(1)}, u32[]{:S(2)}, u32[]{:S(2)}) %collective-permute-start.4) | collective-permute-done | bytes 49184 | tf_op jit(solution)/shard_map/ppermute | solution.py:257
  16.8 0.0 collective-permute-done.5.right_ref
  16.8 1.6 %collective-permute-start.6 = (f32[64,128]{1,0:T(8,128)S(1)}, f32[64,128]{1,0:T(8,128)S(1)}, u32[]{:S(2)}, u32[]{:S(2)}) collective-permute-start(f32[64,128]{1,0:T(8,128)S(1)} %get-tuple-element.19), channel_id=1, source_target_pairs={{0,1},{1,0},{2,3},{3,2},{4,5},{5,4},{6,7},{7,6},{8,9},{9,8},{10,11... | collective-permute-start | bytes 98312 | tf_op jit(solution)/shard_map/ppermute | solution.py:276
  18.4 2.4 %collective-permute-done.6.right_ref = f32[64,128]{1,0:T(8,128)S(1)} collective-permute-done((f32[64,128]{1,0:T(8,128)S(1)}, f32[64,128]{1,0:T(8,128)S(1)}, u32[]{:S(2)}, u32[]{:S(2)}) %collective-permute-start.6) | collective-permute-done | bytes 32800 | tf_op jit(solution)/shard_map/ppermute | solution.py:276
  20.8 2.9 %shard_map.44 = f32[64,64]{1,0:T(8,128)} custom-call(f32[64,128]{1,0:T(8,128)S(1)} %get-tuple-element.18.left_ref, f32[64,128]{1,0:T(8,128)S(1)} %collective-permute-done.6.right_ref, f32[32,128]{1,0:T(8,128)S(1)} %get-tuple-element.20.three_gram_ref), custom_call_target="tpu_custom_call" | custom-call | flops 100000000 | bytes 98304 | tf_op jit(solution)/shard_map/pallas_call | solution.py:196
  (3 shorter events, 0.0 us)
Async XLA Ops:
  0.0 6.3 %copy-start.1 = (f32[128,16]{0,1:T(8,128)S(1)}, f32[128,16]{0,1:T(8,128)}, u32[]{:S(2)}) copy-start(f32[128,16]{0,1:T(8,128)} %param.4) | copy-start | bytes 24580
  0.0 6.3 %copy-start = (f32[32,64]{1,0:T(8,128)S(1)}, f32[32,64]{1,0:T(8,128)}, u32[]{:S(2)}) copy-start(f32[32,64]{1,0:T(8,128)} %three_ref.3) | copy-start | bytes 24580
  0.0 6.1 %collective-permute-start = (f32[16,128]{1,0:T(8,128)}, f32[16,128]{1,0:T(8,128)S(1)}, u32[]{:S(2)}, u32[]{:S(2)}) collective-permute-start(f32[16,128]{1,0:T(8,128)} %bitcast.2), channel_id=1, source_target_pairs={{0,8},{8,0},{16,24},{24,16},{1,9},{9,1},{17,25},{25,17},{2,10},{10... | collective-permute-start | bytes 24584 | tf_op jit(solution)/shard_map/ppermute | solution.py:227
  0.5 5.6 %collective-permute-start.1 = (f32[16,128]{1,0:T(8,128)}, f32[16,128]{1,0:T(8,128)S(1)}, u32[]{:S(2)}, u32[]{:S(2)}) collective-permute-start(f32[16,128]{1,0:T(8,128)} %bitcast.3), channel_id=1, source_target_pairs={{0,16},{8,24},{16,0},{24,8},{1,17},{9,25},{17,1},{25,9},{2,18},{10... | collective-permute-start | bytes 24584 | tf_op jit(solution)/shard_map/ppermute | solution.py:227
  3.0 3.3 %collective-permute-start.2 = (f32[16,128]{1,0:T(8,128)}, f32[16,128]{1,0:T(8,128)S(1)}, u32[]{:S(2)}, u32[]{:S(2)}) collective-permute-start(f32[16,128]{1,0:T(8,128)} %bitcast.4), channel_id=1, source_target_pairs={{0,24},{8,16},{16,8},{24,0},{1,25},{9,17},{17,9},{25,1},{2,26},{10... | collective-permute-start | bytes 24584 | tf_op jit(solution)/shard_map/ppermute | solution.py:227
  8.5 6.7 %collective-permute-start.3 = (f32[96,128]{1,0:T(8,128)S(1)}, f32[96,128]{1,0:T(8,128)S(1)}, u32[]{:S(2)}, u32[]{:S(2)}) collective-permute-start(f32[96,128]{1,0:T(8,128)S(1)} %get-tuple-element.15), channel_id=1, source_target_pairs={{0,4},{1,5},{2,6},{3,7},{4,2},{5,3},{6,0},{7,1},{8,12},{9,13},{10,... | collective-permute-start | bytes 147464 | tf_op jit(solution)/shard_map/ppermute | solution.py:257
  11.1 5.6 %collective-permute-start.4 = (f32[96,128]{1,0:T(8,128)S(1)}, f32[96,128]{1,0:T(8,128)S(1)}, u32[]{:S(2)}, u32[]{:S(2)}) collective-permute-start(f32[96,128]{1,0:T(8,128)S(1)} %get-tuple-element.16), channel_id=1, source_target_pairs={{0,6},{1,7},{2,4},{3,5},{4,0},{5,1},{6,2},{7,3},{8,14},{9,15},{10,... | collective-permute-start | bytes 147464 | tf_op jit(solution)/shard_map/ppermute | solution.py:257
  12.4 4.4 %collective-permute-start.5 = (f32[96,128]{1,0:T(8,128)S(1)}, f32[96,128]{1,0:T(8,128)S(1)}, u32[]{:S(2)}, u32[]{:S(2)}) collective-permute-start(f32[96,128]{1,0:T(8,128)S(1)} %get-tuple-element.17), channel_id=1, source_target_pairs={{0,2},{1,3},{2,0},{3,1},{4,6},{5,7},{6,4},{7,5},{8,10},{9,11},{10,... | collective-permute-start | bytes 147464 | tf_op jit(solution)/shard_map/ppermute | solution.py:257
  16.8 4.0 %collective-permute-start.6 = (f32[64,128]{1,0:T(8,128)S(1)}, f32[64,128]{1,0:T(8,128)S(1)}, u32[]{:S(2)}, u32[]{:S(2)}) collective-permute-start(f32[64,128]{1,0:T(8,128)S(1)} %get-tuple-element.19), channel_id=1, source_target_pairs={{0,1},{1,0},{2,3},{3,2},{4,5},{5,4},{6,7},{7,6},{8,9},{9,8},{10,11... | collective-permute-start | bytes 98312 | tf_op jit(solution)/shard_map/ppermute | solution.py:276

commit v2 on v1

--- a/solution.py
+++ b/solution.py
@@ -18,15 +18,21 @@
     )
 
 
+def narrow_dot(left, right, dims):
+    return lax.dot_general(left, right, ((dims[:1], dims[1:]), ((), ())), preferred_element_type=jnp.float32)
+
+
+def parted(values):
+    high = values.astype(jnp.bfloat16).astype(jnp.float32)
+    return high, values - high
+
+
 def pack(values):
     half = values.shape[0] // 2
     return jnp.concatenate([values[:half], values[half:]], axis=1)
 
 
-def rounds_of(size):
-    if size == 4:
-        return [(2, 3, 1, 0), (3, 2, 0, 1), (1, 0, 3, 2)]
-    return [tuple(place ^ distance for place in range(size)) for distance in range(size - 1, 0, -1)]
+ROUNDS = [(1, 2, 3, 0), (3, 0, 1, 2), (2, 3, 0, 1)]
 
 
 def pick(table, place):
@@ -61,9 +67,10 @@
     return jnp.concatenate([high, low], axis=1)
 
 
-def split_kernel(rounds, chunk, tensor_ref, out_ref, held_ref, sems):
-    me = lax.axis_index("gy") >> 1
-    copies = load(tensor_ref, held_ref, sems, [pick(table, me) for table in rounds])
+def split_kernel(count, chunk, tensor_ref, out_ref, held_ref, sems):
+    me = lax.rem(lax.axis_index("gy"), 4)
+    firsts = [4 * place + pick(table, me) for table in ROUNDS for place in range(count)]
+    copies = load(tensor_ref, held_ref, sems, firsts)
     depth = held_ref.shape[1]
     piece = held_ref.shape[0] // len(copies)
     for index, copy in enumerate(copies):
@@ -96,30 +103,31 @@
     three = three_ref[...]
     three = jnp.concatenate([three, three], axis=1)[None]
     lower_half = lax.broadcasted_iota(jnp.int32, (half, 2 * rank), 1) < rank
-    for block in range(count):
+    for block in range(count * len(outs)):
         for start in range(0, rows, chunk):
             product = jnp.dot(take(block * rows + start), weight_ref[...], preferred_element_type=jnp.float32)
             sum_ref[start : start + chunk, :] = jnp.sum(product.reshape(chunk, depth, 2 * rank) * three, axis=1)
         total = sum_ref[...]
         total = total + pltpu.roll(total, rank, 1)
-        place = block % 2 * half
-        outs[block // 2][place : place + half, :] = jnp.where(lower_half, total[:half], total[half:])
-
-
-def sent_kernel(chunk, split_ref, weight_ref, three_ref, gram_ref, *refs):
+        place = block % count * half
+        outs[block // count][place : place + half, :] = jnp.where(lower_half, total[:half], total[half:])
+
+
+def sent_kernel(count, chunk, split_ref, weight_ref, three_ref, gram_ref, *refs):
     *outs, sum_ref = refs
     depth = three_ref.shape[0]
 
     def take(start):
         return split_ref[start * depth : (start + chunk) * depth, :]
 
-    multiply(2 * len(outs), chunk, take, weight_ref, three_ref, outs, sum_ref)
+    multiply(count, chunk, take, weight_ref, three_ref, outs, sum_ref)
     for out_ref in outs:
-        out_ref[sum_ref.shape[0] :, :] = gram_ref[...]
-
-
-def kept_kernel(chunk, tensor_ref, weight_ref, three_ref, gram_ref, out_ref, sum_ref, held_ref, sems):
-    copies = load(tensor_ref, held_ref, sems, [lax.axis_index("gy") >> 1])
+        out_ref[count * (sum_ref.shape[0] // 2) :, :] = gram_ref[...]
+
+
+def kept_kernel(count, chunk, tensor_ref, weight_ref, three_ref, gram_ref, out_ref, sum_ref, held_ref, sems):
+    me = lax.rem(lax.axis_index("gy"), 4)
+    copies = load(tensor_ref, held_ref, sems, [4 * place + me for place in range(count)])
     piece = held_ref.shape[0] // len(copies)
 
     def take(start):
@@ -127,24 +135,27 @@
             copies[start // piece].wait()
         return halves(held_ref[start : start + chunk])
 
-    multiply(2, chunk, take, weight_ref, three_ref, [out_ref], sum_ref)
-    out_ref[sum_ref.shape[0] :, :] = gram_ref[...]
+    multiply(count, chunk, take, weight_ref, three_ref, [out_ref], sum_ref)
+    out_ref[count * (sum_ref.shape[0] // 2) :, :] = gram_ref[...]
 
 
 def add_kernel(left_ref, right_ref, out_ref):
     out_ref[...] = left_ref[...] + right_ref[...]
 
 
-def combine_kernel(half, left_ref, right_ref, sent_ref, kept_ref):
-    bit = lax.rem(lax.axis_index("gy"), 2)
-    for out_ref, place in ((sent_ref, 1 - bit), (kept_ref, bit)):
-        rows = pl.ds(pl.multiple_of(place * half, half), half)
+def combine_kernel(half, left_ref, right_ref, *out_refs):
+    me, count = lax.axis_index("gy") >> 2, len(out_refs)
+    for distance, out_ref in enumerate(out_refs):
+        rows = pl.ds(pl.multiple_of((me ^ distance) * half, half), half)
         out_ref[:half, :] = left_ref[rows, :] + right_ref[rows, :]
-        out_ref[half:, :] = left_ref[2 * half :, :] + right_ref[2 * half :, :]
-
-
-def solve_kernel(left_ref, right_ref, three_gram_ref, out_ref):
-    total = left_ref[...] + right_ref[...]
+        out_ref[half:, :] = left_ref[count * half :, :] + right_ref[count * half :, :]
+
+
+def solve_kernel(*refs):
+    *parts, three_gram_ref, out_ref = refs
+    total = parts[0][...]
+    for part in parts[1:]:
+        total = total + part[...]
     half, (place, lanes) = out_ref.shape[0] // 2, three_gram_ref.shape
     gram = total[half:] * three_gram_ref[...]
     order = lanes // 2
@@ -165,7 +176,8 @@
     for own in range(len(bands)):
         base, later = 8 * own, range(own + 1, len(bands))
         line = [jnp.broadcast_to(bands[own][q : q + 1], tile) for q in range(8)]
-        entry = [[lane(line[q], base + p) if p >= q else None for p in range(8)] for q in range(8)]
+        across = [lane(bands[own], base + p) for p in range(8)]
+        entry = [[jnp.broadcast_to(across[p][q : q + 1], tile) if p >= q else None for p in range(8)] for q in range(8)]
         column = {h: [lane(bands[h], base + q) for q in range(8)] for h in later}
         band = None
         for q in range(8):
@@ -185,9 +197,21 @@
                 for p in range(q + 1, 8):
                     column[h][p] = column[h][p] - scale * entry[q][p]
         bands[own] = band
-    lower = jnp.concatenate(bands, axis=0)
-    solved = dot_of(right, lower, (1, 1))
-    out_ref[...] = dot_of(solved, lower, (1, 0))[:, :order]
+    left = lane_ids < order
+    lower = jnp.where(left, jnp.concatenate(bands, axis=0), 0.0)
+    lower_high, lower_low = parted(lower)
+    right_high, right_low = parted(right)
+    doubled = lower_high + pltpu.roll(lower_high, order, 1)
+    factors = jnp.concatenate([doubled, lower_low], axis=1).astype(jnp.bfloat16)
+    terms = jnp.concatenate([right_high + pltpu.roll(right_low, order, 1), right_high], axis=1).astype(jnp.bfloat16)
+    solved = narrow_dot(terms, jnp.concatenate([factors, factors], axis=0), (1, 1))
+    solved_high, solved_low = parted(solved)
+    inside = lax.broadcasted_iota(jnp.int32, solved.shape, 1) < order
+    terms = jnp.concatenate(
+        [jnp.where(inside, solved_high, solved_low), jnp.where(inside, solved_high, 0.0)], axis=1
+    ).astype(jnp.bfloat16)
+    factors = jnp.concatenate([lower_high, lower_high, lower_low, lower_low], axis=0).astype(jnp.bfloat16)
+    out_ref[...] = narrow_dot(terms, factors, (1, 0))[:, :order]
 
 
 def call(kernel, out_shape, args, flops, limit, scratch=(), specs=None):
@@ -211,16 +235,16 @@
     owned = rows // blocks
     half = owned // 2
     chunk = min(16, half)
-    rounds = rounds_of(blocks // 2)
+    count = blocks // 4
     f32 = functools.partial(pltpu.VMEM, dtype=jnp.float32)
     packed = f32((rank // 2, 2 * rank))
-    pair = f32((owned + rank // 2, 2 * rank))
+    group = f32((count * half + rank // 2, 2 * rank))
     single = f32((half + rank // 2, 2 * rank))
     sums = f32((owned, 2 * rank))
     hbm = pl.BlockSpec(memory_space=pltpu.HBM)
 
-    def held(size, pieces):
-        return [f32((size * 2 * owned, depth, width)), pltpu.SemaphoreType.DMA((size * pieces,))]
+    def held(size):
+        return [f32((size * owned, depth, width)), pltpu.SemaphoreType.DMA((2 * size,))]
 
     mine = factor_two.T
     shares = [
@@ -229,12 +253,12 @@
     shares = [mine] + shares[::-1]
     tensor = pltpu.with_memory_space_constraint(jnp.transpose(tensor, (0, 2, 1)), pltpu.HBM)
     split = call(
-        functools.partial(split_kernel, rounds, chunk),
-        pltpu.VMEM((len(rounds) * 2 * owned * depth, 2 * width), jnp.bfloat16),
+        functools.partial(split_kernel, count, chunk),
+        pltpu.VMEM((3 * count * owned * depth, 2 * width), jnp.bfloat16),
         (tensor,),
         10**9,
         12,
-        held(len(rounds), 4),
+        held(3 * count),
         [hbm],
     )
     gram, three_gram, weight = call(
@@ -246,36 +270,37 @@
         [f32((rank, width))],
     )
     sent = call(
-        functools.partial(sent_kernel, chunk),
-        (pair,) * len(rounds),
+        functools.partial(sent_kernel, count, chunk),
+        (group,) * len(ROUNDS),
         (split, weight, factor_three, gram),
         2 * 10**9,
         12,
         [sums],
     )
     arrived = [
-        lax.ppermute(
-            value, "gy", [(2 * i + bit, 2 * j + bit) for i, j in enumerate(table) for bit in range(2)]
-        )
-        for value, table in zip(sent, rounds)
+        lax.ppermute(value, "gy", [(i, i - i % 4 + table[i % 4]) for i in range(blocks)])
+        for value, table in zip(sent, ROUNDS)
     ]
     total = call(
-        functools.partial(kept_kernel, chunk),
-        pair,
+        functools.partial(kept_kernel, count, chunk),
+        group,
         (tensor, weight, factor_three, gram),
         2 * 10**9,
         12,
-        [sums, *held(1, 4)],
+        [sums, *held(count)],
         [hbm, WHOLE, WHOLE, WHOLE],
     )
     for part in arrived[:-1]:
-        total = call(add_kernel, pair, (total, part), 10**6, 12)
-    sent, kept = call(
-        functools.partial(combine_kernel, half), (single, single), (total, arrived[-1]), 10**6, 12
-    )
-    last = lax.ppermute(sent, "gy", [(i, i ^ 1) for i in range(blocks)])
+        total = call(add_kernel, group, (total, part), 10**6, 12)
+    kept, *sent = call(
+        functools.partial(combine_kernel, half), (single,) * count, (total, arrived[-1]), 10**6, 12
+    )
+    parts = [
+        lax.ppermute(value, "gy", [(i, i ^ (4 * distance)) for i in range(blocks)])
+        for distance, value in enumerate(sent, 1)
+    ]
     return call(
-        solve_kernel, jax.ShapeDtypeStruct((owned, rank), jnp.float32), (kept, last, three_gram), 10**8, 12
+        solve_kernel, jax.ShapeDtypeStruct((owned, rank), jnp.float32), (kept, *parts, three_gram), 10**8, 12
     )
 
 

time: 23.8 us -> 23.7 us (level)
  waiting for transfers between devices: 4.23 us -> 2.67 us
  starting transfers between devices: 8.84 us -> 10.3 us
    ppermute x4, waiting for transfers between devices: 3.99 us -> 2.42 us  [the longest x1 2.22 us: body(): lax.ppermute(value, 'gy', [(i, i ^ 4 * distance) for i in range(blocks)])]
    ppermute x4, starting transfers between devices: 5.73 us -> 7.16 us  [the longest x3 4.51 us: body(): lax.ppermute(value, 'gy', [(i, i - i % 4 + table[i % 4]) for i in range(b...]
where the time goes in v2:
time: 23.7 us; the launch traced here: 23.5 us
  Pallas kernels  10.5 us (44%)
  starting transfers between devices  10.3 us (43%)
  waiting for transfers between devices  2.67 us (11%)
    pallas_call x8, Pallas kernels, call(): pl.pallas_call(kernel, out_shape=out_shape, in_specs=specs or [WHOLE] * l...  10.5 us
    ppermute x3, starting transfers between devices, body(): lax.ppermute(value, 'gy', [(i, i - i % 4 + table[i % 4]) for i in range(b...  4.51 us
    ppermute x3, starting transfers between devices, body(): lax.ppermute(mine, 'gx', [(i, i ^ distance) for i in range(groups)])  3.11 us
    ppermute x1, starting transfers between devices, body(): lax.ppermute(value, 'gy', [(i, i ^ 4 * distance) for i in range(blocks)])  2.65 us
    ppermute x1, waiting for transfers between devices, body(): lax.ppermute(value, 'gy', [(i, i ^ 4 * distance) for i in range(blocks)])  2.22 us
  transfers between devices with their start and end apart: 7, of which 3 were waited for; matrix products, arithmetic and copies ran while one was open for 0% of the time, Pallas kernels for 23%

profile of v2, /device:TPU:0, one launch (start us, length us, event | category | flops | bytes accessed | tf_op | source)
XLA Modules:
  0.0 23.5 jit_solution(13094084882538288091)
XLA Ops:
  0.0 0.0 copy-start.1
  0.0 0.0 copy-start
  0.0 0.5 %collective-permute-start = (f32[16,128]{1,0:T(8,128)}, f32[16,128]{1,0:T(8,128)S(1)}, u32[]{:S(2)}, u32[]{:S(2)}) collective-permute-start(f32[16,128]{1,0:T(8,128)} %bitcast.2), channel_id=1, source_target_pairs={{0,8},{8,0},{16,24},{24,16},{1,9},{9,1},{17,25},{25,17},{2,10},{10... | collective-permute-start | bytes 24584 | tf_op jit(solution)/shard_map/ppermute | solution.py:251
  0.5 2.6 %collective-permute-start.1 = (f32[16,128]{1,0:T(8,128)}, f32[16,128]{1,0:T(8,128)S(1)}, u32[]{:S(2)}, u32[]{:S(2)}) collective-permute-start(f32[16,128]{1,0:T(8,128)} %bitcast.3), channel_id=1, source_target_pairs={{0,16},{8,24},{16,0},{24,8},{1,17},{9,25},{17,1},{25,9},{2,18},{10... | collective-permute-start | bytes 24584 | tf_op jit(solution)/shard_map/ppermute | solution.py:251
  3.0 0.1 collective-permute-start.2
  3.1 2.9 %shard_map.39.split_ref = bf16[12288,256]{1,0:T(8,128)(2,1)S(1)} custom-call(f32[512,32,128]{2,1,0:T(8,128)} %bitcast.6), custom_call_target="tpu_custom_call" | custom-call | flops 1000000000 | bytes 20971520 | tf_op jit(solution)/shard_map/pallas_call | solution.py:220
  6.1 0.0 collective-permute-done.refs_1_
  6.1 0.0 collective-permute-done.1.refs_2_
  6.1 0.2 %collective-permute-done.2.refs_3_ = f32[16,128]{1,0:T(8,128)S(1)} collective-permute-done((f32[16,128]{1,0:T(8,128)}, f32[16,128]{1,0:T(8,128)S(1)}, u32[]{:S(2)}, u32[]{:S(2)}) %collective-permute-start.2) | collective-permute-done | bytes 8224 | tf_op jit(solution)/shard_map/ppermute | solution.py:251
  6.3 0.0 copy-done.1
  6.3 0.0 copy-done
  6.3 0.3 %shard_map.37 = (f32[32,128]{1,0:T(8,128)S(1)}, f32[32,128]{1,0:T(8,128)S(1)}, bf16[256,128]{1,0:T(8,128)(2,1)S(1)}) custom-call(f32[16,128]{1,0:T(8,128)S(1)} %bitcast.5, f32[16,128]{1,0:T(8,128)S(1)} %collective-permute-done.refs_1_, f32[16,128]{1,0:T(8,128)S(1)} %collective-permute-done.1.refs_2_, f32[16,128]{1,0:T(8,128)S(1)} %collective-permute-done.2.refs_3_, ...), custom_call_target="tpu_custom_call" | custom-call | flops 100000000 | bytes 204800 | tf_op jit(solution)/shard_map/pallas_call | solution.py:220
  6.6 1.9 %shard_map.40 = (f32[96,128]{1,0:T(8,128)S(1)}, f32[96,128]{1,0:T(8,128)S(1)}, f32[96,128]{1,0:T(8,128)S(1)}) custom-call(bf16[12288,256]{1,0:T(8,128)(2,1)S(1)} %shard_map.39.split_ref, bf16[256,128]{1,0:T(8,128)(2,1)S(1)} %get-tuple-element.13.weight_ref, f32[32,64]{1,0:T(8,128)S(1)} %copy-done, f32[32,128]{1,0:T(8,128)S(1)} %get-tuple-element.14.gram_ref), custom_call_target="tpu_custom_call" | custom-call | flops 2000000000 | bytes 12886016 | tf_op jit(solution)/shard_map/pallas_call | solution.py:220
  8.5 1.5 %collective-permute-start.3 = (f32[96,128]{1,0:T(8,128)S(1)}, f32[96,128]{1,0:T(8,128)S(1)}, u32[]{:S(2)}, u32[]{:S(2)}) collective-permute-start(f32[96,128]{1,0:T(8,128)S(1)} %get-tuple-element.15), channel_id=1, source_target_pairs={{0,1},{1,2},{2,3},{3,0},{4,5},{5,6},{6,7},{7,4},{8,9},{9,10},{10,1... | collective-permute-start | bytes 147464 | tf_op jit(solution)/shard_map/ppermute | solution.py:281
  10.0 1.4 %collective-permute-start.4 = (f32[96,128]{1,0:T(8,128)S(1)}, f32[96,128]{1,0:T(8,128)S(1)}, u32[]{:S(2)}, u32[]{:S(2)}) collective-permute-start(f32[96,128]{1,0:T(8,128)S(1)} %get-tuple-element.16), channel_id=1, source_target_pairs={{0,3},{1,0},{2,1},{3,2},{4,7},{5,4},{6,5},{7,6},{8,11},{9,8},{10,9... | collective-permute-start | bytes 147464 | tf_op jit(solution)/shard_map/ppermute | solution.py:281
  11.5 1.6 %collective-permute-start.5 = (f32[96,128]{1,0:T(8,128)S(1)}, f32[96,128]{1,0:T(8,128)S(1)}, u32[]{:S(2)}, u32[]{:S(2)}) collective-permute-start(f32[96,128]{1,0:T(8,128)S(1)} %get-tuple-element.17), channel_id=1, source_target_pairs={{0,2},{1,3},{2,0},{3,1},{4,6},{5,7},{6,4},{7,5},{8,10},{9,11},{10,... | collective-permute-start | bytes 147464 | tf_op jit(solution)/shard_map/ppermute | solution.py:281
  13.0 2.5 %shard_map.38.left_ref = f32[96,128]{1,0:T(8,128)S(1)} custom-call(f32[512,32,128]{2,1,0:T(8,128)} %bitcast.7, bf16[256,128]{1,0:T(8,128)(2,1)S(1)} %get-tuple-element.13.weight_ref, f32[32,64]{1,0:T(8,128)S(1)} %copy-done, f32[32,128]{1,0:T(8,128)S(1)} %get-tuple-element.14.gram_ref), custom_call_target="tpu_custom_call" | custom-call | flops 2000000000 | bytes 8593408 | tf_op jit(solution)/shard_map/pallas_call | solution.py:220
  15.5 0.0 collective-permute-done.3.right_ref
  15.6 0.0 collective-permute-done.4.right_ref
  15.6 0.2 collective-permute-done.5.right_ref
  15.8 2.7 %collective-permute-start.6 = (f32[64,128]{1,0:T(8,128)S(1)}, f32[64,128]{1,0:T(8,128)S(1)}, u32[]{:S(2)}, u32[]{:S(2)}) collective-permute-start(f32[64,128]{1,0:T(8,128)S(1)} %get-tuple-element.19), channel_id=1, source_target_pairs={{0,4},{1,5},{2,6},{3,7},{4,0},{5,1},{6,2},{7,3},{8,12},{9,13},{10,... | collective-permute-start | bytes 98312 | tf_op jit(solution)/shard_map/ppermute | solution.py:299
  18.4 2.2 %collective-permute-done.6.refs_1_ = f32[64,128]{1,0:T(8,128)S(1)} collective-permute-done((f32[64,128]{1,0:T(8,128)S(1)}, f32[64,128]{1,0:T(8,128)S(1)}, u32[]{:S(2)}, u32[]{:S(2)}) %collective-permute-start.6) | collective-permute-done | bytes 32800 | tf_op jit(solution)/shard_map/ppermute | solution.py:299
  20.7 2.9 %shard_map.44 = f32[64,64]{1,0:T(8,128)} custom-call(f32[64,128]{1,0:T(8,128)S(1)} %get-tuple-element.18.refs_0_, f32[64,128]{1,0:T(8,128)S(1)} %collective-permute-done.6.refs_1_, f32[32,128]{1,0:T(8,128)S(1)} %get-tuple-element.20.refs_2_), custom_call_target="tpu_custom_call" | custom-call | flops 100000000 | bytes 98304 | tf_op jit(solution)/shard_map/pallas_call | solution.py:220
  (3 shorter events, 0.0 us)
Async XLA Ops:
  0.0 6.3 %copy-start.1 = (f32[128,16]{0,1:T(8,128)S(1)}, f32[128,16]{0,1:T(8,128)}, u32[]{:S(2)}) copy-start(f32[128,16]{0,1:T(8,128)} %param.4) | copy-start | bytes 24580
  0.0 6.3 %copy-start = (f32[32,64]{1,0:T(8,128)S(1)}, f32[32,64]{1,0:T(8,128)}, u32[]{:S(2)}) copy-start(f32[32,64]{1,0:T(8,128)} %three_ref.3) | copy-start | bytes 24580
  0.0 6.1 %collective-permute-start = (f32[16,128]{1,0:T(8,128)}, f32[16,128]{1,0:T(8,128)S(1)}, u32[]{:S(2)}, u32[]{:S(2)}) collective-permute-start(f32[16,128]{1,0:T(8,128)} %bitcast.2), channel_id=1, source_target_pairs={{0,8},{8,0},{16,24},{24,16},{1,9},{9,1},{17,25},{25,17},{2,10},{10... | collective-permute-start | bytes 24584 | tf_op jit(solution)/shard_map/ppermute | solution.py:251
  0.5 5.6 %collective-permute-start.1 = (f32[16,128]{1,0:T(8,128)}, f32[16,128]{1,0:T(8,128)S(1)}, u32[]{:S(2)}, u32[]{:S(2)}) collective-permute-start(f32[16,128]{1,0:T(8,128)} %bitcast.3), channel_id=1, source_target_pairs={{0,16},{8,24},{16,0},{24,8},{1,17},{9,25},{17,1},{25,9},{2,18},{10... | collective-permute-start | bytes 24584 | tf_op jit(solution)/shard_map/ppermute | solution.py:251
  3.0 3.3 %collective-permute-start.2 = (f32[16,128]{1,0:T(8,128)}, f32[16,128]{1,0:T(8,128)S(1)}, u32[]{:S(2)}, u32[]{:S(2)}) collective-permute-start(f32[16,128]{1,0:T(8,128)} %bitcast.4), channel_id=1, source_target_pairs={{0,24},{8,16},{16,8},{24,0},{1,25},{9,17},{17,9},{25,1},{2,26},{10... | collective-permute-start | bytes 24584 | tf_op jit(solution)/shard_map/ppermute | solution.py:251
  8.5 7.0 %collective-permute-start.3 = (f32[96,128]{1,0:T(8,128)S(1)}, f32[96,128]{1,0:T(8,128)S(1)}, u32[]{:S(2)}, u32[]{:S(2)}) collective-permute-start(f32[96,128]{1,0:T(8,128)S(1)} %get-tuple-element.15), channel_id=1, source_target_pairs={{0,1},{1,2},{2,3},{3,0},{4,5},{5,6},{6,7},{7,4},{8,9},{9,10},{10,1... | collective-permute-start | bytes 147464 | tf_op jit(solution)/shard_map/ppermute | solution.py:281
  10.0 5.5 %collective-permute-start.4 = (f32[96,128]{1,0:T(8,128)S(1)}, f32[96,128]{1,0:T(8,128)S(1)}, u32[]{:S(2)}, u32[]{:S(2)}) collective-permute-start(f32[96,128]{1,0:T(8,128)S(1)} %get-tuple-element.16), channel_id=1, source_target_pairs={{0,3},{1,0},{2,1},{3,2},{4,7},{5,4},{6,5},{7,6},{8,11},{9,8},{10,9... | collective-permute-start | bytes 147464 | tf_op jit(solution)/shard_map/ppermute | solution.py:281
  11.5 4.3 %collective-permute-start.5 = (f32[96,128]{1,0:T(8,128)S(1)}, f32[96,128]{1,0:T(8,128)S(1)}, u32[]{:S(2)}, u32[]{:S(2)}) collective-permute-start(f32[96,128]{1,0:T(8,128)S(1)} %get-tuple-element.17), channel_id=1, source_target_pairs={{0,2},{1,3},{2,0},{3,1},{4,6},{5,7},{6,4},{7,5},{8,10},{9,11},{10,... | collective-permute-start | bytes 147464 | tf_op jit(solution)/shard_map/ppermute | solution.py:281
  15.8 4.9 %collective-permute-start.6 = (f32[64,128]{1,0:T(8,128)S(1)}, f32[64,128]{1,0:T(8,128)S(1)}, u32[]{:S(2)}, u32[]{:S(2)}) collective-permute-start(f32[64,128]{1,0:T(8,128)S(1)} %get-tuple-element.19), channel_id=1, source_target_pairs={{0,4},{1,5},{2,6},{3,7},{4,0},{5,1},{6,2},{7,3},{8,12},{9,13},{10,... | collective-permute-start | bytes 98312 | tf_op jit(solution)/shard_map/ppermute | solution.py:299

commit v3 on v2

--- a/solution.py
+++ b/solution.py
@@ -16,15 +16,6 @@
     return lax.dot_general(
         left, right, ((dims[:1], dims[1:]), ((), ())), precision=HIGHEST, preferred_element_type=jnp.float32
     )
-
-
-def narrow_dot(left, right, dims):
-    return lax.dot_general(left, right, ((dims[:1], dims[1:]), ((), ())), preferred_element_type=jnp.float32)
-
-
-def parted(values):
-    high = values.astype(jnp.bfloat16).astype(jnp.float32)
-    return high, values - high
 
 
 def pack(values):
@@ -79,23 +70,6 @@
             out_ref[start * depth : (start + chunk) * depth, :] = halves(held_ref[start : start + chunk])
 
 
-def gram_kernel(*refs):
-    *shares, three_ref, gram_ref, three_gram_ref, weight_ref, two_ref = refs
-    me = lax.axis_index("gx")
-    share = shares[0].shape[0]
-    for distance, ref in enumerate(shares):
-        two_ref[pl.ds(pl.multiple_of((me ^ distance) * share, share), share), :] = ref[...]
-    two = two_ref[...]
-    gram_ref[...] = pack(dot_of(two, two, (1, 1)))
-    three = three_ref[...]
-    three_gram_ref[...] = pack(dot_of(three, three, (0, 0)))
-    two = two.T
-    high = two.astype(jnp.bfloat16)
-    low = (two - high.astype(jnp.float32)).astype(jnp.bfloat16)
-    both = jnp.concatenate([high, low], axis=1)
-    weight_ref[...] = jnp.concatenate([both, both], axis=0)
-
-
 def multiply(count, chunk, take, weight_ref, three_ref, outs, sum_ref):
     depth, rank = three_ref.shape
     rows = sum_ref.shape[0]
@@ -113,16 +87,30 @@
         outs[block // count][place : place + half, :] = jnp.where(lower_half, total[:half], total[half:])
 
 
-def sent_kernel(count, chunk, split_ref, weight_ref, three_ref, gram_ref, *refs):
-    *outs, sum_ref = refs
-    depth = three_ref.shape[0]
+def sent_kernel(groups, count, chunk, split_ref, three_ref, *refs):
+    shares, refs = refs[:groups], refs[groups:]
+    *outs, gram_ref, three_gram_ref, weight_ref, two_ref, sum_ref = refs
+    me = lax.axis_index("gx")
+    depth, share = three_ref.shape[0], shares[0].shape[0]
+    for distance, ref in enumerate(shares):
+        two_ref[pl.ds(pl.multiple_of((me ^ distance) * share, share), share), :] = ref[...]
+    two = two_ref[...]
+    turned = two.T
+    high = turned.astype(jnp.bfloat16)
+    low = (turned - high.astype(jnp.float32)).astype(jnp.bfloat16)
+    both = jnp.concatenate([high, low], axis=1)
+    weight_ref[...] = jnp.concatenate([both, both], axis=0)
 
     def take(start):
         return split_ref[start * depth : (start + chunk) * depth, :]
 
     multiply(count, chunk, take, weight_ref, three_ref, outs, sum_ref)
+    three = three_ref[...]
+    three_gram_ref[...] = pack(dot_of(three, three, (0, 0)))
+    gram = pack(dot_of(two, two, (1, 1)))
+    gram_ref[...] = gram
     for out_ref in outs:
-        out_ref[count * (sum_ref.shape[0] // 2) :, :] = gram_ref[...]
+        out_ref[count * (sum_ref.shape[0] // 2) :, :] = gram
 
 
 def kept_kernel(count, chunk, tensor_ref, weight_ref, three_ref, gram_ref, out_ref, sum_ref, held_ref, sems):
@@ -173,45 +161,33 @@
     def lane(value, index):
         return jnp.broadcast_to(value[:, order + index : order + index + 1], tile)
 
-    for own in range(len(bands)):
-        base, later = 8 * own, range(own + 1, len(bands))
-        line = [jnp.broadcast_to(bands[own][q : q + 1], tile) for q in range(8)]
-        across = [lane(bands[own], base + p) for p in range(8)]
-        entry = [[jnp.broadcast_to(across[p][q : q + 1], tile) if p >= q else None for p in range(8)] for q in range(8)]
-        column = {h: [lane(bands[h], base + q) for q in range(8)] for h in later}
-        band = None
-        for q in range(8):
+    size, tiles = 16, 2
+    for own in range(order // size):
+        base, later = size * own, range(tiles * (own + 1), len(bands))
+        line = [jnp.broadcast_to(bands[tiles * own + q // 8][q % 8 : q % 8 + 1], tile) for q in range(size)]
+        entry = [[lane(line[q], base + p) if p >= q else None for p in range(size)] for q in range(size)]
+        column = {h: [lane(bands[h], base + q) for q in range(size)] for h in later}
+        done = [None] * tiles
+        for q in range(size):
             pivot = entry[q][q]
             inverse = pltpu.reciprocal(pivot, approx=True)
             row = line[q] * lax.rsqrt(pivot)
-            band = row if band is None else jnp.where(places == q, row, band)
-            factor = [entry[q][p] * inverse if p > q else None for p in range(8)]
-            for p in range(q + 1, 8):
+            done[q // 8] = row if q % 8 == 0 else jnp.where(places == q % 8, row, done[q // 8])
+            factor = [entry[q][p] * inverse if p > q else None for p in range(size)]
+            for p in range(q + 1, size):
                 entry[p][p] = entry[p][p] - (entry[q][p] * entry[q][p]) * inverse
-                for s in range(p + 1, 8):
+                for s in range(p + 1, size):
                     entry[p][s] = entry[p][s] - factor[p] * entry[q][s]
                 line[p] = line[p] - factor[p] * line[q]
             for h in later:
                 scale = column[h][q] * inverse
                 bands[h] = bands[h] - scale * line[q]
-                for p in range(q + 1, 8):
+                for p in range(q + 1, size):
                     column[h][p] = column[h][p] - scale * entry[q][p]
-        bands[own] = band
-    left = lane_ids < order
-    lower = jnp.where(left, jnp.concatenate(bands, axis=0), 0.0)
-    lower_high, lower_low = parted(lower)
-    right_high, right_low = parted(right)
-    doubled = lower_high + pltpu.roll(lower_high, order, 1)
-    factors = jnp.concatenate([doubled, lower_low], axis=1).astype(jnp.bfloat16)
-    terms = jnp.concatenate([right_high + pltpu.roll(right_low, order, 1), right_high], axis=1).astype(jnp.bfloat16)
-    solved = narrow_dot(terms, jnp.concatenate([factors, factors], axis=0), (1, 1))
-    solved_high, solved_low = parted(solved)
-    inside = lax.broadcasted_iota(jnp.int32, solved.shape, 1) < order
-    terms = jnp.concatenate(
-        [jnp.where(inside, solved_high, solved_low), jnp.where(inside, solved_high, 0.0)], axis=1
-    ).astype(jnp.bfloat16)
-    factors = jnp.concatenate([lower_high, lower_high, lower_low, lower_low], axis=0).astype(jnp.bfloat16)
-    out_ref[...] = narrow_dot(terms, factors, (1, 0))[:, :order]
+        bands[tiles * own : tiles * (own + 1)] = done
+    lower = jnp.concatenate(bands, axis=0)
+    solved = dot_of(right, lower, (1, 1))
+    out_ref[...] = dot_of(solved, lower, (1, 0))[:, :order]
 
 
 def call(kernel, out_shape, args, flops, limit, scratch=(), specs=None):
@@ -261,21 +237,13 @@
         held(3 * count),
         [hbm],
     )
-    gram, three_gram, weight = call(
-        gram_kernel,
-        (packed, packed, pltpu.VMEM((2 * width, 2 * rank), jnp.bfloat16)),
-        (*shares, factor_three),
-        10**8,
-        12,
-        [f32((rank, width))],
-    )
-    sent = call(
-        functools.partial(sent_kernel, count, chunk),
-        (group,) * len(ROUNDS),
-        (split, weight, factor_three, gram),
+    *sent, gram, three_gram, weight = call(
+        functools.partial(sent_kernel, groups, count, chunk),
+        (group,) * len(ROUNDS) + (packed, packed, pltpu.VMEM((2 * width, 2 * rank), jnp.bfloat16)),
+        (split, factor_three, *shares),
         2 * 10**9,
         12,
-        [sums],
+        [f32((rank, width)), sums],
     )
     arrived = [
         lax.ppermute(value, "gy", [(i, i - i % 4 + table[i % 4]) for i in range(blocks)])

time: 23.7 us -> 24 us (1.013)
  Pallas kernels: 10.5 us -> 10.9 us
    pallas_call x8 -> x7, Pallas kernels: 10.5 us -> 10.9 us  [call(): pl.pallas_call(kernel, out_shape=out_shape, in_specs=specs or [WHOLE] * l...]
where the time goes in v3:
time: 24 us; the launch traced here: 23.8 us
  Pallas kernels  10.9 us (45%)
  starting transfers between devices  10.3 us (43%)
  waiting for transfers between devices  2.58 us (11%)
    pallas_call x7, Pallas kernels, call(): pl.pallas_call(kernel, out_shape=out_shape, in_specs=specs or [WHOLE] * l...  10.9 us
    ppermute x3, starting transfers between devices, body(): lax.ppermute(value, 'gy', [(i, i - i % 4 + table[i % 4]) for i in range(b...  4.58 us
    ppermute x3, starting transfers between devices, body(): lax.ppermute(mine, 'gx', [(i, i ^ distance) for i in range(groups)])  3.08 us
    ppermute x1, starting transfers between devices, body(): lax.ppermute(value, 'gy', [(i, i ^ 4 * distance) for i in range(blocks)])  2.65 us
    ppermute x1, waiting for transfers between devices, body(): lax.ppermute(value, 'gy', [(i, i ^ 4 * distance) for i in range(blocks)])  2.22 us
  transfers between devices with their start and end apart: 7, of which 3 were waited for; matrix products, arithmetic and copies ran while one was open for 0% of the time, Pallas kernels for 23%

profile of v3, /device:TPU:0, one launch (start us, length us, event | category | flops | bytes accessed | tf_op | source)
XLA Modules:
  0.0 23.8 jit_solution(14938433503955940931)
XLA Ops:
  0.0 0.0 copy-start.1
  0.0 0.0 copy-start
  0.0 2.4 %collective-permute-start.2 = (f32[16,128]{1,0:T(8,128)}, f32[16,128]{1,0:T(8,128)S(1)}, u32[]{:S(2)}, u32[]{:S(2)}) collective-permute-start(f32[16,128]{1,0:T(8,128)} %bitcast.2), channel_id=1, source_target_pairs={{0,24},{8,16},{16,8},{24,0},{1,25},{9,17},{17,9},{25,1},{2,26},{10... | collective-permute-start | bytes 24584 | tf_op jit(solution)/shard_map/ppermute | solution.py:227
  2.4 0.6 %collective-permute-start.1 = (f32[16,128]{1,0:T(8,128)}, f32[16,128]{1,0:T(8,128)S(1)}, u32[]{:S(2)}, u32[]{:S(2)}) collective-permute-start(f32[16,128]{1,0:T(8,128)} %bitcast.3), channel_id=1, source_target_pairs={{0,16},{8,24},{16,0},{24,8},{1,17},{9,25},{17,1},{25,9},{2,18},{10... | collective-permute-start | bytes 24584 | tf_op jit(solution)/shard_map/ppermute | solution.py:227
  3.0 0.0 collective-permute-start
  3.1 2.9 %shard_map.37.split_ref = bf16[12288,256]{1,0:T(8,128)(2,1)S(1)} custom-call(f32[512,32,128]{2,1,0:T(8,128)} %bitcast.6), custom_call_target="tpu_custom_call" | custom-call | flops 1000000000 | bytes 20971520 | tf_op jit(solution)/shard_map/pallas_call | solution.py:196
  6.0 0.0 collective-permute-done.2.refs_3_
  6.0 0.2 collective-permute-done.1.refs_2_
  6.3 0.0 collective-permute-done.refs_1_
  6.3 0.0 copy-done.1
  6.3 0.0 copy-done
  6.3 2.1 %shard_map.38 = (f32[96,128]{1,0:T(8,128)S(1)}, f32[96,128]{1,0:T(8,128)S(1)}, f32[96,128]{1,0:T(8,128)S(1)}, f32[32,128]{1,0:T(8,128)S(1)}, f32[32,128]{1,0:T(8,128)S(1)}, /*index=5*/bf16[256,128]{1,0:T(8,128)(2,1)S(1)}) custom-call(bf16[12288,256]{1,0:T(8,128)(2,1)S(1)} %shard_map.37.split_ref, f32[32,64]{1,0:T(8,128)S(1)} %copy-done, ...), custom_call_target="tpu_custom_call" | custom-call | flops 2000000000 | bytes 12935168 | tf_op jit(solution)/shard_map/pallas_call | solution.py:196
  8.4 1.6 %collective-permute-start.3 = (f32[96,128]{1,0:T(8,128)S(1)}, f32[96,128]{1,0:T(8,128)S(1)}, u32[]{:S(2)}, u32[]{:S(2)}) collective-permute-start(f32[96,128]{1,0:T(8,128)S(1)} %get-tuple-element.15), channel_id=1, source_target_pairs={{0,1},{1,2},{2,3},{3,0},{4,5},{5,6},{6,7},{7,4},{8,9},{9,10},{10,1... | collective-permute-start | bytes 147464 | tf_op jit(solution)/shard_map/ppermute | solution.py:249
  10.0 1.4 %collective-permute-start.4 = (f32[96,128]{1,0:T(8,128)S(1)}, f32[96,128]{1,0:T(8,128)S(1)}, u32[]{:S(2)}, u32[]{:S(2)}) collective-permute-start(f32[96,128]{1,0:T(8,128)S(1)} %get-tuple-element.16), channel_id=1, source_target_pairs={{0,3},{1,0},{2,1},{3,2},{4,7},{5,4},{6,5},{7,6},{8,11},{9,8},{10,9... | collective-permute-start | bytes 147464 | tf_op jit(solution)/shard_map/ppermute | solution.py:249
  11.4 1.6 %collective-permute-start.5 = (f32[96,128]{1,0:T(8,128)S(1)}, f32[96,128]{1,0:T(8,128)S(1)}, u32[]{:S(2)}, u32[]{:S(2)}) collective-permute-start(f32[96,128]{1,0:T(8,128)S(1)} %get-tuple-element.17), channel_id=1, source_target_pairs={{0,2},{1,3},{2,0},{3,1},{4,6},{5,7},{6,4},{7,5},{8,10},{9,11},{10,... | collective-permute-start | bytes 147464 | tf_op jit(solution)/shard_map/ppermute | solution.py:249
  13.0 2.5 %shard_map.39.left_ref = f32[96,128]{1,0:T(8,128)S(1)} custom-call(f32[512,32,128]{2,1,0:T(8,128)} %bitcast.7, bf16[256,128]{1,0:T(8,128)(2,1)S(1)} %get-tuple-element.13.weight_ref, f32[32,64]{1,0:T(8,128)S(1)} %copy-done, f32[32,128]{1,0:T(8,128)S(1)} %get-tuple-element.14.gram_ref), custom_call_target="tpu_custom_call" | custom-call | flops 2000000000 | bytes 8593408 | tf_op jit(solution)/shard_map/pallas_call | solution.py:196
  15.5 0.0 collective-permute-done.3.right_ref
  15.5 0.0 collective-permute-done.4.right_ref
  15.5 0.1 collective-permute-done.5.right_ref
  15.7 2.7 %collective-permute-start.6 = (f32[64,128]{1,0:T(8,128)S(1)}, f32[64,128]{1,0:T(8,128)S(1)}, u32[]{:S(2)}, u32[]{:S(2)}) collective-permute-start(f32[64,128]{1,0:T(8,128)S(1)} %get-tuple-element.19), channel_id=1, source_target_pairs={{0,4},{1,5},{2,6},{3,7},{4,0},{5,1},{6,2},{7,3},{8,12},{9,13},{10,... | collective-permute-start | bytes 98312 | tf_op jit(solution)/shard_map/ppermute | solution.py:267
  18.3 2.2 %collective-permute-done.6.refs_1_ = f32[64,128]{1,0:T(8,128)S(1)} collective-permute-done((f32[64,128]{1,0:T(8,128)S(1)}, f32[64,128]{1,0:T(8,128)S(1)}, u32[]{:S(2)}, u32[]{:S(2)}) %collective-permute-start.6) | collective-permute-done | bytes 32800 | tf_op jit(solution)/shard_map/ppermute | solution.py:267
  20.5 3.3 %shard_map.43 = f32[64,64]{1,0:T(8,128)} custom-call(f32[64,128]{1,0:T(8,128)S(1)} %get-tuple-element.18.refs_0_, f32[64,128]{1,0:T(8,128)S(1)} %collective-permute-done.6.refs_1_, f32[32,128]{1,0:T(8,128)S(1)} %get-tuple-element.20.refs_2_), custom_call_target="tpu_custom_call" | custom-call | flops 100000000 | bytes 98304 | tf_op jit(solution)/shard_map/pallas_call | solution.py:196
  (3 shorter events, 0.0 us)
Async XLA Ops:
  0.0 6.3 %copy-start.1 = (f32[128,16]{0,1:T(8,128)S(1)}, f32[128,16]{0,1:T(8,128)}, u32[]{:S(2)}) copy-start(f32[128,16]{0,1:T(8,128)} %param.4) | copy-start | bytes 24580
  0.0 6.3 %copy-start = (f32[32,64]{1,0:T(8,128)S(1)}, f32[32,64]{1,0:T(8,128)}, u32[]{:S(2)}) copy-start(f32[32,64]{1,0:T(8,128)} %three_ref.3) | copy-start | bytes 24580
  0.0 6.0 %collective-permute-start.2 = (f32[16,128]{1,0:T(8,128)}, f32[16,128]{1,0:T(8,128)S(1)}, u32[]{:S(2)}, u32[]{:S(2)}) collective-permute-start(f32[16,128]{1,0:T(8,128)} %bitcast.2), channel_id=1, source_target_pairs={{0,24},{8,16},{16,8},{24,0},{1,25},{9,17},{17,9},{25,1},{2,26},{10... | collective-permute-start | bytes 24584 | tf_op jit(solution)/shard_map/ppermute | solution.py:227
  2.4 3.9 %collective-permute-start.1 = (f32[16,128]{1,0:T(8,128)}, f32[16,128]{1,0:T(8,128)S(1)}, u32[]{:S(2)}, u32[]{:S(2)}) collective-permute-start(f32[16,128]{1,0:T(8,128)} %bitcast.3), channel_id=1, source_target_pairs={{0,16},{8,24},{16,0},{24,8},{1,17},{9,25},{17,1},{25,9},{2,18},{10... | collective-permute-start | bytes 24584 | tf_op jit(solution)/shard_map/ppermute | solution.py:227
  3.0 3.2 %collective-permute-start = (f32[16,128]{1,0:T(8,128)}, f32[16,128]{1,0:T(8,128)S(1)}, u32[]{:S(2)}, u32[]{:S(2)}) collective-permute-start(f32[16,128]{1,0:T(8,128)} %bitcast.4), channel_id=1, source_target_pairs={{0,8},{8,0},{16,24},{24,16},{1,9},{9,1},{17,25},{25,17},{2,10},{10... | collective-permute-start | bytes 24584 | tf_op jit(solution)/shard_map/ppermute | solution.py:227
  8.4 7.0 %collective-permute-start.3 = (f32[96,128]{1,0:T(8,128)S(1)}, f32[96,128]{1,0:T(8,128)S(1)}, u32[]{:S(2)}, u32[]{:S(2)}) collective-permute-start(f32[96,128]{1,0:T(8,128)S(1)} %get-tuple-element.15), channel_id=1, source_target_pairs={{0,1},{1,2},{2,3},{3,0},{4,5},{5,6},{6,7},{7,4},{8,9},{9,10},{10,1... | collective-permute-start | bytes 147464 | tf_op jit(solution)/shard_map/ppermute | solution.py:249
  10.0 5.5 %collective-permute-start.4 = (f32[96,128]{1,0:T(8,128)S(1)}, f32[96,128]{1,0:T(8,128)S(1)}, u32[]{:S(2)}, u32[]{:S(2)}) collective-permute-start(f32[96,128]{1,0:T(8,128)S(1)} %get-tuple-element.16), channel_id=1, source_target_pairs={{0,3},{1,0},{2,1},{3,2},{4,7},{5,4},{6,5},{7,6},{8,11},{9,8},{10,9... | collective-permute-start | bytes 147464 | tf_op jit(solution)/shard_map/ppermute | solution.py:249
  11.4 4.2 %collective-permute-start.5 = (f32[96,128]{1,0:T(8,128)S(1)}, f32[96,128]{1,0:T(8,128)S(1)}, u32[]{:S(2)}, u32[]{:S(2)}) collective-permute-start(f32[96,128]{1,0:T(8,128)S(1)} %get-tuple-element.17), channel_id=1, source_target_pairs={{0,2},{1,3},{2,0},{3,1},{4,6},{5,7},{6,4},{7,5},{8,10},{9,11},{10,... | collective-permute-start | bytes 147464 | tf_op jit(solution)/shard_map/ppermute | solution.py:249
  15.7 4.9 %collective-permute-start.6 = (f32[64,128]{1,0:T(8,128)S(1)}, f32[64,128]{1,0:T(8,128)S(1)}, u32[]{:S(2)}, u32[]{:S(2)}) collective-permute-start(f32[64,128]{1,0:T(8,128)S(1)} %get-tuple-element.19), channel_id=1, source_target_pairs={{0,4},{1,5},{2,6},{3,7},{4,0},{5,1},{6,2},{7,3},{8,12},{9,13},{10,... | collective-permute-start | bytes 98312 | tf_op jit(solution)/shard_map/ppermute | solution.py:267

commit v4 on v2

--- a/solution.py
+++ b/solution.py
@@ -79,23 +79,6 @@
             out_ref[start * depth : (start + chunk) * depth, :] = halves(held_ref[start : start + chunk])
 
 
-def gram_kernel(*refs):
-    *shares, three_ref, gram_ref, three_gram_ref, weight_ref, two_ref = refs
-    me = lax.axis_index("gx")
-    share = shares[0].shape[0]
-    for distance, ref in enumerate(shares):
-        two_ref[pl.ds(pl.multiple_of((me ^ distance) * share, share), share), :] = ref[...]
-    two = two_ref[...]
-    gram_ref[...] = pack(dot_of(two, two, (1, 1)))
-    three = three_ref[...]
-    three_gram_ref[...] = pack(dot_of(three, three, (0, 0)))
-    two = two.T
-    high = two.astype(jnp.bfloat16)
-    low = (two - high.astype(jnp.float32)).astype(jnp.bfloat16)
-    both = jnp.concatenate([high, low], axis=1)
-    weight_ref[...] = jnp.concatenate([both, both], axis=0)
-
-
 def multiply(count, chunk, take, weight_ref, three_ref, outs, sum_ref):
     depth, rank = three_ref.shape
     rows = sum_ref.shape[0]
@@ -113,19 +96,33 @@
         outs[block // count][place : place + half, :] = jnp.where(lower_half, total[:half], total[half:])
 
 
-def sent_kernel(count, chunk, split_ref, weight_ref, three_ref, gram_ref, *refs):
-    *outs, sum_ref = refs
-    depth = three_ref.shape[0]
+def sent_kernel(groups, count, chunk, split_ref, three_ref, *refs):
+    shares, refs = refs[:groups], refs[groups:]
+    *outs, gram_ref, weight_ref, two_ref, sum_ref = refs
+    me = lax.axis_index("gx")
+    depth, share = three_ref.shape[0], shares[0].shape[0]
+    for distance, ref in enumerate(shares):
+        two_ref[pl.ds(pl.multiple_of((me ^ distance) * share, share), share), :] = ref[...]
+    two = two_ref[...]
+    gram = pack(dot_of(two, two, (1, 1)))
+    gram_ref[...] = gram
+    for out_ref in outs:
+        out_ref[count * (sum_ref.shape[0] // 2) :, :] = gram
+    turned = two.T
+    high = turned.astype(jnp.bfloat16)
+    low = (turned - high.astype(jnp.float32)).astype(jnp.bfloat16)
+    both = jnp.concatenate([high, low], axis=1)
+    weight_ref[...] = jnp.concatenate([both, both], axis=0)
 
     def take(start):
         return split_ref[start * depth : (start + chunk) * depth, :]
 
     multiply(count, chunk, take, weight_ref, three_ref, outs, sum_ref)
-    for out_ref in outs:
-        out_ref[count * (sum_ref.shape[0] // 2) :, :] = gram_ref[...]
-
-
-def kept_kernel(count, chunk, tensor_ref, weight_ref, three_ref, gram_ref, out_ref, sum_ref, held_ref, sems):
+
+
+def kept_kernel(
+    count, chunk, tensor_ref, weight_ref, three_ref, gram_ref, out_ref, three_gram_ref, sum_ref, held_ref, sems
+):
     me = lax.rem(lax.axis_index("gy"), 4)
     copies = load(tensor_ref, held_ref, sems, [4 * place + me for place in range(count)])
     piece = held_ref.shape[0] // len(copies)
@@ -135,6 +132,8 @@
             copies[start // piece].wait()
         return halves(held_ref[start : start + chunk])
 
+    three = three_ref[...]
+    three_gram_ref[...] = pack(dot_of(three, three, (0, 0)))
     multiply(count, chunk, take, weight_ref, three_ref, [out_ref], sum_ref)
     out_ref[count * (sum_ref.shape[0] // 2) :, :] = gram_ref[...]
 
@@ -176,8 +175,7 @@
     for own in range(len(bands)):
         base, later = 8 * own, range(own + 1, len(bands))
         line = [jnp.broadcast_to(bands[own][q : q + 1], tile) for q in range(8)]
-        across = [lane(bands[own], base + p) for p in range(8)]
-        entry = [[jnp.broadcast_to(across[p][q : q + 1], tile) if p >= q else None for p in range(8)] for q in range(8)]
+        entry = [[lane(line[q], base + p) if p >= q else None for p in range(8)] for q in range(8)]
         column = {h: [lane(bands[h], base + q) for q in range(8)] for h in later}
         band = None
         for q in range(8):
@@ -261,29 +259,21 @@
         held(3 * count),
         [hbm],
     )
-    gram, three_gram, weight = call(
-        gram_kernel,
-        (packed, packed, pltpu.VMEM((2 * width, 2 * rank), jnp.bfloat16)),
-        (*shares, factor_three),
-        10**8,
-        12,
-        [f32((rank, width))],
-    )
-    sent = call(
-        functools.partial(sent_kernel, count, chunk),
-        (group,) * len(ROUNDS),
-        (split, weight, factor_three, gram),
+    *sent, gram, weight = call(
+        functools.partial(sent_kernel, groups, count, chunk),
+        (group,) * len(ROUNDS) + (packed, pltpu.VMEM((2 * width, 2 * rank), jnp.bfloat16)),
+        (split, factor_three, *shares),
         2 * 10**9,
         12,
-        [sums],
+        [f32((rank, width)), sums],
     )
     arrived = [
         lax.ppermute(value, "gy", [(i, i - i % 4 + table[i % 4]) for i in range(blocks)])
         for value, table in zip(sent, ROUNDS)
     ]
-    total = call(
+    total, three_gram = call(
         functools.partial(kept_kernel, count, chunk),
-        group,
+        (group, packed),
         (tensor, weight, factor_three, gram),
         2 * 10**9,
         12,

time: 23.7 us -> 23.5 us (level)
    pallas_call x8 -> x7, Pallas kernels: 10.5 us -> 10.4 us  [call(): pl.pallas_call(kernel, out_shape=out_shape, in_specs=specs or [WHOLE] * l...]
where the time goes in v4:
time: 23.5 us; the launch traced here: 23.3 us
  Pallas kernels  10.4 us (44%)
  starting transfers between devices  10.3 us (44%)
  waiting for transfers between devices  2.54 us (11%)
    pallas_call x7, Pallas kernels, call(): pl.pallas_call(kernel, out_shape=out_shape, in_specs=specs or [WHOLE] * l...  10.4 us
    ppermute x3, starting transfers between devices, body(): lax.ppermute(value, 'gy', [(i, i - i % 4 + table[i % 4]) for i in range(b...  4.54 us
    ppermute x3, starting transfers between devices, body(): lax.ppermute(mine, 'gx', [(i, i ^ distance) for i in range(groups)])  3.08 us
    ppermute x1, starting transfers between devices, body(): lax.ppermute(value, 'gy', [(i, i ^ 4 * distance) for i in range(blocks)])  2.65 us
    ppermute x1, waiting for transfers between devices, body(): lax.ppermute(value, 'gy', [(i, i ^ 4 * distance) for i in range(blocks)])  2.22 us
  transfers between devices with their start and end apart: 7, of which 3 were waited for; matrix products, arithmetic and copies ran while one was open for 0% of the time, Pallas kernels for 23%

profile of v4, /device:TPU:0, one launch (start us, length us, event | category | flops | bytes accessed | tf_op | source)
XLA Modules:
  0.0 23.3 jit_solution(6609506888506505861)
XLA Ops:
  0.0 0.0 copy-start.1
  0.0 0.0 copy-start
  0.0 2.4 %collective-permute-start.2 = (f32[16,128]{1,0:T(8,128)}, f32[16,128]{1,0:T(8,128)S(1)}, u32[]{:S(2)}, u32[]{:S(2)}) collective-permute-start(f32[16,128]{1,0:T(8,128)} %bitcast.2), channel_id=1, source_target_pairs={{0,24},{8,16},{16,8},{24,0},{1,25},{9,17},{17,9},{25,1},{2,26},{10... | collective-permute-start | bytes 24584 | tf_op jit(solution)/shard_map/ppermute | solution.py:249
  2.4 0.6 %collective-permute-start.1 = (f32[16,128]{1,0:T(8,128)}, f32[16,128]{1,0:T(8,128)S(1)}, u32[]{:S(2)}, u32[]{:S(2)}) collective-permute-start(f32[16,128]{1,0:T(8,128)} %bitcast.3), channel_id=1, source_target_pairs={{0,16},{8,24},{16,0},{24,8},{1,17},{9,25},{17,1},{25,9},{2,18},{10... | collective-permute-start | bytes 24584 | tf_op jit(solution)/shard_map/ppermute | solution.py:249
  3.0 0.0 collective-permute-start
  3.1 2.9 %shard_map.37.split_ref = bf16[12288,256]{1,0:T(8,128)(2,1)S(1)} custom-call(f32[512,32,128]{2,1,0:T(8,128)} %bitcast.6), custom_call_target="tpu_custom_call" | custom-call | flops 1000000000 | bytes 20971520 | tf_op jit(solution)/shard_map/pallas_call | solution.py:218
  6.0 0.0 collective-permute-done.2.refs_3_
  6.0 0.2 collective-permute-done.1.refs_2_
  6.3 0.0 collective-permute-done.refs_1_
  6.3 0.0 copy-done.1
  6.3 0.0 copy-done
  6.3 2.1 %shard_map.38 = (f32[96,128]{1,0:T(8,128)S(1)}, f32[96,128]{1,0:T(8,128)S(1)}, f32[96,128]{1,0:T(8,128)S(1)}, f32[32,128]{1,0:T(8,128)S(1)}, bf16[256,128]{1,0:T(8,128)(2,1)S(1)}) custom-call(bf16[12288,256]{1,0:T(8,128)(2,1)S(1)} %shard_map.37.split_ref, f32[32,64]{1,0:T(8,128)S(1)} %copy-done, f32[16,128]{1,0:T(8,128)S(1)} %bitcast.5, ...), custom_call_target="tpu_custom_call" | custom-call | flops 2000000000 | bytes 12918784 | tf_op jit(solution)/shard_map/pallas_call | solution.py:218
  8.4 1.5 %collective-permute-start.3 = (f32[96,128]{1,0:T(8,128)S(1)}, f32[96,128]{1,0:T(8,128)S(1)}, u32[]{:S(2)}, u32[]{:S(2)}) collective-permute-start(f32[96,128]{1,0:T(8,128)S(1)} %get-tuple-element.17), channel_id=1, source_target_pairs={{0,1},{1,2},{2,3},{3,0},{4,5},{5,6},{6,7},{7,4},{8,9},{9,10},{10,1... | collective-permute-start | bytes 147464 | tf_op jit(solution)/shard_map/ppermute | solution.py:271
  9.9 1.4 %collective-permute-start.4 = (f32[96,128]{1,0:T(8,128)S(1)}, f32[96,128]{1,0:T(8,128)S(1)}, u32[]{:S(2)}, u32[]{:S(2)}) collective-permute-start(f32[96,128]{1,0:T(8,128)S(1)} %get-tuple-element.18), channel_id=1, source_target_pairs={{0,3},{1,0},{2,1},{3,2},{4,7},{5,4},{6,5},{7,6},{8,11},{9,8},{10,9... | collective-permute-start | bytes 147464 | tf_op jit(solution)/shard_map/ppermute | solution.py:271
  11.3 1.6 %collective-permute-start.5 = (f32[96,128]{1,0:T(8,128)S(1)}, f32[96,128]{1,0:T(8,128)S(1)}, u32[]{:S(2)}, u32[]{:S(2)}) collective-permute-start(f32[96,128]{1,0:T(8,128)S(1)} %get-tuple-element.19), channel_id=1, source_target_pairs={{0,2},{1,3},{2,0},{3,1},{4,6},{5,7},{6,4},{7,5},{8,10},{9,11},{10,... | collective-permute-start | bytes 147464 | tf_op jit(solution)/shard_map/ppermute | solution.py:271
  12.9 2.5 %shard_map.39 = (f32[96,128]{1,0:T(8,128)S(1)}, f32[32,128]{1,0:T(8,128)S(1)}) custom-call(f32[512,32,128]{2,1,0:T(8,128)} %bitcast.7, bf16[256,128]{1,0:T(8,128)(2,1)S(1)} %get-tuple-element.14.weight_ref, f32[32,64]{1,0:T(8,128)S(1)} %copy-done, f32[32,128]{1,0:T(8,128)S(1)} %get-tuple-element.15.gram_ref), custom_call_target="tpu_custom_call" | custom-call | flops 2000000000 | bytes 8609792 | tf_op jit(solution)/shard_map/pallas_call | solution.py:218
  15.4 0.0 collective-permute-done.3.right_ref
  15.5 0.0 collective-permute-done.4.right_ref
  15.5 0.1 collective-permute-done.5.right_ref
  15.6 2.7 %collective-permute-start.6 = (f32[64,128]{1,0:T(8,128)S(1)}, f32[64,128]{1,0:T(8,128)S(1)}, u32[]{:S(2)}, u32[]{:S(2)}) collective-permute-start(f32[64,128]{1,0:T(8,128)S(1)} %get-tuple-element.21), channel_id=1, source_target_pairs={{0,4},{1,5},{2,6},{3,7},{4,0},{5,1},{6,2},{7,3},{8,12},{9,13},{10,... | collective-permute-start | bytes 98312 | tf_op jit(solution)/shard_map/ppermute | solution.py:289
  18.3 2.2 %collective-permute-done.6.refs_1_ = f32[64,128]{1,0:T(8,128)S(1)} collective-permute-done((f32[64,128]{1,0:T(8,128)S(1)}, f32[64,128]{1,0:T(8,128)S(1)}, u32[]{:S(2)}, u32[]{:S(2)}) %collective-permute-start.6) | collective-permute-done | bytes 32800 | tf_op jit(solution)/shard_map/ppermute | solution.py:289
  20.5 2.9 %shard_map.43 = f32[64,64]{1,0:T(8,128)} custom-call(f32[64,128]{1,0:T(8,128)S(1)} %get-tuple-element.20.refs_0_, f32[64,128]{1,0:T(8,128)S(1)} %collective-permute-done.6.refs_1_, f32[32,128]{1,0:T(8,128)S(1)} %get-tuple-element.22.refs_2_), custom_call_target="tpu_custom_call" | custom-call | flops 100000000 | bytes 98304 | tf_op jit(solution)/shard_map/pallas_call | solution.py:218
  (3 shorter events, 0.0 us)
Async XLA Ops:
  0.0 6.3 %copy-start.1 = (f32[128,16]{0,1:T(8,128)S(1)}, f32[128,16]{0,1:T(8,128)}, u32[]{:S(2)}) copy-start(f32[128,16]{0,1:T(8,128)} %param.4) | copy-start | bytes 24580
  0.0 6.3 %copy-start = (f32[32,64]{1,0:T(8,128)S(1)}, f32[32,64]{1,0:T(8,128)}, u32[]{:S(2)}) copy-start(f32[32,64]{1,0:T(8,128)} %three_ref.3) | copy-start | bytes 24580
  0.0 6.0 %collective-permute-start.2 = (f32[16,128]{1,0:T(8,128)}, f32[16,128]{1,0:T(8,128)S(1)}, u32[]{:S(2)}, u32[]{:S(2)}) collective-permute-start(f32[16,128]{1,0:T(8,128)} %bitcast.2), channel_id=1, source_target_pairs={{0,24},{8,16},{16,8},{24,0},{1,25},{9,17},{17,9},{25,1},{2,26},{10... | collective-permute-start | bytes 24584 | tf_op jit(solution)/shard_map/ppermute | solution.py:249
  2.4 3.9 %collective-permute-start.1 = (f32[16,128]{1,0:T(8,128)}, f32[16,128]{1,0:T(8,128)S(1)}, u32[]{:S(2)}, u32[]{:S(2)}) collective-permute-start(f32[16,128]{1,0:T(8,128)} %bitcast.3), channel_id=1, source_target_pairs={{0,16},{8,24},{16,0},{24,8},{1,17},{9,25},{17,1},{25,9},{2,18},{10... | collective-permute-start | bytes 24584 | tf_op jit(solution)/shard_map/ppermute | solution.py:249
  3.0 3.2 %collective-permute-start = (f32[16,128]{1,0:T(8,128)}, f32[16,128]{1,0:T(8,128)S(1)}, u32[]{:S(2)}, u32[]{:S(2)}) collective-permute-start(f32[16,128]{1,0:T(8,128)} %bitcast.4), channel_id=1, source_target_pairs={{0,8},{8,0},{16,24},{24,16},{1,9},{9,1},{17,25},{25,17},{2,10},{10... | collective-permute-start | bytes 24584 | tf_op jit(solution)/shard_map/ppermute | solution.py:249
  8.4 7.0 %collective-permute-start.3 = (f32[96,128]{1,0:T(8,128)S(1)}, f32[96,128]{1,0:T(8,128)S(1)}, u32[]{:S(2)}, u32[]{:S(2)}) collective-permute-start(f32[96,128]{1,0:T(8,128)S(1)} %get-tuple-element.17), channel_id=1, source_target_pairs={{0,1},{1,2},{2,3},{3,0},{4,5},{5,6},{6,7},{7,4},{8,9},{9,10},{10,1... | collective-permute-start | bytes 147464 | tf_op jit(solution)/shard_map/ppermute | solution.py:271
  9.9 5.5 %collective-permute-start.4 = (f32[96,128]{1,0:T(8,128)S(1)}, f32[96,128]{1,0:T(8,128)S(1)}, u32[]{:S(2)}, u32[]{:S(2)}) collective-permute-start(f32[96,128]{1,0:T(8,128)S(1)} %get-tuple-element.18), channel_id=1, source_target_pairs={{0,3},{1,0},{2,1},{3,2},{4,7},{5,4},{6,5},{7,6},{8,11},{9,8},{10,9... | collective-permute-start | bytes 147464 | tf_op jit(solution)/shard_map/ppermute | solution.py:271
  11.3 4.2 %collective-permute-start.5 = (f32[96,128]{1,0:T(8,128)S(1)}, f32[96,128]{1,0:T(8,128)S(1)}, u32[]{:S(2)}, u32[]{:S(2)}) collective-permute-start(f32[96,128]{1,0:T(8,128)S(1)} %get-tuple-element.19), channel_id=1, source_target_pairs={{0,2},{1,3},{2,0},{3,1},{4,6},{5,7},{6,4},{7,5},{8,10},{9,11},{10,... | collective-permute-start | bytes 147464 | tf_op jit(solution)/shard_map/ppermute | solution.py:271
  15.6 4.9 %collective-permute-start.6 = (f32[64,128]{1,0:T(8,128)S(1)}, f32[64,128]{1,0:T(8,128)S(1)}, u32[]{:S(2)}, u32[]{:S(2)}) collective-permute-start(f32[64,128]{1,0:T(8,128)S(1)} %get-tuple-element.21), channel_id=1, source_target_pairs={{0,4},{1,5},{2,6},{3,7},{4,0},{5,1},{6,2},{7,3},{8,12},{9,13},{10,... | collective-permute-start | bytes 98312 | tf_op jit(solution)/shard_map/ppermute | solution.py:289

commit v5 on v4

--- a/solution.py
+++ b/solution.py
@@ -18,21 +18,12 @@
     )
 
 
-def narrow_dot(left, right, dims):
-    return lax.dot_general(left, right, ((dims[:1], dims[1:]), ((), ())), preferred_element_type=jnp.float32)
-
-
-def parted(values):
-    high = values.astype(jnp.bfloat16).astype(jnp.float32)
-    return high, values - high
-
-
 def pack(values):
     half = values.shape[0] // 2
     return jnp.concatenate([values[:half], values[half:]], axis=1)
 
 
-ROUNDS = [(1, 2, 3, 0), (3, 0, 1, 2), (2, 3, 0, 1)]
+ROUNDS = [(2, 3, 1, 0), (3, 2, 0, 1), (1, 0, 3, 2)]
 
 
 def pick(table, place):
@@ -195,21 +186,9 @@
                 for p in range(q + 1, 8):
                     column[h][p] = column[h][p] - scale * entry[q][p]
         bands[own] = band
-    left = lane_ids < order
-    lower = jnp.where(left, jnp.concatenate(bands, axis=0), 0.0)
-    lower_high, lower_low = parted(lower)
-    right_high, right_low = parted(right)
-    doubled = lower_high + pltpu.roll(lower_high, order, 1)
-    factors = jnp.concatenate([doubled, lower_low], axis=1).astype(jnp.bfloat16)
-    terms = jnp.concatenate([right_high + pltpu.roll(right_low, order, 1), right_high], axis=1).astype(jnp.bfloat16)
-    solved = narrow_dot(terms, jnp.concatenate([factors, factors], axis=0), (1, 1))
-    solved_high, solved_low = parted(solved)
-    inside = lax.broadcasted_iota(jnp.int32, solved.shape, 1) < order
-    terms = jnp.concatenate(
-        [jnp.where(inside, solved_high, solved_low), jnp.where(inside, solved_high, 0.0)], axis=1
-    ).astype(jnp.bfloat16)
-    factors = jnp.concatenate([lower_high, lower_high, lower_low, lower_low], axis=0).astype(jnp.bfloat16)
-    out_ref[...] = narrow_dot(terms, factors, (1, 0))[:, :order]
+    lower = jnp.concatenate(bands, axis=0)
+    solved = dot_of(right, lower, (1, 1))
+    out_ref[...] = dot_of(solved, lower, (1, 0))[:, :order]
 
 
 def call(kernel, out_shape, args, flops, limit, scratch=(), specs=None):

time: 23.5 us -> 23.4 us (level)
  transfers between devices with their start and end apart: 7 -> 7, of which waited for: 3 -> 2; matrix products, arithmetic and copies ran while one was open for 0% -> 0% of each run, Pallas kernels for 23% -> 23%
where the time goes in v5:
time: 23.4 us; the launch traced here: 23.2 us
  Pallas kernels  10.5 us (45%)
  starting transfers between devices  10.2 us (44%)
  waiting for transfers between devices  2.45 us (10%)
    pallas_call x7, Pallas kernels, call(): pl.pallas_call(kernel, out_shape=out_shape, in_specs=specs or [WHOLE] * l...  10.5 us
    ppermute x3, starting transfers between devices, body(): lax.ppermute(value, 'gy', [(i, i - i % 4 + table[i % 4]) for i in range(b...  4.45 us
    ppermute x3, starting transfers between devices, body(): lax.ppermute(mine, 'gx', [(i, i ^ distance) for i in range(groups)])  3.08 us
    ppermute x1, starting transfers between devices, body(): lax.ppermute(value, 'gy', [(i, i ^ 4 * distance) for i in range(blocks)])  2.68 us
    ppermute x1, waiting for transfers between devices, body(): lax.ppermute(value, 'gy', [(i, i ^ 4 * distance) for i in range(blocks)])  2.2 us
  transfers between devices with their start and end apart: 7, of which 2 were waited for; matrix products, arithmetic and copies ran while one was open for 0% of the time, Pallas kernels for 23%

profile of v5, /device:TPU:0, one launch (start us, length us, event | category | flops | bytes accessed | tf_op | source)
XLA Modules:
  0.0 23.2 jit_solution(143479877514237831)
XLA Ops:
  0.0 0.0 copy-start.1
  0.0 0.0 copy-start
  0.0 2.4 %collective-permute-start.2 = (f32[16,128]{1,0:T(8,128)}, f32[16,128]{1,0:T(8,128)S(1)}, u32[]{:S(2)}, u32[]{:S(2)}) collective-permute-start(f32[16,128]{1,0:T(8,128)} %bitcast.2), channel_id=1, source_target_pairs={{0,24},{8,16},{16,8},{24,0},{1,25},{9,17},{17,9},{25,1},{2,26},{10... | collective-permute-start | bytes 24584 | tf_op jit(solution)/shard_map/ppermute | solution.py:228
  2.4 0.6 %collective-permute-start.1 = (f32[16,128]{1,0:T(8,128)}, f32[16,128]{1,0:T(8,128)S(1)}, u32[]{:S(2)}, u32[]{:S(2)}) collective-permute-start(f32[16,128]{1,0:T(8,128)} %bitcast.3), channel_id=1, source_target_pairs={{0,16},{8,24},{16,0},{24,8},{1,17},{9,25},{17,1},{25,9},{2,18},{10... | collective-permute-start | bytes 24584 | tf_op jit(solution)/shard_map/ppermute | solution.py:228
  3.0 0.0 collective-permute-start
  3.1 2.9 %shard_map.37.split_ref = bf16[12288,256]{1,0:T(8,128)(2,1)S(1)} custom-call(f32[512,32,128]{2,1,0:T(8,128)} %bitcast.6), custom_call_target="tpu_custom_call" | custom-call | flops 1000000000 | bytes 20971520 | tf_op jit(solution)/shard_map/pallas_call | solution.py:197
  6.0 0.0 collective-permute-done.2.refs_3_
  6.0 0.2 collective-permute-done.1.refs_2_
  6.3 0.0 collective-permute-done.refs_1_
  6.3 0.0 copy-done.1
  6.3 0.0 copy-done
  6.3 2.1 %shard_map.38 = (f32[96,128]{1,0:T(8,128)S(1)}, f32[96,128]{1,0:T(8,128)S(1)}, f32[96,128]{1,0:T(8,128)S(1)}, f32[32,128]{1,0:T(8,128)S(1)}, bf16[256,128]{1,0:T(8,128)(2,1)S(1)}) custom-call(bf16[12288,256]{1,0:T(8,128)(2,1)S(1)} %shard_map.37.split_ref, f32[32,64]{1,0:T(8,128)S(1)} %copy-done, f32[16,128]{1,0:T(8,128)S(1)} %bitcast.5, ...), custom_call_target="tpu_custom_call" | custom-call | flops 2000000000 | bytes 12918784 | tf_op jit(solution)/shard_map/pallas_call | solution.py:197
  8.4 1.6 %collective-permute-start.3 = (f32[96,128]{1,0:T(8,128)S(1)}, f32[96,128]{1,0:T(8,128)S(1)}, u32[]{:S(2)}, u32[]{:S(2)}) collective-permute-start(f32[96,128]{1,0:T(8,128)S(1)} %get-tuple-element.17), channel_id=1, source_target_pairs={{0,2},{1,3},{2,1},{3,0},{4,6},{5,7},{6,5},{7,4},{8,10},{9,11},{10,... | collective-permute-start | bytes 147464 | tf_op jit(solution)/shard_map/ppermute | solution.py:250
  10.0 1.3 %collective-permute-start.4 = (f32[96,128]{1,0:T(8,128)S(1)}, f32[96,128]{1,0:T(8,128)S(1)}, u32[]{:S(2)}, u32[]{:S(2)}) collective-permute-start(f32[96,128]{1,0:T(8,128)S(1)} %get-tuple-element.18), channel_id=1, source_target_pairs={{0,3},{1,2},{2,0},{3,1},{4,7},{5,6},{6,4},{7,5},{8,11},{9,10},{10,... | collective-permute-start | bytes 147464 | tf_op jit(solution)/shard_map/ppermute | solution.py:250
  11.3 1.5 %collective-permute-start.5 = (f32[96,128]{1,0:T(8,128)S(1)}, f32[96,128]{1,0:T(8,128)S(1)}, u32[]{:S(2)}, u32[]{:S(2)}) collective-permute-start(f32[96,128]{1,0:T(8,128)S(1)} %get-tuple-element.19), channel_id=1, source_target_pairs={{0,1},{1,0},{2,3},{3,2},{4,5},{5,4},{6,7},{7,6},{8,9},{9,8},{10,11... | collective-permute-start | bytes 147464 | tf_op jit(solution)/shard_map/ppermute | solution.py:250
  12.9 2.5 %shard_map.39 = (f32[96,128]{1,0:T(8,128)S(1)}, f32[32,128]{1,0:T(8,128)S(1)}) custom-call(f32[512,32,128]{2,1,0:T(8,128)} %bitcast.7, bf16[256,128]{1,0:T(8,128)(2,1)S(1)} %get-tuple-element.14.weight_ref, f32[32,64]{1,0:T(8,128)S(1)} %copy-done, f32[32,128]{1,0:T(8,128)S(1)} %get-tuple-element.15.gram_ref), custom_call_target="tpu_custom_call" | custom-call | flops 2000000000 | bytes 8609792 | tf_op jit(solution)/shard_map/pallas_call | solution.py:197
  15.4 0.0 collective-permute-done.3.right_ref
  15.4 0.0 collective-permute-done.4.right_ref
  15.4 0.0 collective-permute-done.5.right_ref
  15.4 2.7 %collective-permute-start.6 = (f32[64,128]{1,0:T(8,128)S(1)}, f32[64,128]{1,0:T(8,128)S(1)}, u32[]{:S(2)}, u32[]{:S(2)}) collective-permute-start(f32[64,128]{1,0:T(8,128)S(1)} %get-tuple-element.21), channel_id=1, source_target_pairs={{0,4},{1,5},{2,6},{3,7},{4,0},{5,1},{6,2},{7,3},{8,12},{9,13},{10,... | collective-permute-start | bytes 98312 | tf_op jit(solution)/shard_map/ppermute | solution.py:268
  18.1 2.2 %collective-permute-done.6.refs_1_ = f32[64,128]{1,0:T(8,128)S(1)} collective-permute-done((f32[64,128]{1,0:T(8,128)S(1)}, f32[64,128]{1,0:T(8,128)S(1)}, u32[]{:S(2)}, u32[]{:S(2)}) %collective-permute-start.6) | collective-permute-done | bytes 32800 | tf_op jit(solution)/shard_map/ppermute | solution.py:268
  20.3 2.9 %shard_map.43 = f32[64,64]{1,0:T(8,128)} custom-call(f32[64,128]{1,0:T(8,128)S(1)} %get-tuple-element.20.refs_0_, f32[64,128]{1,0:T(8,128)S(1)} %collective-permute-done.6.refs_1_, f32[32,128]{1,0:T(8,128)S(1)} %get-tuple-element.22.refs_2_), custom_call_target="tpu_custom_call" | custom-call | flops 100000000 | bytes 98304 | tf_op jit(solution)/shard_map/pallas_call | solution.py:197
  (3 shorter events, 0.0 us)
Async XLA Ops:
  0.0 6.3 %copy-start.1 = (f32[128,16]{0,1:T(8,128)S(1)}, f32[128,16]{0,1:T(8,128)}, u32[]{:S(2)}) copy-start(f32[128,16]{0,1:T(8,128)} %param.4) | copy-start | bytes 24580
  0.0 6.3 %copy-start = (f32[32,64]{1,0:T(8,128)S(1)}, f32[32,64]{1,0:T(8,128)}, u32[]{:S(2)}) copy-start(f32[32,64]{1,0:T(8,128)} %three_ref.3) | copy-start | bytes 24580
  0.0 6.0 %collective-permute-start.2 = (f32[16,128]{1,0:T(8,128)}, f32[16,128]{1,0:T(8,128)S(1)}, u32[]{:S(2)}, u32[]{:S(2)}) collective-permute-start(f32[16,128]{1,0:T(8,128)} %bitcast.2), channel_id=1, source_target_pairs={{0,24},{8,16},{16,8},{24,0},{1,25},{9,17},{17,9},{25,1},{2,26},{10... | collective-permute-start | bytes 24584 | tf_op jit(solution)/shard_map/ppermute | solution.py:228
  2.4 3.9 %collective-permute-start.1 = (f32[16,128]{1,0:T(8,128)}, f32[16,128]{1,0:T(8,128)S(1)}, u32[]{:S(2)}, u32[]{:S(2)}) collective-permute-start(f32[16,128]{1,0:T(8,128)} %bitcast.3), channel_id=1, source_target_pairs={{0,16},{8,24},{16,0},{24,8},{1,17},{9,25},{17,1},{25,9},{2,18},{10... | collective-permute-start | bytes 24584 | tf_op jit(solution)/shard_map/ppermute | solution.py:228
  3.0 3.2 %collective-permute-start = (f32[16,128]{1,0:T(8,128)}, f32[16,128]{1,0:T(8,128)S(1)}, u32[]{:S(2)}, u32[]{:S(2)}) collective-permute-start(f32[16,128]{1,0:T(8,128)} %bitcast.4), channel_id=1, source_target_pairs={{0,8},{8,0},{16,24},{24,16},{1,9},{9,1},{17,25},{25,17},{2,10},{10... | collective-permute-start | bytes 24584 | tf_op jit(solution)/shard_map/ppermute | solution.py:228
  8.4 7.0 %collective-permute-start.3 = (f32[96,128]{1,0:T(8,128)S(1)}, f32[96,128]{1,0:T(8,128)S(1)}, u32[]{:S(2)}, u32[]{:S(2)}) collective-permute-start(f32[96,128]{1,0:T(8,128)S(1)} %get-tuple-element.17), channel_id=1, source_target_pairs={{0,2},{1,3},{2,1},{3,0},{4,6},{5,7},{6,5},{7,4},{8,10},{9,11},{10,... | collective-permute-start | bytes 147464 | tf_op jit(solution)/shard_map/ppermute | solution.py:250
  10.0 5.4 %collective-permute-start.4 = (f32[96,128]{1,0:T(8,128)S(1)}, f32[96,128]{1,0:T(8,128)S(1)}, u32[]{:S(2)}, u32[]{:S(2)}) collective-permute-start(f32[96,128]{1,0:T(8,128)S(1)} %get-tuple-element.18), channel_id=1, source_target_pairs={{0,3},{1,2},{2,0},{3,1},{4,7},{5,6},{6,4},{7,5},{8,11},{9,10},{10,... | collective-permute-start | bytes 147464 | tf_op jit(solution)/shard_map/ppermute | solution.py:250
  11.3 4.1 %collective-permute-start.5 = (f32[96,128]{1,0:T(8,128)S(1)}, f32[96,128]{1,0:T(8,128)S(1)}, u32[]{:S(2)}, u32[]{:S(2)}) collective-permute-start(f32[96,128]{1,0:T(8,128)S(1)} %get-tuple-element.19), channel_id=1, source_target_pairs={{0,1},{1,0},{2,3},{3,2},{4,5},{5,4},{6,7},{7,6},{8,9},{9,8},{10,11... | collective-permute-start | bytes 147464 | tf_op jit(solution)/shard_map/ppermute | solution.py:250
  15.4 4.9 %collective-permute-start.6 = (f32[64,128]{1,0:T(8,128)S(1)}, f32[64,128]{1,0:T(8,128)S(1)}, u32[]{:S(2)}, u32[]{:S(2)}) collective-permute-start(f32[64,128]{1,0:T(8,128)S(1)} %get-tuple-element.21), channel_id=1, source_target_pairs={{0,4},{1,5},{2,6},{3,7},{4,0},{5,1},{6,2},{7,3},{8,12},{9,13},{10,... | collective-permute-start | bytes 98312 | tf_op jit(solution)/shard_map/ppermute | solution.py:268

commit v6 on v5

--- a/solution.py
+++ b/solution.py
@@ -23,7 +23,7 @@
     return jnp.concatenate([values[:half], values[half:]], axis=1)
 
 
-ROUNDS = [(2, 3, 1, 0), (3, 2, 0, 1), (1, 0, 3, 2)]
+ROUNDS = [(3, 2, 1, 0), (2, 3, 0, 1), (1, 0, 3, 2)]
 
 
 def pick(table, place):
@@ -164,28 +164,38 @@
         return jnp.broadcast_to(value[:, order + index : order + index + 1], tile)
 
     for own in range(len(bands)):
-        base, later = 8 * own, range(own + 1, len(bands))
+        base = 8 * own
         line = [jnp.broadcast_to(bands[own][q : q + 1], tile) for q in range(8)]
         entry = [[lane(line[q], base + p) if p >= q else None for p in range(8)] for q in range(8)]
-        column = {h: [lane(bands[h], base + q) for q in range(8)] for h in later}
-        band = None
+        inverse, done = [None] * 8, None
+
+        def follow(band, column, q):
+            scale = column[q] * inverse[q]
+            band = band - scale * line[q]
+            for p in range(q + 1, 8):
+                column[p] = column[p] - scale * entry[q][p]
+            return band
+
+        near = bands[own + 1 : own + 2]
+        column = [lane(band, base + q) for band in near for q in range(8)]
         for q in range(8):
             pivot = entry[q][q]
-            inverse = pltpu.reciprocal(pivot, approx=True)
+            inverse[q] = pltpu.reciprocal(pivot, approx=True)
             row = line[q] * lax.rsqrt(pivot)
-            band = row if band is None else jnp.where(places == q, row, band)
-            factor = [entry[q][p] * inverse if p > q else None for p in range(8)]
+            done = row if done is None else jnp.where(places == q, row, done)
+            factor = [entry[q][p] * inverse[q] if p > q else None for p in range(8)]
             for p in range(q + 1, 8):
-                entry[p][p] = entry[p][p] - (entry[q][p] * entry[q][p]) * inverse
+                entry[p][p] = entry[p][p] - (entry[q][p] * entry[q][p]) * inverse[q]
                 for s in range(p + 1, 8):
                     entry[p][s] = entry[p][s] - factor[p] * entry[q][s]
                 line[p] = line[p] - factor[p] * line[q]
-            for h in later:
-                scale = column[h][q] * inverse
-                bands[h] = bands[h] - scale * line[q]
-                for p in range(q + 1, 8):
-                    column[h][p] = column[h][p] - scale * entry[q][p]
-        bands[own] = band
+            if near:
+                bands[own + 1] = follow(bands[own + 1], column, q)
+        bands[own] = done
+        for h in range(own + 2, len(bands)):
+            column = [lane(bands[h], base + q) for q in range(8)]
+            for q in range(8):
+                bands[h] = follow(bands[h], column, q)
     lower = jnp.concatenate(bands, axis=0)
     solved = dot_of(right, lower, (1, 1))
     out_ref[...] = dot_of(solved, lower, (1, 0))[:, :order]

time: 23.4 us -> 23.4 us (level)
  waiting for transfers between devices: 2.45 us -> 3.48 us
  starting transfers between devices: 10.2 us -> 9.24 us
    ppermute x3, waiting for transfers between devices: 0.02 us -> 1.02 us  [body(): lax.ppermute(value, 'gy', [(i, i - i % 4 + table[i % 4]) for i in range(b...]
    ppermute x3, starting transfers between devices: 4.45 us -> 3.5 us  [body(): lax.ppermute(value, 'gy', [(i, i - i % 4 + table[i % 4]) for i in range(b...]
  transfers between devices with their start and end apart: 7 -> 7, of which waited for: 2 -> 4; matrix products, arithmetic and copies ran while one was open for 0% -> 0% of each run, Pallas kernels for 23% -> 23%
where the time goes in v6:
time: 23.4 us; the launch traced here: 23.3 us
  Pallas kernels  10.5 us (45%)
  starting transfers between devices  9.24 us (39%)
  waiting for transfers between devices  3.48 us (15%)
    pallas_call x7, Pallas kernels, call(): pl.pallas_call(kernel, out_shape=out_shape, in_specs=specs or [WHOLE] * l...  10.5 us
    ppermute x3, starting transfers between devices, body(): lax.ppermute(value, 'gy', [(i, i - i % 4 + table[i % 4]) for i in range(b...  3.5 us
    ppermute x3, starting transfers between devices, body(): lax.ppermute(mine, 'gx', [(i, i ^ distance) for i in range(groups)])  3.08 us
    ppermute x1, starting transfers between devices, body(): lax.ppermute(value, 'gy', [(i, i ^ 4 * distance) for i in range(blocks)])  2.65 us
    ppermute x1, waiting for transfers between devices, body(): lax.ppermute(value, 'gy', [(i, i ^ 4 * distance) for i in range(blocks)])  2.22 us
    ppermute x3, waiting for transfers between devices, body(): lax.ppermute(value, 'gy', [(i, i - i % 4 + table[i % 4]) for i in range(b...  1.02 us
  transfers between devices with their start and end apart: 7, of which 4 were waited for; matrix products, arithmetic and copies ran while one was open for 0% of the time, Pallas kernels for 23%

profile of v6, /device:TPU:0, one launch (start us, length us, event | category | flops | bytes accessed | tf_op | source)
XLA Modules:
  0.0 23.3 jit_solution(16276286057865737770)
XLA Ops:
  0.0 0.0 copy-start.1
  0.0 0.0 copy-start
  0.0 2.4 %collective-permute-start.2 = (f32[16,128]{1,0:T(8,128)}, f32[16,128]{1,0:T(8,128)S(1)}, u32[]{:S(2)}, u32[]{:S(2)}) collective-permute-start(f32[16,128]{1,0:T(8,128)} %bitcast.2), channel_id=1, source_target_pairs={{0,24},{8,16},{16,8},{24,0},{1,25},{9,17},{17,9},{25,1},{2,26},{10... | collective-permute-start | bytes 24584 | tf_op jit(solution)/shard_map/ppermute | solution.py:238
  2.4 0.6 %collective-permute-start.1 = (f32[16,128]{1,0:T(8,128)}, f32[16,128]{1,0:T(8,128)S(1)}, u32[]{:S(2)}, u32[]{:S(2)}) collective-permute-start(f32[16,128]{1,0:T(8,128)} %bitcast.3), channel_id=1, source_target_pairs={{0,16},{8,24},{16,0},{24,8},{1,17},{9,25},{17,1},{25,9},{2,18},{10... | collective-permute-start | bytes 24584 | tf_op jit(solution)/shard_map/ppermute | solution.py:238
  3.0 0.0 collective-permute-start
  3.1 2.9 %shard_map.37.split_ref = bf16[12288,256]{1,0:T(8,128)(2,1)S(1)} custom-call(f32[512,32,128]{2,1,0:T(8,128)} %bitcast.6), custom_call_target="tpu_custom_call" | custom-call | flops 1000000000 | bytes 20971520 | tf_op jit(solution)/shard_map/pallas_call | solution.py:207
  6.0 0.0 collective-permute-done.2.refs_3_
  6.0 0.2 collective-permute-done.1.refs_2_
  6.3 0.0 collective-permute-done.refs_1_
  6.3 0.0 copy-done.1
  6.3 0.0 copy-done
  6.3 2.1 %shard_map.38 = (f32[96,128]{1,0:T(8,128)S(1)}, f32[96,128]{1,0:T(8,128)S(1)}, f32[96,128]{1,0:T(8,128)S(1)}, f32[32,128]{1,0:T(8,128)S(1)}, bf16[256,128]{1,0:T(8,128)(2,1)S(1)}) custom-call(bf16[12288,256]{1,0:T(8,128)(2,1)S(1)} %shard_map.37.split_ref, f32[32,64]{1,0:T(8,128)S(1)} %copy-done, f32[16,128]{1,0:T(8,128)S(1)} %bitcast.5, ...), custom_call_target="tpu_custom_call" | custom-call | flops 2000000000 | bytes 12918784 | tf_op jit(solution)/shard_map/pallas_call | solution.py:207
  8.4 2.5 %collective-permute-start.3 = (f32[96,128]{1,0:T(8,128)S(1)}, f32[96,128]{1,0:T(8,128)S(1)}, u32[]{:S(2)}, u32[]{:S(2)}) collective-permute-start(f32[96,128]{1,0:T(8,128)S(1)} %get-tuple-element.17), channel_id=1, source_target_pairs={{0,3},{1,2},{2,1},{3,0},{4,7},{5,6},{6,5},{7,4},{8,11},{9,10},{10,... | collective-permute-start | bytes 147464 | tf_op jit(solution)/shard_map/ppermute | solution.py:260
  11.0 0.4 %collective-permute-start.4 = (f32[96,128]{1,0:T(8,128)S(1)}, f32[96,128]{1,0:T(8,128)S(1)}, u32[]{:S(2)}, u32[]{:S(2)}) collective-permute-start(f32[96,128]{1,0:T(8,128)S(1)} %get-tuple-element.18), channel_id=1, source_target_pairs={{0,2},{1,3},{2,0},{3,1},{4,6},{5,7},{6,4},{7,5},{8,10},{9,11},{10,... | collective-permute-start | bytes 147464 | tf_op jit(solution)/shard_map/ppermute | solution.py:260
  11.4 0.5 %collective-permute-start.5 = (f32[96,128]{1,0:T(8,128)S(1)}, f32[96,128]{1,0:T(8,128)S(1)}, u32[]{:S(2)}, u32[]{:S(2)}) collective-permute-start(f32[96,128]{1,0:T(8,128)S(1)} %get-tuple-element.19), channel_id=1, source_target_pairs={{0,1},{1,0},{2,3},{3,2},{4,5},{5,4},{6,7},{7,6},{8,9},{9,8},{10,11... | collective-permute-start | bytes 147464 | tf_op jit(solution)/shard_map/ppermute | solution.py:260
  11.9 2.5 %shard_map.39 = (f32[96,128]{1,0:T(8,128)S(1)}, f32[32,128]{1,0:T(8,128)S(1)}) custom-call(f32[512,32,128]{2,1,0:T(8,128)} %bitcast.7, bf16[256,128]{1,0:T(8,128)(2,1)S(1)} %get-tuple-element.14.weight_ref, f32[32,64]{1,0:T(8,128)S(1)} %copy-done, f32[32,128]{1,0:T(8,128)S(1)} %get-tuple-element.15.gram_ref), custom_call_target="tpu_custom_call" | custom-call | flops 2000000000 | bytes 8609792 | tf_op jit(solution)/shard_map/pallas_call | solution.py:207
  14.4 0.0 collective-permute-done.3.right_ref
  14.5 0.6 %collective-permute-done.4.right_ref = f32[96,128]{1,0:T(8,128)S(1)} collective-permute-done((f32[96,128]{1,0:T(8,128)S(1)}, f32[96,128]{1,0:T(8,128)S(1)}, u32[]{:S(2)}, u32[]{:S(2)}) %collective-permute-start.4) | collective-permute-done | bytes 49184 | tf_op jit(solution)/shard_map/ppermute | solution.py:260
  15.1 0.4 %collective-permute-done.5.right_ref = f32[96,128]{1,0:T(8,128)S(1)} collective-permute-done((f32[96,128]{1,0:T(8,128)S(1)}, f32[96,128]{1,0:T(8,128)S(1)}, u32[]{:S(2)}, u32[]{:S(2)}) %collective-permute-start.5) | collective-permute-done | bytes 49184 | tf_op jit(solution)/shard_map/ppermute | solution.py:260
  15.5 2.7 %collective-permute-start.6 = (f32[64,128]{1,0:T(8,128)S(1)}, f32[64,128]{1,0:T(8,128)S(1)}, u32[]{:S(2)}, u32[]{:S(2)}) collective-permute-start(f32[64,128]{1,0:T(8,128)S(1)} %get-tuple-element.21), channel_id=1, source_target_pairs={{0,4},{1,5},{2,6},{3,7},{4,0},{5,1},{6,2},{7,3},{8,12},{9,13},{10,... | collective-permute-start | bytes 98312 | tf_op jit(solution)/shard_map/ppermute | solution.py:278
  18.2 2.2 %collective-permute-done.6.refs_1_ = f32[64,128]{1,0:T(8,128)S(1)} collective-permute-done((f32[64,128]{1,0:T(8,128)S(1)}, f32[64,128]{1,0:T(8,128)S(1)}, u32[]{:S(2)}, u32[]{:S(2)}) %collective-permute-start.6) | collective-permute-done | bytes 32800 | tf_op jit(solution)/shard_map/ppermute | solution.py:278
  20.4 2.9 %shard_map.43 = f32[64,64]{1,0:T(8,128)} custom-call(f32[64,128]{1,0:T(8,128)S(1)} %get-tuple-element.20.refs_0_, f32[64,128]{1,0:T(8,128)S(1)} %collective-permute-done.6.refs_1_, f32[32,128]{1,0:T(8,128)S(1)} %get-tuple-element.22.refs_2_), custom_call_target="tpu_custom_call" | custom-call | flops 100000000 | bytes 98304 | tf_op jit(solution)/shard_map/pallas_call | solution.py:207
  (3 shorter events, 0.0 us)
Async XLA Ops:
  0.0 6.3 %copy-start.1 = (f32[128,16]{0,1:T(8,128)S(1)}, f32[128,16]{0,1:T(8,128)}, u32[]{:S(2)}) copy-start(f32[128,16]{0,1:T(8,128)} %param.4) | copy-start | bytes 24580
  0.0 6.3 %copy-start = (f32[32,64]{1,0:T(8,128)S(1)}, f32[32,64]{1,0:T(8,128)}, u32[]{:S(2)}) copy-start(f32[32,64]{1,0:T(8,128)} %three_ref.3) | copy-start | bytes 24580
  0.0 6.0 %collective-permute-start.2 = (f32[16,128]{1,0:T(8,128)}, f32[16,128]{1,0:T(8,128)S(1)}, u32[]{:S(2)}, u32[]{:S(2)}) collective-permute-start(f32[16,128]{1,0:T(8,128)} %bitcast.2), channel_id=1, source_target_pairs={{0,24},{8,16},{16,8},{24,0},{1,25},{9,17},{17,9},{25,1},{2,26},{10... | collective-permute-start | bytes 24584 | tf_op jit(solution)/shard_map/ppermute | solution.py:238
  2.4 3.9 %collective-permute-start.1 = (f32[16,128]{1,0:T(8,128)}, f32[16,128]{1,0:T(8,128)S(1)}, u32[]{:S(2)}, u32[]{:S(2)}) collective-permute-start(f32[16,128]{1,0:T(8,128)} %bitcast.3), channel_id=1, source_target_pairs={{0,16},{8,24},{16,0},{24,8},{1,17},{9,25},{17,1},{25,9},{2,18},{10... | collective-permute-start | bytes 24584 | tf_op jit(solution)/shard_map/ppermute | solution.py:238
  3.0 3.2 %collective-permute-start = (f32[16,128]{1,0:T(8,128)}, f32[16,128]{1,0:T(8,128)S(1)}, u32[]{:S(2)}, u32[]{:S(2)}) collective-permute-start(f32[16,128]{1,0:T(8,128)} %bitcast.4), channel_id=1, source_target_pairs={{0,8},{8,0},{16,24},{24,16},{1,9},{9,1},{17,25},{25,17},{2,10},{10... | collective-permute-start | bytes 24584 | tf_op jit(solution)/shard_map/ppermute | solution.py:238
  8.4 6.0 %collective-permute-start.3 = (f32[96,128]{1,0:T(8,128)S(1)}, f32[96,128]{1,0:T(8,128)S(1)}, u32[]{:S(2)}, u32[]{:S(2)}) collective-permute-start(f32[96,128]{1,0:T(8,128)S(1)} %get-tuple-element.17), channel_id=1, source_target_pairs={{0,3},{1,2},{2,1},{3,0},{4,7},{5,6},{6,5},{7,4},{8,11},{9,10},{10,... | collective-permute-start | bytes 147464 | tf_op jit(solution)/shard_map/ppermute | solution.py:260
  11.0 4.1 %collective-permute-start.4 = (f32[96,128]{1,0:T(8,128)S(1)}, f32[96,128]{1,0:T(8,128)S(1)}, u32[]{:S(2)}, u32[]{:S(2)}) collective-permute-start(f32[96,128]{1,0:T(8,128)S(1)} %get-tuple-element.18), channel_id=1, source_target_pairs={{0,2},{1,3},{2,0},{3,1},{4,6},{5,7},{6,4},{7,5},{8,10},{9,11},{10,... | collective-permute-start | bytes 147464 | tf_op jit(solution)/shard_map/ppermute | solution.py:260
  11.4 4.1 %collective-permute-start.5 = (f32[96,128]{1,0:T(8,128)S(1)}, f32[96,128]{1,0:T(8,128)S(1)}, u32[]{:S(2)}, u32[]{:S(2)}) collective-permute-start(f32[96,128]{1,0:T(8,128)S(1)} %get-tuple-element.19), channel_id=1, source_target_pairs={{0,1},{1,0},{2,3},{3,2},{4,5},{5,4},{6,7},{7,6},{8,9},{9,8},{10,11... | collective-permute-start | bytes 147464 | tf_op jit(solution)/shard_map/ppermute | solution.py:260
  15.5 4.9 %collective-permute-start.6 = (f32[64,128]{1,0:T(8,128)S(1)}, f32[64,128]{1,0:T(8,128)S(1)}, u32[]{:S(2)}, u32[]{:S(2)}) collective-permute-start(f32[64,128]{1,0:T(8,128)S(1)} %get-tuple-element.21), channel_id=1, source_target_pairs={{0,4},{1,5},{2,6},{3,7},{4,0},{5,1},{6,2},{7,3},{8,12},{9,13},{10,... | collective-permute-start | bytes 98312 | tf_op jit(solution)/shard_map/ppermute | solution.py:278

commit v7 on v6

--- a/solution.py
+++ b/solution.py
@@ -99,10 +99,8 @@
     gram_ref[...] = gram
     for out_ref in outs:
         out_ref[count * (sum_ref.shape[0] // 2) :, :] = gram
-    turned = two.T
-    high = turned.astype(jnp.bfloat16)
-    low = (turned - high.astype(jnp.float32)).astype(jnp.bfloat16)
-    both = jnp.concatenate([high, low], axis=1)
+    high = two.astype(jnp.bfloat16).astype(jnp.float32)
+    both = jnp.concatenate([high, two - high], axis=0).T.astype(jnp.bfloat16)
     weight_ref[...] = jnp.concatenate([both, both], axis=0)
 
     def take(start):
@@ -129,20 +127,21 @@
     out_ref[count * (sum_ref.shape[0] // 2) :, :] = gram_ref[...]
 
 
-def add_kernel(left_ref, right_ref, out_ref):
-    out_ref[...] = left_ref[...] + right_ref[...]
-
-
-def combine_kernel(half, left_ref, right_ref, *out_refs):
-    me, count = lax.axis_index("gy") >> 2, len(out_refs)
+def combine_kernel(half, count, *refs):
+    parts, out_refs = refs[:-count], refs[-count:]
+    me = lax.axis_index("gy") >> 2
+
+    def total(rows):
+        return functools.reduce(jnp.add, [part[rows, :] for part in parts])
+
+    gram = total(slice(count * half, None))
     for distance, out_ref in enumerate(out_refs):
-        rows = pl.ds(pl.multiple_of((me ^ distance) * half, half), half)
-        out_ref[:half, :] = left_ref[rows, :] + right_ref[rows, :]
-        out_ref[half:, :] = left_ref[count * half :, :] + right_ref[count * half :, :]
+        out_ref[:half, :] = total(pl.ds(pl.multiple_of((me ^ distance) * half, half), half))
+        out_ref[half:, :] = gram
 
 
 def solve_kernel(*refs):
-    *parts, three_gram_ref, out_ref = refs
+    *parts, three_gram_ref, out_ref, band_ref = refs
     total = parts[0][...]
     for part in parts[1:]:
         total = total + part[...]
@@ -165,7 +164,8 @@
 
     for own in range(len(bands)):
         base = 8 * own
-        line = [jnp.broadcast_to(bands[own][q : q + 1], tile) for q in range(8)]
+        band_ref[8 * own : 8 * own + 8, :] = bands[own]
+        line = [jnp.broadcast_to(band_ref[8 * own + q : 8 * own + q + 1, :], tile) for q in range(8)]
         entry = [[lane(line[q], base + p) if p >= q else None for p in range(8)] for q in range(8)]
         inverse, done = [None] * 8, None
 
@@ -269,17 +269,15 @@
         [sums, *held(count)],
         [hbm, WHOLE, WHOLE, WHOLE],
     )
-    for part in arrived[:-1]:
-        total = call(add_kernel, group, (total, part), 10**6, 12)
     kept, *sent = call(
-        functools.partial(combine_kernel, half), (single,) * count, (total, arrived[-1]), 10**6, 12
+        functools.partial(combine_kernel, half, count), (single,) * count, (total, *arrived), 10**6, 12
     )
     parts = [
         lax.ppermute(value, "gy", [(i, i ^ (4 * distance)) for i in range(blocks)])
         for distance, value in enumerate(sent, 1)
     ]
     return call(
-        solve_kernel, jax.ShapeDtypeStruct((owned, rank), jnp.float32), (kept, *parts, three_gram), 10**8, 12
+        solve_kernel, jax.ShapeDtypeStruct((owned, rank), jnp.float32), (kept, *parts, three_gram), 10**8, 12, [f32((rank, 2 * rank))]
     )
 
 

time: 23.4 us -> 23.4 us (level)
    pallas_call x7 -> x5, Pallas kernels: 10.5 us -> 10.4 us  [call(): pl.pallas_call(kernel, out_shape=out_shape, in_specs=specs or [WHOLE] * l...]
  transfers between devices with their start and end apart: 7 -> 7, of which waited for: 4 -> 4; matrix products, arithmetic and copies ran while one was open for 0% -> 0% of each run, Pallas kernels for 23% -> 24%
where the time goes in v7:
time: 23.4 us; the launch traced here: 23.2 us
  Pallas kernels  10.4 us (44%)
  starting transfers between devices  9.24 us (39%)
  waiting for transfers between devices  3.5 us (15%)
    pallas_call x5, Pallas kernels, call(): pl.pallas_call(kernel, out_shape=out_shape, in_specs=specs or [WHOLE] * l...  10.4 us
    ppermute x3, starting transfers between devices, body(): lax.ppermute(value, 'gy', [(i, i - i % 4 + table[i % 4]) for i in range(b...  3.5 us
    ppermute x3, starting transfers between devices, body(): lax.ppermute(mine, 'gx', [(i, i ^ distance) for i in range(groups)])  3.08 us
    ppermute x1, starting transfers between devices, body(): lax.ppermute(value, 'gy', [(i, i ^ 4 * distance) for i in range(blocks)])  2.66 us
    ppermute x1, waiting for transfers between devices, body(): lax.ppermute(value, 'gy', [(i, i ^ 4 * distance) for i in range(blocks)])  2.22 us
    ppermute x3, waiting for transfers between devices, body(): lax.ppermute(value, 'gy', [(i, i - i % 4 + table[i % 4]) for i in range(b...  1.04 us
  transfers between devices with their start and end apart: 7, of which 4 were waited for; matrix products, arithmetic and copies ran while one was open for 0% of the time, Pallas kernels for 24%

profile of v7, /device:TPU:0, one launch (start us, length us, event | category | flops | bytes accessed | tf_op | source)
XLA Modules:
  0.0 23.2 jit_solution(11621540155170601079)
XLA Ops:
  0.0 0.0 copy-start.1
  0.0 0.0 copy-start
  0.0 2.4 %collective-permute-start.2 = (f32[16,128]{1,0:T(8,128)}, f32[16,128]{1,0:T(8,128)S(1)}, u32[]{:S(2)}, u32[]{:S(2)}) collective-permute-start(f32[16,128]{1,0:T(8,128)} %bitcast.2), channel_id=1, source_target_pairs={{0,24},{8,16},{16,8},{24,0},{1,25},{9,17},{17,9},{25,1},{2,26},{10... | collective-permute-start | bytes 24584 | tf_op jit(solution)/shard_map/ppermute | solution.py:238
  2.4 0.6 %collective-permute-start.1 = (f32[16,128]{1,0:T(8,128)}, f32[16,128]{1,0:T(8,128)S(1)}, u32[]{:S(2)}, u32[]{:S(2)}) collective-permute-start(f32[16,128]{1,0:T(8,128)} %bitcast.3), channel_id=1, source_target_pairs={{0,16},{8,24},{16,0},{24,8},{1,17},{9,25},{17,1},{25,9},{2,18},{10... | collective-permute-start | bytes 24584 | tf_op jit(solution)/shard_map/ppermute | solution.py:238
  3.0 0.0 collective-permute-start
  3.1 2.9 %shard_map.37.split_ref = bf16[12288,256]{1,0:T(8,128)(2,1)S(1)} custom-call(f32[512,32,128]{2,1,0:T(8,128)} %bitcast.6), custom_call_target="tpu_custom_call" | custom-call | flops 1000000000 | bytes 20971520 | tf_op jit(solution)/shard_map/pallas_call | solution.py:207
  6.0 0.0 collective-permute-done.2.refs_3_
  6.0 0.2 collective-permute-done.1.refs_2_
  6.3 0.0 collective-permute-done.refs_1_
  6.3 0.0 copy-done.1
  6.3 0.0 copy-done
  6.3 2.0 %shard_map.38 = (f32[96,128]{1,0:T(8,128)S(1)}, f32[96,128]{1,0:T(8,128)S(1)}, f32[96,128]{1,0:T(8,128)S(1)}, f32[32,128]{1,0:T(8,128)S(1)}, bf16[256,128]{1,0:T(8,128)(2,1)S(1)}) custom-call(bf16[12288,256]{1,0:T(8,128)(2,1)S(1)} %shard_map.37.split_ref, f32[32,64]{1,0:T(8,128)S(1)} %copy-done, f32[16,128]{1,0:T(8,128)S(1)} %bitcast.5, ...), custom_call_target="tpu_custom_call" | custom-call | flops 2000000000 | bytes 12918784 | tf_op jit(solution)/shard_map/pallas_call | solution.py:207
  8.3 2.5 %collective-permute-start.3 = (f32[96,128]{1,0:T(8,128)S(1)}, f32[96,128]{1,0:T(8,128)S(1)}, u32[]{:S(2)}, u32[]{:S(2)}) collective-permute-start(f32[96,128]{1,0:T(8,128)S(1)} %get-tuple-element.17), channel_id=1, source_target_pairs={{0,3},{1,2},{2,1},{3,0},{4,7},{5,6},{6,5},{7,4},{8,11},{9,10},{10,... | collective-permute-start | bytes 147464 | tf_op jit(solution)/shard_map/ppermute | solution.py:260
  10.9 0.4 %collective-permute-start.4 = (f32[96,128]{1,0:T(8,128)S(1)}, f32[96,128]{1,0:T(8,128)S(1)}, u32[]{:S(2)}, u32[]{:S(2)}) collective-permute-start(f32[96,128]{1,0:T(8,128)S(1)} %get-tuple-element.18), channel_id=1, source_target_pairs={{0,2},{1,3},{2,0},{3,1},{4,6},{5,7},{6,4},{7,5},{8,10},{9,11},{10,... | collective-permute-start | bytes 147464 | tf_op jit(solution)/shard_map/ppermute | solution.py:260
  11.3 0.5 %collective-permute-start.5 = (f32[96,128]{1,0:T(8,128)S(1)}, f32[96,128]{1,0:T(8,128)S(1)}, u32[]{:S(2)}, u32[]{:S(2)}) collective-permute-start(f32[96,128]{1,0:T(8,128)S(1)} %get-tuple-element.19), channel_id=1, source_target_pairs={{0,1},{1,0},{2,3},{3,2},{4,5},{5,4},{6,7},{7,6},{8,9},{9,8},{10,11... | collective-permute-start | bytes 147464 | tf_op jit(solution)/shard_map/ppermute | solution.py:260
  11.8 2.5 %shard_map.39 = (f32[96,128]{1,0:T(8,128)S(1)}, f32[32,128]{1,0:T(8,128)S(1)}) custom-call(f32[512,32,128]{2,1,0:T(8,128)} %bitcast.7, bf16[256,128]{1,0:T(8,128)(2,1)S(1)} %get-tuple-element.14.weight_ref, f32[32,64]{1,0:T(8,128)S(1)} %copy-done, f32[32,128]{1,0:T(8,128)S(1)} %get-tuple-element.15.gram_ref), custom_call_target="tpu_custom_call" | custom-call | flops 2000000000 | bytes 8609792 | tf_op jit(solution)/shard_map/pallas_call | solution.py:207
  14.4 0.0 collective-permute-done.3.refs_1_
  14.4 0.6 %collective-permute-done.4.refs_2_ = f32[96,128]{1,0:T(8,128)S(1)} collective-permute-done((f32[96,128]{1,0:T(8,128)S(1)}, f32[96,128]{1,0:T(8,128)S(1)}, u32[]{:S(2)}, u32[]{:S(2)}) %collective-permute-start.4) | collective-permute-done | bytes 49184 | tf_op jit(solution)/shard_map/ppermute | solution.py:260
  15.0 0.4 %collective-permute-done.5.refs_3_ = f32[96,128]{1,0:T(8,128)S(1)} collective-permute-done((f32[96,128]{1,0:T(8,128)S(1)}, f32[96,128]{1,0:T(8,128)S(1)}, u32[]{:S(2)}, u32[]{:S(2)}) %collective-permute-start.5) | collective-permute-done | bytes 49184 | tf_op jit(solution)/shard_map/ppermute | solution.py:260
  15.4 2.7 %collective-permute-start.6 = (f32[64,128]{1,0:T(8,128)S(1)}, f32[64,128]{1,0:T(8,128)S(1)}, u32[]{:S(2)}, u32[]{:S(2)}) collective-permute-start(f32[64,128]{1,0:T(8,128)S(1)} %get-tuple-element.21), channel_id=1, source_target_pairs={{0,4},{1,5},{2,6},{3,7},{4,0},{5,1},{6,2},{7,3},{8,12},{9,13},{10,... | collective-permute-start | bytes 98312 | tf_op jit(solution)/shard_map/ppermute | solution.py:276
  18.1 2.2 %collective-permute-done.6.refs_1_ = f32[64,128]{1,0:T(8,128)S(1)} collective-permute-done((f32[64,128]{1,0:T(8,128)S(1)}, f32[64,128]{1,0:T(8,128)S(1)}, u32[]{:S(2)}, u32[]{:S(2)}) %collective-permute-start.6) | collective-permute-done | bytes 32800 | tf_op jit(solution)/shard_map/ppermute | solution.py:276
  20.3 2.9 %shard_map.41 = f32[64,64]{1,0:T(8,128)} custom-call(f32[64,128]{1,0:T(8,128)S(1)} %get-tuple-element.20.refs_0_, f32[64,128]{1,0:T(8,128)S(1)} %collective-permute-done.6.refs_1_, f32[32,128]{1,0:T(8,128)S(1)} %get-tuple-element.22.refs_2_), custom_call_target="tpu_custom_call" | custom-call | flops 100000000 | bytes 98304 | tf_op jit(solution)/shard_map/pallas_call | solution.py:207
  (1 shorter events, 0.0 us)
Async XLA Ops:
  0.0 6.3 %copy-start.1 = (f32[128,16]{0,1:T(8,128)S(1)}, f32[128,16]{0,1:T(8,128)}, u32[]{:S(2)}) copy-start(f32[128,16]{0,1:T(8,128)} %param.4) | copy-start | bytes 24580
  0.0 6.3 %copy-start = (f32[32,64]{1,0:T(8,128)S(1)}, f32[32,64]{1,0:T(8,128)}, u32[]{:S(2)}) copy-start(f32[32,64]{1,0:T(8,128)} %three_ref.3) | copy-start | bytes 24580
  0.0 6.0 %collective-permute-start.2 = (f32[16,128]{1,0:T(8,128)}, f32[16,128]{1,0:T(8,128)S(1)}, u32[]{:S(2)}, u32[]{:S(2)}) collective-permute-start(f32[16,128]{1,0:T(8,128)} %bitcast.2), channel_id=1, source_target_pairs={{0,24},{8,16},{16,8},{24,0},{1,25},{9,17},{17,9},{25,1},{2,26},{10... | collective-permute-start | bytes 24584 | tf_op jit(solution)/shard_map/ppermute | solution.py:238
  2.4 3.9 %collective-permute-start.1 = (f32[16,128]{1,0:T(8,128)}, f32[16,128]{1,0:T(8,128)S(1)}, u32[]{:S(2)}, u32[]{:S(2)}) collective-permute-start(f32[16,128]{1,0:T(8,128)} %bitcast.3), channel_id=1, source_target_pairs={{0,16},{8,24},{16,0},{24,8},{1,17},{9,25},{17,1},{25,9},{2,18},{10... | collective-permute-start | bytes 24584 | tf_op jit(solution)/shard_map/ppermute | solution.py:238
  3.0 3.2 %collective-permute-start = (f32[16,128]{1,0:T(8,128)}, f32[16,128]{1,0:T(8,128)S(1)}, u32[]{:S(2)}, u32[]{:S(2)}) collective-permute-start(f32[16,128]{1,0:T(8,128)} %bitcast.4), channel_id=1, source_target_pairs={{0,8},{8,0},{16,24},{24,16},{1,9},{9,1},{17,25},{25,17},{2,10},{10... | collective-permute-start | bytes 24584 | tf_op jit(solution)/shard_map/ppermute | solution.py:238
  8.3 6.0 %collective-permute-start.3 = (f32[96,128]{1,0:T(8,128)S(1)}, f32[96,128]{1,0:T(8,128)S(1)}, u32[]{:S(2)}, u32[]{:S(2)}) collective-permute-start(f32[96,128]{1,0:T(8,128)S(1)} %get-tuple-element.17), channel_id=1, source_target_pairs={{0,3},{1,2},{2,1},{3,0},{4,7},{5,6},{6,5},{7,4},{8,11},{9,10},{10,... | collective-permute-start | bytes 147464 | tf_op jit(solution)/shard_map/ppermute | solution.py:260
  10.9 4.1 %collective-permute-start.4 = (f32[96,128]{1,0:T(8,128)S(1)}, f32[96,128]{1,0:T(8,128)S(1)}, u32[]{:S(2)}, u32[]{:S(2)}) collective-permute-start(f32[96,128]{1,0:T(8,128)S(1)} %get-tuple-element.18), channel_id=1, source_target_pairs={{0,2},{1,3},{2,0},{3,1},{4,6},{5,7},{6,4},{7,5},{8,10},{9,11},{10,... | collective-permute-start | bytes 147464 | tf_op jit(solution)/shard_map/ppermute | solution.py:260
  11.3 4.1 %collective-permute-start.5 = (f32[96,128]{1,0:T(8,128)S(1)}, f32[96,128]{1,0:T(8,128)S(1)}, u32[]{:S(2)}, u32[]{:S(2)}) collective-permute-start(f32[96,128]{1,0:T(8,128)S(1)} %get-tuple-element.19), channel_id=1, source_target_pairs={{0,1},{1,0},{2,3},{3,2},{4,5},{5,4},{6,7},{7,6},{8,9},{9,8},{10,11... | collective-permute-start | bytes 147464 | tf_op jit(solution)/shard_map/ppermute | solution.py:260
  15.4 4.9 %collective-permute-start.6 = (f32[64,128]{1,0:T(8,128)S(1)}, f32[64,128]{1,0:T(8,128)S(1)}, u32[]{:S(2)}, u32[]{:S(2)}) collective-permute-start(f32[64,128]{1,0:T(8,128)S(1)} %get-tuple-element.21), channel_id=1, source_target_pairs={{0,4},{1,5},{2,6},{3,7},{4,0},{5,1},{6,2},{7,3},{8,12},{9,13},{10,... | collective-permute-start | bytes 98312 | tf_op jit(solution)/shard_map/ppermute | solution.py:276

commit v8 on v7

--- a/solution.py
+++ b/solution.py
@@ -141,7 +141,7 @@
 
 
 def solve_kernel(*refs):
-    *parts, three_gram_ref, out_ref, band_ref = refs
+    *parts, three_gram_ref, out_ref = refs
     total = parts[0][...]
     for part in parts[1:]:
         total = total + part[...]
@@ -151,7 +151,11 @@
     rows = lax.broadcasted_iota(jnp.int32, (order, lanes), 0)
     lane_ids = lax.broadcasted_iota(jnp.int32, (order, lanes), 1)
     joined = jnp.concatenate([pltpu.roll(gram, order, 1), gram], axis=0)
-    joined = jnp.where(lane_ids < order, jnp.where(rows == lane_ids, 1.0, 0.0), joined)
+    diagonal = jnp.where(lane_ids - order == rows, joined, 0.0)
+    down = lax.rsqrt(jnp.sum(diagonal, axis=1, keepdims=True))
+    over = jnp.sum(diagonal, axis=0, keepdims=True)
+    over = lax.rsqrt(jnp.where(lane_ids[:1] < order, 1.0, over))
+    joined = down * jnp.where(lane_ids < order, jnp.where(rows == lane_ids, 1.0, 0.0), joined * over)
     right = jnp.concatenate([total[:half], pltpu.roll(total[:half], order, 1)], axis=0)
     right = jnp.where(lax.broadcasted_iota(jnp.int32, right.shape, 1) < order, right, 0.0)
 
@@ -164,8 +168,7 @@
 
     for own in range(len(bands)):
         base = 8 * own
-        band_ref[8 * own : 8 * own + 8, :] = bands[own]
-        line = [jnp.broadcast_to(band_ref[8 * own + q : 8 * own + q + 1, :], tile) for q in range(8)]
+        line = [jnp.broadcast_to(bands[own][q : q + 1], tile) for q in range(8)]
         entry = [[lane(line[q], base + p) if p >= q else None for p in range(8)] for q in range(8)]
         inverse, done = [None] * 8, None
 
@@ -178,19 +181,34 @@
 
         near = bands[own + 1 : own + 2]
         column = [lane(band, base + q) for band in near for q in range(8)]
-        for q in range(8):
-            pivot = entry[q][q]
-            inverse[q] = pltpu.reciprocal(pivot, approx=True)
-            row = line[q] * lax.rsqrt(pivot)
-            done = row if done is None else jnp.where(places == q, row, done)
-            factor = [entry[q][p] * inverse[q] if p > q else None for p in range(8)]
-            for p in range(q + 1, 8):
-                entry[p][p] = entry[p][p] - (entry[q][p] * entry[q][p]) * inverse[q]
-                for s in range(p + 1, 8):
-                    entry[p][s] = entry[p][s] - factor[p] * entry[q][s]
-                line[p] = line[p] - factor[p] * line[q]
+        for q in range(0, 8, 2):
+            r = q + 1
+            a, b, c = entry[q][q], entry[q][r], entry[r][r]
+            inverse[q] = pltpu.reciprocal(a, approx=True)
+            inverse_det = pltpu.reciprocal(a * c - b * b, approx=True)
+            inverse[r] = a * inverse_det
+            both = inverse[q] * inverse_det
+            slope = b * inverse[q]
+            line[r] = line[r] - slope * line[q]
+            first = line[q] * lax.rsqrt(a)
+            second = line[r] * lax.rsqrt(c - b * slope)
+            done = first if done is None else jnp.where(places == q, first, done)
+            done = jnp.where(places == r, second, done)
+            cross = [a * entry[r][p] - b * entry[q][p] if p > r else None for p in range(8)]
+            for p in range(r + 1, 8):
+                entry[r][p] = cross[p] * inverse[q]
+                upper, under = entry[q][p] * inverse[q], cross[p] * inverse_det
+                line[p] = line[p] - upper * line[q] - under * line[r]
+                under = cross[p] * both
+                for s in range(p, 8):
+                    if s <= r + 2:
+                        fall = (entry[q][p] * entry[q][s]) * inverse[q] + (cross[p] * cross[s]) * both
+                    else:
+                        fall = upper * entry[q][s] + under * cross[s]
+                    entry[p][s] = entry[p][s] - fall
             if near:
                 bands[own + 1] = follow(bands[own + 1], column, q)
+                bands[own + 1] = follow(bands[own + 1], column, r)
         bands[own] = done
         for h in range(own + 2, len(bands)):
             column = [lane(bands[h], base + q) for q in range(8)]
@@ -277,7 +295,7 @@
         for distance, value in enumerate(sent, 1)
     ]
     return call(
-        solve_kernel, jax.ShapeDtypeStruct((owned, rank), jnp.float32), (kept, *parts, three_gram), 10**8, 12, [f32((rank, 2 * rank))]
+        solve_kernel, jax.ShapeDtypeStruct((owned, rank), jnp.float32), (kept, *parts, three_gram), 10**8, 12
     )
 
 

time: 23.4 us -> 23.4 us (level)
  no operation moved by 1% of the time
where the time goes in v8:
time: 23.4 us; the launch traced here: 23.2 us
  Pallas kernels  10.4 us (44%)
  starting transfers between devices  9.24 us (39%)
  waiting for transfers between devices  3.5 us (15%)
    pallas_call x5, Pallas kernels, call(): pl.pallas_call(kernel, out_shape=out_shape, in_specs=specs or [WHOLE] * l...  10.4 us
    ppermute x3, starting transfers between devices, body(): lax.ppermute(value, 'gy', [(i, i - i % 4 + table[i % 4]) for i in range(b...  3.5 us
    ppermute x3, starting transfers between devices, body(): lax.ppermute(mine, 'gx', [(i, i ^ distance) for i in range(groups)])  3.08 us
    ppermute x1, starting transfers between devices, body(): lax.ppermute(value, 'gy', [(i, i ^ 4 * distance) for i in range(blocks)])  2.66 us
    ppermute x1, waiting for transfers between devices, body(): lax.ppermute(value, 'gy', [(i, i ^ 4 * distance) for i in range(blocks)])  2.22 us
    ppermute x3, waiting for transfers between devices, body(): lax.ppermute(value, 'gy', [(i, i - i % 4 + table[i % 4]) for i in range(b...  1.04 us
  transfers between devices with their start and end apart: 7, of which 4 were waited for; matrix products, arithmetic and copies ran while one was open for 0% of the time, Pallas kernels for 24%

profile of v8, /device:TPU:0, one launch (start us, length us, event | category | flops | bytes accessed | tf_op | source)
XLA Modules:
  0.0 23.2 jit_solution(9671570762078323296)
XLA Ops:
  0.0 0.0 copy-start.1
  0.0 0.0 copy-start
  0.0 2.4 %collective-permute-start.2 = (f32[16,128]{1,0:T(8,128)}, f32[16,128]{1,0:T(8,128)S(1)}, u32[]{:S(2)}, u32[]{:S(2)}) collective-permute-start(f32[16,128]{1,0:T(8,128)} %bitcast.2), channel_id=1, source_target_pairs={{0,24},{8,16},{16,8},{24,0},{1,25},{9,17},{17,9},{25,1},{2,26},{10... | collective-permute-start | bytes 24584 | tf_op jit(solution)/shard_map/ppermute | solution.py:256
  2.4 0.6 %collective-permute-start.1 = (f32[16,128]{1,0:T(8,128)}, f32[16,128]{1,0:T(8,128)S(1)}, u32[]{:S(2)}, u32[]{:S(2)}) collective-permute-start(f32[16,128]{1,0:T(8,128)} %bitcast.3), channel_id=1, source_target_pairs={{0,16},{8,24},{16,0},{24,8},{1,17},{9,25},{17,1},{25,9},{2,18},{10... | collective-permute-start | bytes 24584 | tf_op jit(solution)/shard_map/ppermute | solution.py:256
  3.0 0.0 collective-permute-start
  3.1 2.9 %shard_map.37.split_ref = bf16[12288,256]{1,0:T(8,128)(2,1)S(1)} custom-call(f32[512,32,128]{2,1,0:T(8,128)} %bitcast.6), custom_call_target="tpu_custom_call" | custom-call | flops 1000000000 | bytes 20971520 | tf_op jit(solution)/shard_map/pallas_call | solution.py:225
  6.0 0.0 collective-permute-done.2.refs_3_
  6.0 0.2 collective-permute-done.1.refs_2_
  6.3 0.0 collective-permute-done.refs_1_
  6.3 0.0 copy-done.1
  6.3 0.0 copy-done
  6.3 2.0 %shard_map.38 = (f32[96,128]{1,0:T(8,128)S(1)}, f32[96,128]{1,0:T(8,128)S(1)}, f32[96,128]{1,0:T(8,128)S(1)}, f32[32,128]{1,0:T(8,128)S(1)}, bf16[256,128]{1,0:T(8,128)(2,1)S(1)}) custom-call(bf16[12288,256]{1,0:T(8,128)(2,1)S(1)} %shard_map.37.split_ref, f32[32,64]{1,0:T(8,128)S(1)} %copy-done, f32[16,128]{1,0:T(8,128)S(1)} %bitcast.5, ...), custom_call_target="tpu_custom_call" | custom-call | flops 2000000000 | bytes 12918784 | tf_op jit(solution)/shard_map/pallas_call | solution.py:225
  8.3 2.5 %collective-permute-start.3 = (f32[96,128]{1,0:T(8,128)S(1)}, f32[96,128]{1,0:T(8,128)S(1)}, u32[]{:S(2)}, u32[]{:S(2)}) collective-permute-start(f32[96,128]{1,0:T(8,128)S(1)} %get-tuple-element.17), channel_id=1, source_target_pairs={{0,3},{1,2},{2,1},{3,0},{4,7},{5,6},{6,5},{7,4},{8,11},{9,10},{10,... | collective-permute-start | bytes 147464 | tf_op jit(solution)/shard_map/ppermute | solution.py:278
  10.9 0.4 %collective-permute-start.4 = (f32[96,128]{1,0:T(8,128)S(1)}, f32[96,128]{1,0:T(8,128)S(1)}, u32[]{:S(2)}, u32[]{:S(2)}) collective-permute-start(f32[96,128]{1,0:T(8,128)S(1)} %get-tuple-element.18), channel_id=1, source_target_pairs={{0,2},{1,3},{2,0},{3,1},{4,6},{5,7},{6,4},{7,5},{8,10},{9,11},{10,... | collective-permute-start | bytes 147464 | tf_op jit(solution)/shard_map/ppermute | solution.py:278
  11.3 0.5 %collective-permute-start.5 = (f32[96,128]{1,0:T(8,128)S(1)}, f32[96,128]{1,0:T(8,128)S(1)}, u32[]{:S(2)}, u32[]{:S(2)}) collective-permute-start(f32[96,128]{1,0:T(8,128)S(1)} %get-tuple-element.19), channel_id=1, source_target_pairs={{0,1},{1,0},{2,3},{3,2},{4,5},{5,4},{6,7},{7,6},{8,9},{9,8},{10,11... | collective-permute-start | bytes 147464 | tf_op jit(solution)/shard_map/ppermute | solution.py:278
  11.8 2.5 %shard_map.39 = (f32[96,128]{1,0:T(8,128)S(1)}, f32[32,128]{1,0:T(8,128)S(1)}) custom-call(f32[512,32,128]{2,1,0:T(8,128)} %bitcast.7, bf16[256,128]{1,0:T(8,128)(2,1)S(1)} %get-tuple-element.14.weight_ref, f32[32,64]{1,0:T(8,128)S(1)} %copy-done, f32[32,128]{1,0:T(8,128)S(1)} %get-tuple-element.15.gram_ref), custom_call_target="tpu_custom_call" | custom-call | flops 2000000000 | bytes 8609792 | tf_op jit(solution)/shard_map/pallas_call | solution.py:225
  14.4 0.0 collective-permute-done.3.refs_1_
  14.4 0.6 %collective-permute-done.4.refs_2_ = f32[96,128]{1,0:T(8,128)S(1)} collective-permute-done((f32[96,128]{1,0:T(8,128)S(1)}, f32[96,128]{1,0:T(8,128)S(1)}, u32[]{:S(2)}, u32[]{:S(2)}) %collective-permute-start.4) | collective-permute-done | bytes 49184 | tf_op jit(solution)/shard_map/ppermute | solution.py:278
  15.0 0.4 %collective-permute-done.5.refs_3_ = f32[96,128]{1,0:T(8,128)S(1)} collective-permute-done((f32[96,128]{1,0:T(8,128)S(1)}, f32[96,128]{1,0:T(8,128)S(1)}, u32[]{:S(2)}, u32[]{:S(2)}) %collective-permute-start.5) | collective-permute-done | bytes 49184 | tf_op jit(solution)/shard_map/ppermute | solution.py:278
  15.4 2.7 %collective-permute-start.6 = (f32[64,128]{1,0:T(8,128)S(1)}, f32[64,128]{1,0:T(8,128)S(1)}, u32[]{:S(2)}, u32[]{:S(2)}) collective-permute-start(f32[64,128]{1,0:T(8,128)S(1)} %get-tuple-element.21), channel_id=1, source_target_pairs={{0,4},{1,5},{2,6},{3,7},{4,0},{5,1},{6,2},{7,3},{8,12},{9,13},{10,... | collective-permute-start | bytes 98312 | tf_op jit(solution)/shard_map/ppermute | solution.py:294
  18.1 2.2 %collective-permute-done.6.refs_1_ = f32[64,128]{1,0:T(8,128)S(1)} collective-permute-done((f32[64,128]{1,0:T(8,128)S(1)}, f32[64,128]{1,0:T(8,128)S(1)}, u32[]{:S(2)}, u32[]{:S(2)}) %collective-permute-start.6) | collective-permute-done | bytes 32800 | tf_op jit(solution)/shard_map/ppermute | solution.py:294
  20.3 2.9 %shard_map.41 = f32[64,64]{1,0:T(8,128)} custom-call(f32[64,128]{1,0:T(8,128)S(1)} %get-tuple-element.20.refs_0_, f32[64,128]{1,0:T(8,128)S(1)} %collective-permute-done.6.refs_1_, f32[32,128]{1,0:T(8,128)S(1)} %get-tuple-element.22.refs_2_), custom_call_target="tpu_custom_call" | custom-call | flops 100000000 | bytes 98304 | tf_op jit(solution)/shard_map/pallas_call | solution.py:225
  (1 shorter events, 0.0 us)
Async XLA Ops:
  0.0 6.3 %copy-start.1 = (f32[128,16]{0,1:T(8,128)S(1)}, f32[128,16]{0,1:T(8,128)}, u32[]{:S(2)}) copy-start(f32[128,16]{0,1:T(8,128)} %param.4) | copy-start | bytes 24580
  0.0 6.3 %copy-start = (f32[32,64]{1,0:T(8,128)S(1)}, f32[32,64]{1,0:T(8,128)}, u32[]{:S(2)}) copy-start(f32[32,64]{1,0:T(8,128)} %three_ref.3) | copy-start | bytes 24580
  0.0 6.0 %collective-permute-start.2 = (f32[16,128]{1,0:T(8,128)}, f32[16,128]{1,0:T(8,128)S(1)}, u32[]{:S(2)}, u32[]{:S(2)}) collective-permute-start(f32[16,128]{1,0:T(8,128)} %bitcast.2), channel_id=1, source_target_pairs={{0,24},{8,16},{16,8},{24,0},{1,25},{9,17},{17,9},{25,1},{2,26},{10... | collective-permute-start | bytes 24584 | tf_op jit(solution)/shard_map/ppermute | solution.py:256
  2.4 3.9 %collective-permute-start.1 = (f32[16,128]{1,0:T(8,128)}, f32[16,128]{1,0:T(8,128)S(1)}, u32[]{:S(2)}, u32[]{:S(2)}) collective-permute-start(f32[16,128]{1,0:T(8,128)} %bitcast.3), channel_id=1, source_target_pairs={{0,16},{8,24},{16,0},{24,8},{1,17},{9,25},{17,1},{25,9},{2,18},{10... | collective-permute-start | bytes 24584 | tf_op jit(solution)/shard_map/ppermute | solution.py:256
  3.0 3.2 %collective-permute-start = (f32[16,128]{1,0:T(8,128)}, f32[16,128]{1,0:T(8,128)S(1)}, u32[]{:S(2)}, u32[]{:S(2)}) collective-permute-start(f32[16,128]{1,0:T(8,128)} %bitcast.4), channel_id=1, source_target_pairs={{0,8},{8,0},{16,24},{24,16},{1,9},{9,1},{17,25},{25,17},{2,10},{10... | collective-permute-start | bytes 24584 | tf_op jit(solution)/shard_map/ppermute | solution.py:256
  8.3 6.0 %collective-permute-start.3 = (f32[96,128]{1,0:T(8,128)S(1)}, f32[96,128]{1,0:T(8,128)S(1)}, u32[]{:S(2)}, u32[]{:S(2)}) collective-permute-start(f32[96,128]{1,0:T(8,128)S(1)} %get-tuple-element.17), channel_id=1, source_target_pairs={{0,3},{1,2},{2,1},{3,0},{4,7},{5,6},{6,5},{7,4},{8,11},{9,10},{10,... | collective-permute-start | bytes 147464 | tf_op jit(solution)/shard_map/ppermute | solution.py:278
  10.9 4.1 %collective-permute-start.4 = (f32[96,128]{1,0:T(8,128)S(1)}, f32[96,128]{1,0:T(8,128)S(1)}, u32[]{:S(2)}, u32[]{:S(2)}) collective-permute-start(f32[96,128]{1,0:T(8,128)S(1)} %get-tuple-element.18), channel_id=1, source_target_pairs={{0,2},{1,3},{2,0},{3,1},{4,6},{5,7},{6,4},{7,5},{8,10},{9,11},{10,... | collective-permute-start | bytes 147464 | tf_op jit(solution)/shard_map/ppermute | solution.py:278
  11.3 4.1 %collective-permute-start.5 = (f32[96,128]{1,0:T(8,128)S(1)}, f32[96,128]{1,0:T(8,128)S(1)}, u32[]{:S(2)}, u32[]{:S(2)}) collective-permute-start(f32[96,128]{1,0:T(8,128)S(1)} %get-tuple-element.19), channel_id=1, source_target_pairs={{0,1},{1,0},{2,3},{3,2},{4,5},{5,4},{6,7},{7,6},{8,9},{9,8},{10,11... | collective-permute-start | bytes 147464 | tf_op jit(solution)/shard_map/ppermute | solution.py:278
  15.4 4.9 %collective-permute-start.6 = (f32[64,128]{1,0:T(8,128)S(1)}, f32[64,128]{1,0:T(8,128)S(1)}, u32[]{:S(2)}, u32[]{:S(2)}) collective-permute-start(f32[64,128]{1,0:T(8,128)S(1)} %get-tuple-element.21), channel_id=1, source_target_pairs={{0,4},{1,5},{2,6},{3,7},{4,0},{5,1},{6,2},{7,3},{8,12},{9,13},{10,... | collective-permute-start | bytes 98312 | tf_op jit(solution)/shard_map/ppermute | solution.py:294

commit v9 on v7

--- a/solution.py
+++ b/solution.py
@@ -141,7 +141,7 @@
 
 
 def solve_kernel(*refs):
-    *parts, three_gram_ref, out_ref, band_ref = refs
+    *parts, three_gram_ref, out_ref, spread_ref = refs
     total = parts[0][...]
     for part in parts[1:]:
         total = total + part[...]
@@ -164,9 +164,16 @@
 
     for own in range(len(bands)):
         base = 8 * own
-        band_ref[8 * own : 8 * own + 8, :] = bands[own]
-        line = [jnp.broadcast_to(band_ref[8 * own + q : 8 * own + q + 1, :], tile) for q in range(8)]
-        entry = [[lane(line[q], base + p) if p >= q else None for p in range(8)] for q in range(8)]
+        spot = 72 * own
+        for p in range(8):
+            spread_ref[spot + 8 * p : spot + 8 * p + 8, :] = lane(bands[own], base + p)
+        spread_ref[spot + 64 : spot + 72, :] = bands[own]
+
+        def spread(place):
+            return jnp.broadcast_to(spread_ref[place : place + 1, :], tile)
+
+        line = [spread(spot + 64 + q) for q in range(8)]
+        entry = [[spread(spot + 8 * p + q) if p >= q else None for p in range(8)] for q in range(8)]
         inverse, done = [None] * 8, None
 
         def follow(band, column, q):
@@ -277,7 +284,7 @@
         for distance, value in enumerate(sent, 1)
     ]
     return call(
-        solve_kernel, jax.ShapeDtypeStruct((owned, rank), jnp.float32), (kept, *parts, three_gram), 10**8, 12, [f32((rank, 2 * rank))]
+        solve_kernel, jax.ShapeDtypeStruct((owned, rank), jnp.float32), (kept, *parts, three_gram), 10**8, 12, [f32((9 * rank, 2 * rank))]
     )
 
 

time: 23.4 us -> 22.8 us (0.974)
  Pallas kernels: 10.4 us -> 9.9 us
    pallas_call x5, Pallas kernels: 10.4 us -> 9.9 us  [call(): pl.pallas_call(kernel, out_shape=out_shape, in_specs=specs or [WHOLE] * l...]
where the time goes in v9:
time: 22.8 us; the launch traced here: 22.7 us
  Pallas kernels  9.9 us (43%)
  starting transfers between devices  9.24 us (41%)
  waiting for transfers between devices  3.5 us (15%)
    pallas_call x5, Pallas kernels, call(): pl.pallas_call(kernel, out_shape=out_shape, in_specs=specs or [WHOLE] * l...  9.9 us
    ppermute x3, starting transfers between devices, body(): lax.ppermute(value, 'gy', [(i, i - i % 4 + table[i % 4]) for i in range(b...  3.5 us
    ppermute x3, starting transfers between devices, body(): lax.ppermute(mine, 'gx', [(i, i ^ distance) for i in range(groups)])  3.08 us
    ppermute x1, starting transfers between devices, body(): lax.ppermute(value, 'gy', [(i, i ^ 4 * distance) for i in range(blocks)])  2.66 us
    ppermute x1, waiting for transfers between devices, body(): lax.ppermute(value, 'gy', [(i, i ^ 4 * distance) for i in range(blocks)])  2.22 us
    ppermute x3, waiting for transfers between devices, body(): lax.ppermute(value, 'gy', [(i, i - i % 4 + table[i % 4]) for i in range(b...  1.04 us
  transfers between devices with their start and end apart: 7, of which 4 were waited for; matrix products, arithmetic and copies ran while one was open for 0% of the time, Pallas kernels for 24%

profile of v9, /device:TPU:0, one launch (start us, length us, event | category | flops | bytes accessed | tf_op | source)
XLA Modules:
  0.0 22.7 jit_solution(15706585754885377666)
XLA Ops:
  0.0 0.0 copy-start.1
  0.0 0.0 copy-start
  0.0 2.4 %collective-permute-start.2 = (f32[16,128]{1,0:T(8,128)}, f32[16,128]{1,0:T(8,128)S(1)}, u32[]{:S(2)}, u32[]{:S(2)}) collective-permute-start(f32[16,128]{1,0:T(8,128)} %bitcast.2), channel_id=1, source_target_pairs={{0,24},{8,16},{16,8},{24,0},{1,25},{9,17},{17,9},{25,1},{2,26},{10... | collective-permute-start | bytes 24584 | tf_op jit(solution)/shard_map/ppermute | solution.py:245
  2.4 0.6 %collective-permute-start.1 = (f32[16,128]{1,0:T(8,128)}, f32[16,128]{1,0:T(8,128)S(1)}, u32[]{:S(2)}, u32[]{:S(2)}) collective-permute-start(f32[16,128]{1,0:T(8,128)} %bitcast.3), channel_id=1, source_target_pairs={{0,16},{8,24},{16,0},{24,8},{1,17},{9,25},{17,1},{25,9},{2,18},{10... | collective-permute-start | bytes 24584 | tf_op jit(solution)/shard_map/ppermute | solution.py:245
  3.0 0.0 collective-permute-start
  3.1 2.9 %shard_map.37.split_ref = bf16[12288,256]{1,0:T(8,128)(2,1)S(1)} custom-call(f32[512,32,128]{2,1,0:T(8,128)} %bitcast.6), custom_call_target="tpu_custom_call" | custom-call | flops 1000000000 | bytes 20971520 | tf_op jit(solution)/shard_map/pallas_call | solution.py:214
  6.0 0.0 collective-permute-done.2.refs_3_
  6.0 0.2 collective-permute-done.1.refs_2_
  6.3 0.0 collective-permute-done.refs_1_
  6.3 0.0 copy-done.1
  6.3 0.0 copy-done
  6.3 2.0 %shard_map.38 = (f32[96,128]{1,0:T(8,128)S(1)}, f32[96,128]{1,0:T(8,128)S(1)}, f32[96,128]{1,0:T(8,128)S(1)}, f32[32,128]{1,0:T(8,128)S(1)}, bf16[256,128]{1,0:T(8,128)(2,1)S(1)}) custom-call(bf16[12288,256]{1,0:T(8,128)(2,1)S(1)} %shard_map.37.split_ref, f32[32,64]{1,0:T(8,128)S(1)} %copy-done, f32[16,128]{1,0:T(8,128)S(1)} %bitcast.5, ...), custom_call_target="tpu_custom_call" | custom-call | flops 2000000000 | bytes 12918784 | tf_op jit(solution)/shard_map/pallas_call | solution.py:214
  8.3 2.5 %collective-permute-start.3 = (f32[96,128]{1,0:T(8,128)S(1)}, f32[96,128]{1,0:T(8,128)S(1)}, u32[]{:S(2)}, u32[]{:S(2)}) collective-permute-start(f32[96,128]{1,0:T(8,128)S(1)} %get-tuple-element.17), channel_id=1, source_target_pairs={{0,3},{1,2},{2,1},{3,0},{4,7},{5,6},{6,5},{7,4},{8,11},{9,10},{10,... | collective-permute-start | bytes 147464 | tf_op jit(solution)/shard_map/ppermute | solution.py:267
  10.9 0.4 %collective-permute-start.4 = (f32[96,128]{1,0:T(8,128)S(1)}, f32[96,128]{1,0:T(8,128)S(1)}, u32[]{:S(2)}, u32[]{:S(2)}) collective-permute-start(f32[96,128]{1,0:T(8,128)S(1)} %get-tuple-element.18), channel_id=1, source_target_pairs={{0,2},{1,3},{2,0},{3,1},{4,6},{5,7},{6,4},{7,5},{8,10},{9,11},{10,... | collective-permute-start | bytes 147464 | tf_op jit(solution)/shard_map/ppermute | solution.py:267
  11.3 0.5 %collective-permute-start.5 = (f32[96,128]{1,0:T(8,128)S(1)}, f32[96,128]{1,0:T(8,128)S(1)}, u32[]{:S(2)}, u32[]{:S(2)}) collective-permute-start(f32[96,128]{1,0:T(8,128)S(1)} %get-tuple-element.19), channel_id=1, source_target_pairs={{0,1},{1,0},{2,3},{3,2},{4,5},{5,4},{6,7},{7,6},{8,9},{9,8},{10,11... | collective-permute-start | bytes 147464 | tf_op jit(solution)/shard_map/ppermute | solution.py:267
  11.8 2.5 %shard_map.39 = (f32[96,128]{1,0:T(8,128)S(1)}, f32[32,128]{1,0:T(8,128)S(1)}) custom-call(f32[512,32,128]{2,1,0:T(8,128)} %bitcast.7, bf16[256,128]{1,0:T(8,128)(2,1)S(1)} %get-tuple-element.14.weight_ref, f32[32,64]{1,0:T(8,128)S(1)} %copy-done, f32[32,128]{1,0:T(8,128)S(1)} %get-tuple-element.15.gram_ref), custom_call_target="tpu_custom_call" | custom-call | flops 2000000000 | bytes 8609792 | tf_op jit(solution)/shard_map/pallas_call | solution.py:214
  14.4 0.0 collective-permute-done.3.refs_1_
  14.4 0.6 %collective-permute-done.4.refs_2_ = f32[96,128]{1,0:T(8,128)S(1)} collective-permute-done((f32[96,128]{1,0:T(8,128)S(1)}, f32[96,128]{1,0:T(8,128)S(1)}, u32[]{:S(2)}, u32[]{:S(2)}) %collective-permute-start.4) | collective-permute-done | bytes 49184 | tf_op jit(solution)/shard_map/ppermute | solution.py:267
  15.0 0.4 %collective-permute-done.5.refs_3_ = f32[96,128]{1,0:T(8,128)S(1)} collective-permute-done((f32[96,128]{1,0:T(8,128)S(1)}, f32[96,128]{1,0:T(8,128)S(1)}, u32[]{:S(2)}, u32[]{:S(2)}) %collective-permute-start.5) | collective-permute-done | bytes 49184 | tf_op jit(solution)/shard_map/ppermute | solution.py:267
  15.4 2.7 %collective-permute-start.6 = (f32[64,128]{1,0:T(8,128)S(1)}, f32[64,128]{1,0:T(8,128)S(1)}, u32[]{:S(2)}, u32[]{:S(2)}) collective-permute-start(f32[64,128]{1,0:T(8,128)S(1)} %get-tuple-element.21), channel_id=1, source_target_pairs={{0,4},{1,5},{2,6},{3,7},{4,0},{5,1},{6,2},{7,3},{8,12},{9,13},{10,... | collective-permute-start | bytes 98312 | tf_op jit(solution)/shard_map/ppermute | solution.py:283
  18.1 2.2 %collective-permute-done.6.refs_1_ = f32[64,128]{1,0:T(8,128)S(1)} collective-permute-done((f32[64,128]{1,0:T(8,128)S(1)}, f32[64,128]{1,0:T(8,128)S(1)}, u32[]{:S(2)}, u32[]{:S(2)}) %collective-permute-start.6) | collective-permute-done | bytes 32800 | tf_op jit(solution)/shard_map/ppermute | solution.py:283
  20.3 2.4 %shard_map.41 = f32[64,64]{1,0:T(8,128)} custom-call(f32[64,128]{1,0:T(8,128)S(1)} %get-tuple-element.20.refs_0_, f32[64,128]{1,0:T(8,128)S(1)} %collective-permute-done.6.refs_1_, f32[32,128]{1,0:T(8,128)S(1)} %get-tuple-element.22.refs_2_), custom_call_target="tpu_custom_call" | custom-call | flops 100000000 | bytes 98304 | tf_op jit(solution)/shard_map/pallas_call | solution.py:214
  (1 shorter events, 0.0 us)
Async XLA Ops:
  0.0 6.3 %copy-start.1 = (f32[128,16]{0,1:T(8,128)S(1)}, f32[128,16]{0,1:T(8,128)}, u32[]{:S(2)}) copy-start(f32[128,16]{0,1:T(8,128)} %param.4) | copy-start | bytes 24580
  0.0 6.3 %copy-start = (f32[32,64]{1,0:T(8,128)S(1)}, f32[32,64]{1,0:T(8,128)}, u32[]{:S(2)}) copy-start(f32[32,64]{1,0:T(8,128)} %three_ref.3) | copy-start | bytes 24580
  0.0 6.0 %collective-permute-start.2 = (f32[16,128]{1,0:T(8,128)}, f32[16,128]{1,0:T(8,128)S(1)}, u32[]{:S(2)}, u32[]{:S(2)}) collective-permute-start(f32[16,128]{1,0:T(8,128)} %bitcast.2), channel_id=1, source_target_pairs={{0,24},{8,16},{16,8},{24,0},{1,25},{9,17},{17,9},{25,1},{2,26},{10... | collective-permute-start | bytes 24584 | tf_op jit(solution)/shard_map/ppermute | solution.py:245
  2.4 3.9 %collective-permute-start.1 = (f32[16,128]{1,0:T(8,128)}, f32[16,128]{1,0:T(8,128)S(1)}, u32[]{:S(2)}, u32[]{:S(2)}) collective-permute-start(f32[16,128]{1,0:T(8,128)} %bitcast.3), channel_id=1, source_target_pairs={{0,16},{8,24},{16,0},{24,8},{1,17},{9,25},{17,1},{25,9},{2,18},{10... | collective-permute-start | bytes 24584 | tf_op jit(solution)/shard_map/ppermute | solution.py:245
  3.0 3.2 %collective-permute-start = (f32[16,128]{1,0:T(8,128)}, f32[16,128]{1,0:T(8,128)S(1)}, u32[]{:S(2)}, u32[]{:S(2)}) collective-permute-start(f32[16,128]{1,0:T(8,128)} %bitcast.4), channel_id=1, source_target_pairs={{0,8},{8,0},{16,24},{24,16},{1,9},{9,1},{17,25},{25,17},{2,10},{10... | collective-permute-start | bytes 24584 | tf_op jit(solution)/shard_map/ppermute | solution.py:245
  8.3 6.0 %collective-permute-start.3 = (f32[96,128]{1,0:T(8,128)S(1)}, f32[96,128]{1,0:T(8,128)S(1)}, u32[]{:S(2)}, u32[]{:S(2)}) collective-permute-start(f32[96,128]{1,0:T(8,128)S(1)} %get-tuple-element.17), channel_id=1, source_target_pairs={{0,3},{1,2},{2,1},{3,0},{4,7},{5,6},{6,5},{7,4},{8,11},{9,10},{10,... | collective-permute-start | bytes 147464 | tf_op jit(solution)/shard_map/ppermute | solution.py:267
  10.9 4.1 %collective-permute-start.4 = (f32[96,128]{1,0:T(8,128)S(1)}, f32[96,128]{1,0:T(8,128)S(1)}, u32[]{:S(2)}, u32[]{:S(2)}) collective-permute-start(f32[96,128]{1,0:T(8,128)S(1)} %get-tuple-element.18), channel_id=1, source_target_pairs={{0,2},{1,3},{2,0},{3,1},{4,6},{5,7},{6,4},{7,5},{8,10},{9,11},{10,... | collective-permute-start | bytes 147464 | tf_op jit(solution)/shard_map/ppermute | solution.py:267
  11.3 4.1 %collective-permute-start.5 = (f32[96,128]{1,0:T(8,128)S(1)}, f32[96,128]{1,0:T(8,128)S(1)}, u32[]{:S(2)}, u32[]{:S(2)}) collective-permute-start(f32[96,128]{1,0:T(8,128)S(1)} %get-tuple-element.19), channel_id=1, source_target_pairs={{0,1},{1,0},{2,3},{3,2},{4,5},{5,4},{6,7},{7,6},{8,9},{9,8},{10,11... | collective-permute-start | bytes 147464 | tf_op jit(solution)/shard_map/ppermute | solution.py:267
  15.4 4.9 %collective-permute-start.6 = (f32[64,128]{1,0:T(8,128)S(1)}, f32[64,128]{1,0:T(8,128)S(1)}, u32[]{:S(2)}, u32[]{:S(2)}) collective-permute-start(f32[64,128]{1,0:T(8,128)S(1)} %get-tuple-element.21), channel_id=1, source_target_pairs={{0,4},{1,5},{2,6},{3,7},{4,0},{5,1},{6,2},{7,3},{8,12},{9,13},{10,... | collective-permute-start | bytes 98312 | tf_op jit(solution)/shard_map/ppermute | solution.py:283

commit v10 on v9

--- a/solution.py
+++ b/solution.py
@@ -70,17 +70,37 @@
             out_ref[start * depth : (start + chunk) * depth, :] = halves(held_ref[start : start + chunk])
 
 
+def folded(rows):
+    places = lax.broadcasted_iota(jnp.int32, rows[0].shape, 0)
+
+    def four(x, y):
+        low = places < 4
+        return jnp.where(low, x, y) + pltpu.roll(jnp.where(low, y, x), 4, 0)
+
+    def two(x, y):
+        return jnp.where(places % 4 >= 2, x + pltpu.roll(x, 2, 0), y + pltpu.roll(y, 6, 0))
+
+    def one(x, y):
+        return jnp.where(places % 2 == 1, x + pltpu.roll(x, 1, 0), y + pltpu.roll(y, 7, 0))
+
+    odd = two(four(rows[3], rows[7]), four(rows[1], rows[5]))
+    even = two(four(rows[2], rows[6]), four(rows[0], rows[4]))
+    return one(odd, even)
+
+
 def multiply(count, chunk, take, weight_ref, three_ref, outs, sum_ref):
     depth, rank = three_ref.shape
     rows = sum_ref.shape[0]
     half = rows // 2
     three = three_ref[...]
-    three = jnp.concatenate([three, three], axis=1)[None]
+    three = jnp.concatenate([three, three], axis=1).reshape(1, depth // 8, 8, 2 * rank)
     lower_half = lax.broadcasted_iota(jnp.int32, (half, 2 * rank), 1) < rank
     for block in range(count * len(outs)):
         for start in range(0, rows, chunk):
             product = jnp.dot(take(block * rows + start), weight_ref[...], preferred_element_type=jnp.float32)
-            sum_ref[start : start + chunk, :] = jnp.sum(product.reshape(chunk, depth, 2 * rank) * three, axis=1)
+            partial = jnp.sum(product.reshape(chunk, depth // 8, 8, 2 * rank) * three, axis=1)
+            for first in range(0, chunk, 8):
+                sum_ref[start + first : start + first + 8, :] = folded([partial[first + row] for row in range(8)])
         total = sum_ref[...]
         total = total + pltpu.roll(total, rank, 1)
         place = block % count * half

time: 22.8 us -> 22.8 us (level)
  no operation moved by 1% of the time
where the time goes in v10:
time: 22.8 us; the launch traced here: 22.7 us
  Pallas kernels  9.88 us (43%)
  starting transfers between devices  9.24 us (41%)
  waiting for transfers between devices  3.52 us (15%)
    pallas_call x5, Pallas kernels, call(): pl.pallas_call(kernel, out_shape=out_shape, in_specs=specs or [WHOLE] * l...  9.88 us
    ppermute x3, starting transfers between devices, body(): lax.ppermute(value, 'gy', [(i, i - i % 4 + table[i % 4]) for i in range(b...  3.5 us
    ppermute x3, starting transfers between devices, body(): lax.ppermute(mine, 'gx', [(i, i ^ distance) for i in range(groups)])  3.08 us
    ppermute x1, starting transfers between devices, body(): lax.ppermute(value, 'gy', [(i, i ^ 4 * distance) for i in range(blocks)])  2.66 us
    ppermute x1, waiting for transfers between devices, body(): lax.ppermute(value, 'gy', [(i, i ^ 4 * distance) for i in range(blocks)])  2.22 us
    ppermute x3, waiting for transfers between devices, body(): lax.ppermute(value, 'gy', [(i, i - i % 4 + table[i % 4]) for i in range(b...  1.06 us
  transfers between devices with their start and end apart: 7, of which 4 were waited for; matrix products, arithmetic and copies ran while one was open for 0% of the time, Pallas kernels for 24%

profile of v10, /device:TPU:0, one launch (start us, length us, event | category | flops | bytes accessed | tf_op | source)
XLA Modules:
  0.0 22.7 jit_solution(15576957975897509696)
XLA Ops:
  0.0 0.0 copy-start.1
  0.0 0.0 copy-start
  0.0 2.4 %collective-permute-start.2 = (f32[16,128]{1,0:T(8,128)}, f32[16,128]{1,0:T(8,128)S(1)}, u32[]{:S(2)}, u32[]{:S(2)}) collective-permute-start(f32[16,128]{1,0:T(8,128)} %bitcast.2), channel_id=1, source_target_pairs={{0,24},{8,16},{16,8},{24,0},{1,25},{9,17},{17,9},{25,1},{2,26},{10... | collective-permute-start | bytes 24584 | tf_op jit(solution)/shard_map/ppermute | solution.py:265
  2.4 0.6 %collective-permute-start.1 = (f32[16,128]{1,0:T(8,128)}, f32[16,128]{1,0:T(8,128)S(1)}, u32[]{:S(2)}, u32[]{:S(2)}) collective-permute-start(f32[16,128]{1,0:T(8,128)} %bitcast.3), channel_id=1, source_target_pairs={{0,16},{8,24},{16,0},{24,8},{1,17},{9,25},{17,1},{25,9},{2,18},{10... | collective-permute-start | bytes 24584 | tf_op jit(solution)/shard_map/ppermute | solution.py:265
  3.0 0.0 collective-permute-start
  3.1 2.9 %shard_map.37.split_ref = bf16[12288,256]{1,0:T(8,128)(2,1)S(1)} custom-call(f32[512,32,128]{2,1,0:T(8,128)} %bitcast.6), custom_call_target="tpu_custom_call" | custom-call | flops 1000000000 | bytes 20971520 | tf_op jit(solution)/shard_map/pallas_call | solution.py:234
  6.0 0.0 collective-permute-done.2.refs_3_
  6.0 0.2 collective-permute-done.1.refs_2_
  6.3 0.0 collective-permute-done.refs_1_
  6.3 0.0 copy-done.1
  6.3 0.0 copy-done
  6.3 2.0 %shard_map.38 = (f32[96,128]{1,0:T(8,128)S(1)}, f32[96,128]{1,0:T(8,128)S(1)}, f32[96,128]{1,0:T(8,128)S(1)}, f32[32,128]{1,0:T(8,128)S(1)}, bf16[256,128]{1,0:T(8,128)(2,1)S(1)}) custom-call(bf16[12288,256]{1,0:T(8,128)(2,1)S(1)} %shard_map.37.split_ref, f32[32,64]{1,0:T(8,128)S(1)} %copy-done, f32[16,128]{1,0:T(8,128)S(1)} %bitcast.5, ...), custom_call_target="tpu_custom_call" | custom-call | flops 2000000000 | bytes 12918784 | tf_op jit(solution)/shard_map/pallas_call | solution.py:234
  8.3 2.5 %collective-permute-start.3 = (f32[96,128]{1,0:T(8,128)S(1)}, f32[96,128]{1,0:T(8,128)S(1)}, u32[]{:S(2)}, u32[]{:S(2)}) collective-permute-start(f32[96,128]{1,0:T(8,128)S(1)} %get-tuple-element.17), channel_id=1, source_target_pairs={{0,3},{1,2},{2,1},{3,0},{4,7},{5,6},{6,5},{7,4},{8,11},{9,10},{10,... | collective-permute-start | bytes 147464 | tf_op jit(solution)/shard_map/ppermute | solution.py:287
  10.9 0.4 %collective-permute-start.4 = (f32[96,128]{1,0:T(8,128)S(1)}, f32[96,128]{1,0:T(8,128)S(1)}, u32[]{:S(2)}, u32[]{:S(2)}) collective-permute-start(f32[96,128]{1,0:T(8,128)S(1)} %get-tuple-element.18), channel_id=1, source_target_pairs={{0,2},{1,3},{2,0},{3,1},{4,6},{5,7},{6,4},{7,5},{8,10},{9,11},{10,... | collective-permute-start | bytes 147464 | tf_op jit(solution)/shard_map/ppermute | solution.py:287
  11.3 0.5 %collective-permute-start.5 = (f32[96,128]{1,0:T(8,128)S(1)}, f32[96,128]{1,0:T(8,128)S(1)}, u32[]{:S(2)}, u32[]{:S(2)}) collective-permute-start(f32[96,128]{1,0:T(8,128)S(1)} %get-tuple-element.19), channel_id=1, source_target_pairs={{0,1},{1,0},{2,3},{3,2},{4,5},{5,4},{6,7},{7,6},{8,9},{9,8},{10,11... | collective-permute-start | bytes 147464 | tf_op jit(solution)/shard_map/ppermute | solution.py:287
  11.8 2.5 %shard_map.39 = (f32[96,128]{1,0:T(8,128)S(1)}, f32[32,128]{1,0:T(8,128)S(1)}) custom-call(f32[512,32,128]{2,1,0:T(8,128)} %bitcast.7, bf16[256,128]{1,0:T(8,128)(2,1)S(1)} %get-tuple-element.14.weight_ref, f32[32,64]{1,0:T(8,128)S(1)} %copy-done, f32[32,128]{1,0:T(8,128)S(1)} %get-tuple-element.15.gram_ref), custom_call_target="tpu_custom_call" | custom-call | flops 2000000000 | bytes 8609792 | tf_op jit(solution)/shard_map/pallas_call | solution.py:234
  14.3 0.0 collective-permute-done.3.refs_1_
  14.4 0.6 %collective-permute-done.4.refs_2_ = f32[96,128]{1,0:T(8,128)S(1)} collective-permute-done((f32[96,128]{1,0:T(8,128)S(1)}, f32[96,128]{1,0:T(8,128)S(1)}, u32[]{:S(2)}, u32[]{:S(2)}) %collective-permute-start.4) | collective-permute-done | bytes 49184 | tf_op jit(solution)/shard_map/ppermute | solution.py:287
  15.0 0.4 %collective-permute-done.5.refs_3_ = f32[96,128]{1,0:T(8,128)S(1)} collective-permute-done((f32[96,128]{1,0:T(8,128)S(1)}, f32[96,128]{1,0:T(8,128)S(1)}, u32[]{:S(2)}, u32[]{:S(2)}) %collective-permute-start.5) | collective-permute-done | bytes 49184 | tf_op jit(solution)/shard_map/ppermute | solution.py:287
  15.4 2.7 %collective-permute-start.6 = (f32[64,128]{1,0:T(8,128)S(1)}, f32[64,128]{1,0:T(8,128)S(1)}, u32[]{:S(2)}, u32[]{:S(2)}) collective-permute-start(f32[64,128]{1,0:T(8,128)S(1)} %get-tuple-element.21), channel_id=1, source_target_pairs={{0,4},{1,5},{2,6},{3,7},{4,0},{5,1},{6,2},{7,3},{8,12},{9,13},{10,... | collective-permute-start | bytes 98312 | tf_op jit(solution)/shard_map/ppermute | solution.py:303
  18.1 2.2 %collective-permute-done.6.refs_1_ = f32[64,128]{1,0:T(8,128)S(1)} collective-permute-done((f32[64,128]{1,0:T(8,128)S(1)}, f32[64,128]{1,0:T(8,128)S(1)}, u32[]{:S(2)}, u32[]{:S(2)}) %collective-permute-start.6) | collective-permute-done | bytes 32800 | tf_op jit(solution)/shard_map/ppermute | solution.py:303
  20.3 2.4 %shard_map.41 = f32[64,64]{1,0:T(8,128)} custom-call(f32[64,128]{1,0:T(8,128)S(1)} %get-tuple-element.20.refs_0_, f32[64,128]{1,0:T(8,128)S(1)} %collective-permute-done.6.refs_1_, f32[32,128]{1,0:T(8,128)S(1)} %get-tuple-element.22.refs_2_), custom_call_target="tpu_custom_call" | custom-call | flops 100000000 | bytes 98304 | tf_op jit(solution)/shard_map/pallas_call | solution.py:234
  (1 shorter events, 0.0 us)
Async XLA Ops:
  0.0 6.3 %copy-start.1 = (f32[128,16]{0,1:T(8,128)S(1)}, f32[128,16]{0,1:T(8,128)}, u32[]{:S(2)}) copy-start(f32[128,16]{0,1:T(8,128)} %param.4) | copy-start | bytes 24580
  0.0 6.3 %copy-start = (f32[32,64]{1,0:T(8,128)S(1)}, f32[32,64]{1,0:T(8,128)}, u32[]{:S(2)}) copy-start(f32[32,64]{1,0:T(8,128)} %three_ref.3) | copy-start | bytes 24580
  0.0 6.0 %collective-permute-start.2 = (f32[16,128]{1,0:T(8,128)}, f32[16,128]{1,0:T(8,128)S(1)}, u32[]{:S(2)}, u32[]{:S(2)}) collective-permute-start(f32[16,128]{1,0:T(8,128)} %bitcast.2), channel_id=1, source_target_pairs={{0,24},{8,16},{16,8},{24,0},{1,25},{9,17},{17,9},{25,1},{2,26},{10... | collective-permute-start | bytes 24584 | tf_op jit(solution)/shard_map/ppermute | solution.py:265
  2.4 3.9 %collective-permute-start.1 = (f32[16,128]{1,0:T(8,128)}, f32[16,128]{1,0:T(8,128)S(1)}, u32[]{:S(2)}, u32[]{:S(2)}) collective-permute-start(f32[16,128]{1,0:T(8,128)} %bitcast.3), channel_id=1, source_target_pairs={{0,16},{8,24},{16,0},{24,8},{1,17},{9,25},{17,1},{25,9},{2,18},{10... | collective-permute-start | bytes 24584 | tf_op jit(solution)/shard_map/ppermute | solution.py:265
  3.0 3.2 %collective-permute-start = (f32[16,128]{1,0:T(8,128)}, f32[16,128]{1,0:T(8,128)S(1)}, u32[]{:S(2)}, u32[]{:S(2)}) collective-permute-start(f32[16,128]{1,0:T(8,128)} %bitcast.4), channel_id=1, source_target_pairs={{0,8},{8,0},{16,24},{24,16},{1,9},{9,1},{17,25},{25,17},{2,10},{10... | collective-permute-start | bytes 24584 | tf_op jit(solution)/shard_map/ppermute | solution.py:265
  8.3 6.0 %collective-permute-start.3 = (f32[96,128]{1,0:T(8,128)S(1)}, f32[96,128]{1,0:T(8,128)S(1)}, u32[]{:S(2)}, u32[]{:S(2)}) collective-permute-start(f32[96,128]{1,0:T(8,128)S(1)} %get-tuple-element.17), channel_id=1, source_target_pairs={{0,3},{1,2},{2,1},{3,0},{4,7},{5,6},{6,5},{7,4},{8,11},{9,10},{10,... | collective-permute-start | bytes 147464 | tf_op jit(solution)/shard_map/ppermute | solution.py:287
  10.9 4.1 %collective-permute-start.4 = (f32[96,128]{1,0:T(8,128)S(1)}, f32[96,128]{1,0:T(8,128)S(1)}, u32[]{:S(2)}, u32[]{:S(2)}) collective-permute-start(f32[96,128]{1,0:T(8,128)S(1)} %get-tuple-element.18), channel_id=1, source_target_pairs={{0,2},{1,3},{2,0},{3,1},{4,6},{5,7},{6,4},{7,5},{8,10},{9,11},{10,... | collective-permute-start | bytes 147464 | tf_op jit(solution)/shard_map/ppermute | solution.py:287
  11.3 4.1 %collective-permute-start.5 = (f32[96,128]{1,0:T(8,128)S(1)}, f32[96,128]{1,0:T(8,128)S(1)}, u32[]{:S(2)}, u32[]{:S(2)}) collective-permute-start(f32[96,128]{1,0:T(8,128)S(1)} %get-tuple-element.19), channel_id=1, source_target_pairs={{0,1},{1,0},{2,3},{3,2},{4,5},{5,4},{6,7},{7,6},{8,9},{9,8},{10,11... | collective-permute-start | bytes 147464 | tf_op jit(solution)/shard_map/ppermute | solution.py:287
  15.4 4.9 %collective-permute-start.6 = (f32[64,128]{1,0:T(8,128)S(1)}, f32[64,128]{1,0:T(8,128)S(1)}, u32[]{:S(2)}, u32[]{:S(2)}) collective-permute-start(f32[64,128]{1,0:T(8,128)S(1)} %get-tuple-element.21), channel_id=1, source_target_pairs={{0,4},{1,5},{2,6},{3,7},{4,0},{5,1},{6,2},{7,3},{8,12},{9,13},{10,... | collective-permute-start | bytes 98312 | tf_op jit(solution)/shard_map/ppermute | solution.py:303

commit v11 on v8

--- a/solution.py
+++ b/solution.py
@@ -141,7 +141,7 @@
 
 
 def solve_kernel(*refs):
-    *parts, three_gram_ref, out_ref = refs
+    *parts, three_gram_ref, out_ref, spread_ref = refs
     total = parts[0][...]
     for part in parts[1:]:
         total = total + part[...]
@@ -168,8 +168,16 @@
 
     for own in range(len(bands)):
         base = 8 * own
-        line = [jnp.broadcast_to(bands[own][q : q + 1], tile) for q in range(8)]
-        entry = [[lane(line[q], base + p) if p >= q else None for p in range(8)] for q in range(8)]
+        spot = 72 * own
+        for p in range(8):
+            spread_ref[spot + 8 * p : spot + 8 * p + 8, :] = lane(bands[own], base + p)
+        spread_ref[spot + 64 : spot + 72, :] = bands[own]
+
+        def spread(place):
+            return jnp.broadcast_to(spread_ref[place : place + 1, :], tile)
+
+        line = [spread(spot + 64 + q) for q in range(8)]
+        entry = [[spread(spot + 8 * p + q) if p >= q else None for p in range(8)] for q in range(8)]
         inverse, done = [None] * 8, None
 
         def follow(band, column, q):
@@ -295,7 +303,7 @@
         for distance, value in enumerate(sent, 1)
     ]
     return call(
-        solve_kernel, jax.ShapeDtypeStruct((owned, rank), jnp.float32), (kept, *parts, three_gram), 10**8, 12
+        solve_kernel, jax.ShapeDtypeStruct((owned, rank), jnp.float32), (kept, *parts, three_gram), 10**8, 12, [f32((9 * rank, 2 * rank))]
     )
 
 

time: 23.4 us -> 22.9 us (0.979)
  Pallas kernels: 10.4 us -> 9.98 us
    pallas_call x5, Pallas kernels: 10.4 us -> 9.98 us  [call(): pl.pallas_call(kernel, out_shape=out_shape, in_specs=specs or [WHOLE] * l...]
where the time goes in v11:
time: 22.9 us; the launch traced here: 22.8 us
  Pallas kernels  9.98 us (44%)
  starting transfers between devices  9.24 us (40%)
  waiting for transfers between devices  3.5 us (15%)
    pallas_call x5, Pallas kernels, call(): pl.pallas_call(kernel, out_shape=out_shape, in_specs=specs or [WHOLE] * l...  9.98 us
    ppermute x3, starting transfers between devices, body(): lax.ppermute(value, 'gy', [(i, i - i % 4 + table[i % 4]) for i in range(b...  3.5 us
    ppermute x3, starting transfers between devices, body(): lax.ppermute(mine, 'gx', [(i, i ^ distance) for i in range(groups)])  3.08 us
    ppermute x1, starting transfers between devices, body(): lax.ppermute(value, 'gy', [(i, i ^ 4 * distance) for i in range(blocks)])  2.66 us
    ppermute x1, waiting for transfers between devices, body(): lax.ppermute(value, 'gy', [(i, i ^ 4 * distance) for i in range(blocks)])  2.22 us
    ppermute x3, waiting for transfers between devices, body(): lax.ppermute(value, 'gy', [(i, i - i % 4 + table[i % 4]) for i in range(b...  1.04 us
  transfers between devices with their start and end apart: 7, of which 4 were waited for; matrix products, arithmetic and copies ran while one was open for 0% of the time, Pallas kernels for 24%

profile of v11, /device:TPU:0, one launch (start us, length us, event | category | flops | bytes accessed | tf_op | source)
XLA Modules:
  0.0 22.8 jit_solution(12187247014076016260)
XLA Ops:
  0.0 0.0 copy-start.1
  0.0 0.0 copy-start
  0.0 2.4 %collective-permute-start.2 = (f32[16,128]{1,0:T(8,128)}, f32[16,128]{1,0:T(8,128)S(1)}, u32[]{:S(2)}, u32[]{:S(2)}) collective-permute-start(f32[16,128]{1,0:T(8,128)} %bitcast.2), channel_id=1, source_target_pairs={{0,24},{8,16},{16,8},{24,0},{1,25},{9,17},{17,9},{25,1},{2,26},{10... | collective-permute-start | bytes 24584 | tf_op jit(solution)/shard_map/ppermute | solution.py:264
  2.4 0.6 %collective-permute-start.1 = (f32[16,128]{1,0:T(8,128)}, f32[16,128]{1,0:T(8,128)S(1)}, u32[]{:S(2)}, u32[]{:S(2)}) collective-permute-start(f32[16,128]{1,0:T(8,128)} %bitcast.3), channel_id=1, source_target_pairs={{0,16},{8,24},{16,0},{24,8},{1,17},{9,25},{17,1},{25,9},{2,18},{10... | collective-permute-start | bytes 24584 | tf_op jit(solution)/shard_map/ppermute | solution.py:264
  3.0 0.0 collective-permute-start
  3.1 2.9 %shard_map.37.split_ref = bf16[12288,256]{1,0:T(8,128)(2,1)S(1)} custom-call(f32[512,32,128]{2,1,0:T(8,128)} %bitcast.6), custom_call_target="tpu_custom_call" | custom-call | flops 1000000000 | bytes 20971520 | tf_op jit(solution)/shard_map/pallas_call | solution.py:233
  6.0 0.0 collective-permute-done.2.refs_3_
  6.0 0.2 collective-permute-done.1.refs_2_
  6.3 0.0 collective-permute-done.refs_1_
  6.3 0.0 copy-done.1
  6.3 0.0 copy-done
  6.3 2.0 %shard_map.38 = (f32[96,128]{1,0:T(8,128)S(1)}, f32[96,128]{1,0:T(8,128)S(1)}, f32[96,128]{1,0:T(8,128)S(1)}, f32[32,128]{1,0:T(8,128)S(1)}, bf16[256,128]{1,0:T(8,128)(2,1)S(1)}) custom-call(bf16[12288,256]{1,0:T(8,128)(2,1)S(1)} %shard_map.37.split_ref, f32[32,64]{1,0:T(8,128)S(1)} %copy-done, f32[16,128]{1,0:T(8,128)S(1)} %bitcast.5, ...), custom_call_target="tpu_custom_call" | custom-call | flops 2000000000 | bytes 12918784 | tf_op jit(solution)/shard_map/pallas_call | solution.py:233
  8.3 2.5 %collective-permute-start.3 = (f32[96,128]{1,0:T(8,128)S(1)}, f32[96,128]{1,0:T(8,128)S(1)}, u32[]{:S(2)}, u32[]{:S(2)}) collective-permute-start(f32[96,128]{1,0:T(8,128)S(1)} %get-tuple-element.17), channel_id=1, source_target_pairs={{0,3},{1,2},{2,1},{3,0},{4,7},{5,6},{6,5},{7,4},{8,11},{9,10},{10,... | collective-permute-start | bytes 147464 | tf_op jit(solution)/shard_map/ppermute | solution.py:286
  10.9 0.4 %collective-permute-start.4 = (f32[96,128]{1,0:T(8,128)S(1)}, f32[96,128]{1,0:T(8,128)S(1)}, u32[]{:S(2)}, u32[]{:S(2)}) collective-permute-start(f32[96,128]{1,0:T(8,128)S(1)} %get-tuple-element.18), channel_id=1, source_target_pairs={{0,2},{1,3},{2,0},{3,1},{4,6},{5,7},{6,4},{7,5},{8,10},{9,11},{10,... | collective-permute-start | bytes 147464 | tf_op jit(solution)/shard_map/ppermute | solution.py:286
  11.3 0.5 %collective-permute-start.5 = (f32[96,128]{1,0:T(8,128)S(1)}, f32[96,128]{1,0:T(8,128)S(1)}, u32[]{:S(2)}, u32[]{:S(2)}) collective-permute-start(f32[96,128]{1,0:T(8,128)S(1)} %get-tuple-element.19), channel_id=1, source_target_pairs={{0,1},{1,0},{2,3},{3,2},{4,5},{5,4},{6,7},{7,6},{8,9},{9,8},{10,11... | collective-permute-start | bytes 147464 | tf_op jit(solution)/shard_map/ppermute | solution.py:286
  11.8 2.5 %shard_map.39 = (f32[96,128]{1,0:T(8,128)S(1)}, f32[32,128]{1,0:T(8,128)S(1)}) custom-call(f32[512,32,128]{2,1,0:T(8,128)} %bitcast.7, bf16[256,128]{1,0:T(8,128)(2,1)S(1)} %get-tuple-element.14.weight_ref, f32[32,64]{1,0:T(8,128)S(1)} %copy-done, f32[32,128]{1,0:T(8,128)S(1)} %get-tuple-element.15.gram_ref), custom_call_target="tpu_custom_call" | custom-call | flops 2000000000 | bytes 8609792 | tf_op jit(solution)/shard_map/pallas_call | solution.py:233
  14.4 0.0 collective-permute-done.3.refs_1_
  14.4 0.6 %collective-permute-done.4.refs_2_ = f32[96,128]{1,0:T(8,128)S(1)} collective-permute-done((f32[96,128]{1,0:T(8,128)S(1)}, f32[96,128]{1,0:T(8,128)S(1)}, u32[]{:S(2)}, u32[]{:S(2)}) %collective-permute-start.4) | collective-permute-done | bytes 49184 | tf_op jit(solution)/shard_map/ppermute | solution.py:286
  15.0 0.4 %collective-permute-done.5.refs_3_ = f32[96,128]{1,0:T(8,128)S(1)} collective-permute-done((f32[96,128]{1,0:T(8,128)S(1)}, f32[96,128]{1,0:T(8,128)S(1)}, u32[]{:S(2)}, u32[]{:S(2)}) %collective-permute-start.5) | collective-permute-done | bytes 49184 | tf_op jit(solution)/shard_map/ppermute | solution.py:286
  15.4 2.7 %collective-permute-start.6 = (f32[64,128]{1,0:T(8,128)S(1)}, f32[64,128]{1,0:T(8,128)S(1)}, u32[]{:S(2)}, u32[]{:S(2)}) collective-permute-start(f32[64,128]{1,0:T(8,128)S(1)} %get-tuple-element.21), channel_id=1, source_target_pairs={{0,4},{1,5},{2,6},{3,7},{4,0},{5,1},{6,2},{7,3},{8,12},{9,13},{10,... | collective-permute-start | bytes 98312 | tf_op jit(solution)/shard_map/ppermute | solution.py:302
  18.1 2.2 %collective-permute-done.6.refs_1_ = f32[64,128]{1,0:T(8,128)S(1)} collective-permute-done((f32[64,128]{1,0:T(8,128)S(1)}, f32[64,128]{1,0:T(8,128)S(1)}, u32[]{:S(2)}, u32[]{:S(2)}) %collective-permute-start.6) | collective-permute-done | bytes 32800 | tf_op jit(solution)/shard_map/ppermute | solution.py:302
  20.3 2.5 %shard_map.41 = f32[64,64]{1,0:T(8,128)} custom-call(f32[64,128]{1,0:T(8,128)S(1)} %get-tuple-element.20.refs_0_, f32[64,128]{1,0:T(8,128)S(1)} %collective-permute-done.6.refs_1_, f32[32,128]{1,0:T(8,128)S(1)} %get-tuple-element.22.refs_2_), custom_call_target="tpu_custom_call" | custom-call | flops 100000000 | bytes 98304 | tf_op jit(solution)/shard_map/pallas_call | solution.py:233
  (1 shorter events, 0.0 us)
Async XLA Ops:
  0.0 6.3 %copy-start.1 = (f32[128,16]{0,1:T(8,128)S(1)}, f32[128,16]{0,1:T(8,128)}, u32[]{:S(2)}) copy-start(f32[128,16]{0,1:T(8,128)} %param.4) | copy-start | bytes 24580
  0.0 6.3 %copy-start = (f32[32,64]{1,0:T(8,128)S(1)}, f32[32,64]{1,0:T(8,128)}, u32[]{:S(2)}) copy-start(f32[32,64]{1,0:T(8,128)} %three_ref.3) | copy-start | bytes 24580
  0.0 6.0 %collective-permute-start.2 = (f32[16,128]{1,0:T(8,128)}, f32[16,128]{1,0:T(8,128)S(1)}, u32[]{:S(2)}, u32[]{:S(2)}) collective-permute-start(f32[16,128]{1,0:T(8,128)} %bitcast.2), channel_id=1, source_target_pairs={{0,24},{8,16},{16,8},{24,0},{1,25},{9,17},{17,9},{25,1},{2,26},{10... | collective-permute-start | bytes 24584 | tf_op jit(solution)/shard_map/ppermute | solution.py:264
  2.4 3.9 %collective-permute-start.1 = (f32[16,128]{1,0:T(8,128)}, f32[16,128]{1,0:T(8,128)S(1)}, u32[]{:S(2)}, u32[]{:S(2)}) collective-permute-start(f32[16,128]{1,0:T(8,128)} %bitcast.3), channel_id=1, source_target_pairs={{0,16},{8,24},{16,0},{24,8},{1,17},{9,25},{17,1},{25,9},{2,18},{10... | collective-permute-start | bytes 24584 | tf_op jit(solution)/shard_map/ppermute | solution.py:264
  3.0 3.2 %collective-permute-start = (f32[16,128]{1,0:T(8,128)}, f32[16,128]{1,0:T(8,128)S(1)}, u32[]{:S(2)}, u32[]{:S(2)}) collective-permute-start(f32[16,128]{1,0:T(8,128)} %bitcast.4), channel_id=1, source_target_pairs={{0,8},{8,0},{16,24},{24,16},{1,9},{9,1},{17,25},{25,17},{2,10},{10... | collective-permute-start | bytes 24584 | tf_op jit(solution)/shard_map/ppermute | solution.py:264
  8.3 6.0 %collective-permute-start.3 = (f32[96,128]{1,0:T(8,128)S(1)}, f32[96,128]{1,0:T(8,128)S(1)}, u32[]{:S(2)}, u32[]{:S(2)}) collective-permute-start(f32[96,128]{1,0:T(8,128)S(1)} %get-tuple-element.17), channel_id=1, source_target_pairs={{0,3},{1,2},{2,1},{3,0},{4,7},{5,6},{6,5},{7,4},{8,11},{9,10},{10,... | collective-permute-start | bytes 147464 | tf_op jit(solution)/shard_map/ppermute | solution.py:286
  10.9 4.1 %collective-permute-start.4 = (f32[96,128]{1,0:T(8,128)S(1)}, f32[96,128]{1,0:T(8,128)S(1)}, u32[]{:S(2)}, u32[]{:S(2)}) collective-permute-start(f32[96,128]{1,0:T(8,128)S(1)} %get-tuple-element.18), channel_id=1, source_target_pairs={{0,2},{1,3},{2,0},{3,1},{4,6},{5,7},{6,4},{7,5},{8,10},{9,11},{10,... | collective-permute-start | bytes 147464 | tf_op jit(solution)/shard_map/ppermute | solution.py:286
  11.3 4.1 %collective-permute-start.5 = (f32[96,128]{1,0:T(8,128)S(1)}, f32[96,128]{1,0:T(8,128)S(1)}, u32[]{:S(2)}, u32[]{:S(2)}) collective-permute-start(f32[96,128]{1,0:T(8,128)S(1)} %get-tuple-element.19), channel_id=1, source_target_pairs={{0,1},{1,0},{2,3},{3,2},{4,5},{5,4},{6,7},{7,6},{8,9},{9,8},{10,11... | collective-permute-start | bytes 147464 | tf_op jit(solution)/shard_map/ppermute | solution.py:286
  15.4 4.9 %collective-permute-start.6 = (f32[64,128]{1,0:T(8,128)S(1)}, f32[64,128]{1,0:T(8,128)S(1)}, u32[]{:S(2)}, u32[]{:S(2)}) collective-permute-start(f32[64,128]{1,0:T(8,128)S(1)} %get-tuple-element.21), channel_id=1, source_target_pairs={{0,4},{1,5},{2,6},{3,7},{4,0},{5,1},{6,2},{7,3},{8,12},{9,13},{10,... | collective-permute-start | bytes 98312 | tf_op jit(solution)/shard_map/ppermute | solution.py:302

commit v12 on v9

--- a/solution.py
+++ b/solution.py
@@ -183,8 +183,8 @@
                 column[p] = column[p] - scale * entry[q][p]
             return band
 
-        near = bands[own + 1 : own + 2]
-        column = [lane(band, base + q) for band in near for q in range(8)]
+        later = range(own + 1, len(bands))
+        columns = {h: [lane(bands[h], base + q) for q in range(8)] for h in later}
         for q in range(8):
             pivot = entry[q][q]
             inverse[q] = pltpu.reciprocal(pivot, approx=True)
@@ -196,13 +196,9 @@
                 for s in range(p + 1, 8):
                     entry[p][s] = entry[p][s] - factor[p] * entry[q][s]
                 line[p] = line[p] - factor[p] * line[q]
-            if near:
-                bands[own + 1] = follow(bands[own + 1], column, q)
+            for h in later:
+                bands[h] = follow(bands[h], columns[h], q)
         bands[own] = done
-        for h in range(own + 2, len(bands)):
-            column = [lane(bands[h], base + q) for q in range(8)]
-            for q in range(8):
-                bands[h] = follow(bands[h], column, q)
     lower = jnp.concatenate(bands, axis=0)
     solved = dot_of(right, lower, (1, 1))
     out_ref[...] = dot_of(solved, lower, (1, 0))[:, :order]

time: 22.8 us -> 22.8 us (level)
  no operation moved by 1% of the time
where the time goes in v12:
time: 22.8 us; the launch traced here: 22.7 us
  Pallas kernels  9.9 us (43%)
  starting transfers between devices  9.24 us (41%)
  waiting for transfers between devices  3.5 us (15%)
    pallas_call x5, Pallas kernels, call(): pl.pallas_call(kernel, out_shape=out_shape, in_specs=specs or [WHOLE] * l...  9.9 us
    ppermute x3, starting transfers between devices, body(): lax.ppermute(value, 'gy', [(i, i - i % 4 + table[i % 4]) for i in range(b...  3.5 us
    ppermute x3, starting transfers between devices, body(): lax.ppermute(mine, 'gx', [(i, i ^ distance) for i in range(groups)])  3.08 us
    ppermute x1, starting transfers between devices, body(): lax.ppermute(value, 'gy', [(i, i ^ 4 * distance) for i in range(blocks)])  2.66 us
    ppermute x1, waiting for transfers between devices, body(): lax.ppermute(value, 'gy', [(i, i ^ 4 * distance) for i in range(blocks)])  2.22 us
    ppermute x3, waiting for transfers between devices, body(): lax.ppermute(value, 'gy', [(i, i - i % 4 + table[i % 4]) for i in range(b...  1.04 us
  transfers between devices with their start and end apart: 7, of which 4 were waited for; matrix products, arithmetic and copies ran while one was open for 0% of the time, Pallas kernels for 24%

profile of v12, /device:TPU:0, one launch (start us, length us, event | category | flops | bytes accessed | tf_op | source)
XLA Modules:
  0.0 22.7 jit_solution(15706585754885377666)
XLA Ops:
  0.0 0.0 copy-start.1
  0.0 0.0 copy-start
  0.0 2.4 %collective-permute-start.2 = (f32[16,128]{1,0:T(8,128)}, f32[16,128]{1,0:T(8,128)S(1)}, u32[]{:S(2)}, u32[]{:S(2)}) collective-permute-start(f32[16,128]{1,0:T(8,128)} %bitcast.2), channel_id=1, source_target_pairs={{0,24},{8,16},{16,8},{24,0},{1,25},{9,17},{17,9},{25,1},{2,26},{10... | collective-permute-start | bytes 24584 | tf_op jit(solution)/shard_map/ppermute | solution.py:241
  2.4 0.6 %collective-permute-start.1 = (f32[16,128]{1,0:T(8,128)}, f32[16,128]{1,0:T(8,128)S(1)}, u32[]{:S(2)}, u32[]{:S(2)}) collective-permute-start(f32[16,128]{1,0:T(8,128)} %bitcast.3), channel_id=1, source_target_pairs={{0,16},{8,24},{16,0},{24,8},{1,17},{9,25},{17,1},{25,9},{2,18},{10... | collective-permute-start | bytes 24584 | tf_op jit(solution)/shard_map/ppermute | solution.py:241
  3.0 0.0 collective-permute-start
  3.1 2.9 %shard_map.37.split_ref = bf16[12288,256]{1,0:T(8,128)(2,1)S(1)} custom-call(f32[512,32,128]{2,1,0:T(8,128)} %bitcast.6), custom_call_target="tpu_custom_call" | custom-call | flops 1000000000 | bytes 20971520 | tf_op jit(solution)/shard_map/pallas_call | solution.py:210
  6.0 0.0 collective-permute-done.2.refs_3_
  6.0 0.2 collective-permute-done.1.refs_2_
  6.3 0.0 collective-permute-done.refs_1_
  6.3 0.0 copy-done.1
  6.3 0.0 copy-done
  6.3 2.0 %shard_map.38 = (f32[96,128]{1,0:T(8,128)S(1)}, f32[96,128]{1,0:T(8,128)S(1)}, f32[96,128]{1,0:T(8,128)S(1)}, f32[32,128]{1,0:T(8,128)S(1)}, bf16[256,128]{1,0:T(8,128)(2,1)S(1)}) custom-call(bf16[12288,256]{1,0:T(8,128)(2,1)S(1)} %shard_map.37.split_ref, f32[32,64]{1,0:T(8,128)S(1)} %copy-done, f32[16,128]{1,0:T(8,128)S(1)} %bitcast.5, ...), custom_call_target="tpu_custom_call" | custom-call | flops 2000000000 | bytes 12918784 | tf_op jit(solution)/shard_map/pallas_call | solution.py:210
  8.3 2.5 %collective-permute-start.3 = (f32[96,128]{1,0:T(8,128)S(1)}, f32[96,128]{1,0:T(8,128)S(1)}, u32[]{:S(2)}, u32[]{:S(2)}) collective-permute-start(f32[96,128]{1,0:T(8,128)S(1)} %get-tuple-element.17), channel_id=1, source_target_pairs={{0,3},{1,2},{2,1},{3,0},{4,7},{5,6},{6,5},{7,4},{8,11},{9,10},{10,... | collective-permute-start | bytes 147464 | tf_op jit(solution)/shard_map/ppermute | solution.py:263
  10.9 0.4 %collective-permute-start.4 = (f32[96,128]{1,0:T(8,128)S(1)}, f32[96,128]{1,0:T(8,128)S(1)}, u32[]{:S(2)}, u32[]{:S(2)}) collective-permute-start(f32[96,128]{1,0:T(8,128)S(1)} %get-tuple-element.18), channel_id=1, source_target_pairs={{0,2},{1,3},{2,0},{3,1},{4,6},{5,7},{6,4},{7,5},{8,10},{9,11},{10,... | collective-permute-start | bytes 147464 | tf_op jit(solution)/shard_map/ppermute | solution.py:263
  11.3 0.5 %collective-permute-start.5 = (f32[96,128]{1,0:T(8,128)S(1)}, f32[96,128]{1,0:T(8,128)S(1)}, u32[]{:S(2)}, u32[]{:S(2)}) collective-permute-start(f32[96,128]{1,0:T(8,128)S(1)} %get-tuple-element.19), channel_id=1, source_target_pairs={{0,1},{1,0},{2,3},{3,2},{4,5},{5,4},{6,7},{7,6},{8,9},{9,8},{10,11... | collective-permute-start | bytes 147464 | tf_op jit(solution)/shard_map/ppermute | solution.py:263
  11.8 2.5 %shard_map.39 = (f32[96,128]{1,0:T(8,128)S(1)}, f32[32,128]{1,0:T(8,128)S(1)}) custom-call(f32[512,32,128]{2,1,0:T(8,128)} %bitcast.7, bf16[256,128]{1,0:T(8,128)(2,1)S(1)} %get-tuple-element.14.weight_ref, f32[32,64]{1,0:T(8,128)S(1)} %copy-done, f32[32,128]{1,0:T(8,128)S(1)} %get-tuple-element.15.gram_ref), custom_call_target="tpu_custom_call" | custom-call | flops 2000000000 | bytes 8609792 | tf_op jit(solution)/shard_map/pallas_call | solution.py:210
  14.4 0.0 collective-permute-done.3.refs_1_
  14.4 0.6 %collective-permute-done.4.refs_2_ = f32[96,128]{1,0:T(8,128)S(1)} collective-permute-done((f32[96,128]{1,0:T(8,128)S(1)}, f32[96,128]{1,0:T(8,128)S(1)}, u32[]{:S(2)}, u32[]{:S(2)}) %collective-permute-start.4) | collective-permute-done | bytes 49184 | tf_op jit(solution)/shard_map/ppermute | solution.py:263
  15.0 0.4 %collective-permute-done.5.refs_3_ = f32[96,128]{1,0:T(8,128)S(1)} collective-permute-done((f32[96,128]{1,0:T(8,128)S(1)}, f32[96,128]{1,0:T(8,128)S(1)}, u32[]{:S(2)}, u32[]{:S(2)}) %collective-permute-start.5) | collective-permute-done | bytes 49184 | tf_op jit(solution)/shard_map/ppermute | solution.py:263
  15.4 2.7 %collective-permute-start.6 = (f32[64,128]{1,0:T(8,128)S(1)}, f32[64,128]{1,0:T(8,128)S(1)}, u32[]{:S(2)}, u32[]{:S(2)}) collective-permute-start(f32[64,128]{1,0:T(8,128)S(1)} %get-tuple-element.21), channel_id=1, source_target_pairs={{0,4},{1,5},{2,6},{3,7},{4,0},{5,1},{6,2},{7,3},{8,12},{9,13},{10,... | collective-permute-start | bytes 98312 | tf_op jit(solution)/shard_map/ppermute | solution.py:279
  18.1 2.2 %collective-permute-done.6.refs_1_ = f32[64,128]{1,0:T(8,128)S(1)} collective-permute-done((f32[64,128]{1,0:T(8,128)S(1)}, f32[64,128]{1,0:T(8,128)S(1)}, u32[]{:S(2)}, u32[]{:S(2)}) %collective-permute-start.6) | collective-permute-done | bytes 32800 | tf_op jit(solution)/shard_map/ppermute | solution.py:279
  20.3 2.4 %shard_map.41 = f32[64,64]{1,0:T(8,128)} custom-call(f32[64,128]{1,0:T(8,128)S(1)} %get-tuple-element.20.refs_0_, f32[64,128]{1,0:T(8,128)S(1)} %collective-permute-done.6.refs_1_, f32[32,128]{1,0:T(8,128)S(1)} %get-tuple-element.22.refs_2_), custom_call_target="tpu_custom_call" | custom-call | flops 100000000 | bytes 98304 | tf_op jit(solution)/shard_map/pallas_call | solution.py:210
  (1 shorter events, 0.0 us)
Async XLA Ops:
  0.0 6.3 %copy-start.1 = (f32[128,16]{0,1:T(8,128)S(1)}, f32[128,16]{0,1:T(8,128)}, u32[]{:S(2)}) copy-start(f32[128,16]{0,1:T(8,128)} %param.4) | copy-start | bytes 24580
  0.0 6.3 %copy-start = (f32[32,64]{1,0:T(8,128)S(1)}, f32[32,64]{1,0:T(8,128)}, u32[]{:S(2)}) copy-start(f32[32,64]{1,0:T(8,128)} %three_ref.3) | copy-start | bytes 24580
  0.0 6.0 %collective-permute-start.2 = (f32[16,128]{1,0:T(8,128)}, f32[16,128]{1,0:T(8,128)S(1)}, u32[]{:S(2)}, u32[]{:S(2)}) collective-permute-start(f32[16,128]{1,0:T(8,128)} %bitcast.2), channel_id=1, source_target_pairs={{0,24},{8,16},{16,8},{24,0},{1,25},{9,17},{17,9},{25,1},{2,26},{10... | collective-permute-start | bytes 24584 | tf_op jit(solution)/shard_map/ppermute | solution.py:241
  2.4 3.9 %collective-permute-start.1 = (f32[16,128]{1,0:T(8,128)}, f32[16,128]{1,0:T(8,128)S(1)}, u32[]{:S(2)}, u32[]{:S(2)}) collective-permute-start(f32[16,128]{1,0:T(8,128)} %bitcast.3), channel_id=1, source_target_pairs={{0,16},{8,24},{16,0},{24,8},{1,17},{9,25},{17,1},{25,9},{2,18},{10... | collective-permute-start | bytes 24584 | tf_op jit(solution)/shard_map/ppermute | solution.py:241
  3.0 3.2 %collective-permute-start = (f32[16,128]{1,0:T(8,128)}, f32[16,128]{1,0:T(8,128)S(1)}, u32[]{:S(2)}, u32[]{:S(2)}) collective-permute-start(f32[16,128]{1,0:T(8,128)} %bitcast.4), channel_id=1, source_target_pairs={{0,8},{8,0},{16,24},{24,16},{1,9},{9,1},{17,25},{25,17},{2,10},{10... | collective-permute-start | bytes 24584 | tf_op jit(solution)/shard_map/ppermute | solution.py:241
  8.3 6.0 %collective-permute-start.3 = (f32[96,128]{1,0:T(8,128)S(1)}, f32[96,128]{1,0:T(8,128)S(1)}, u32[]{:S(2)}, u32[]{:S(2)}) collective-permute-start(f32[96,128]{1,0:T(8,128)S(1)} %get-tuple-element.17), channel_id=1, source_target_pairs={{0,3},{1,2},{2,1},{3,0},{4,7},{5,6},{6,5},{7,4},{8,11},{9,10},{10,... | collective-permute-start | bytes 147464 | tf_op jit(solution)/shard_map/ppermute | solution.py:263
  10.9 4.1 %collective-permute-start.4 = (f32[96,128]{1,0:T(8,128)S(1)}, f32[96,128]{1,0:T(8,128)S(1)}, u32[]{:S(2)}, u32[]{:S(2)}) collective-permute-start(f32[96,128]{1,0:T(8,128)S(1)} %get-tuple-element.18), channel_id=1, source_target_pairs={{0,2},{1,3},{2,0},{3,1},{4,6},{5,7},{6,4},{7,5},{8,10},{9,11},{10,... | collective-permute-start | bytes 147464 | tf_op jit(solution)/shard_map/ppermute | solution.py:263
  11.3 4.1 %collective-permute-start.5 = (f32[96,128]{1,0:T(8,128)S(1)}, f32[96,128]{1,0:T(8,128)S(1)}, u32[]{:S(2)}, u32[]{:S(2)}) collective-permute-start(f32[96,128]{1,0:T(8,128)S(1)} %get-tuple-element.19), channel_id=1, source_target_pairs={{0,1},{1,0},{2,3},{3,2},{4,5},{5,4},{6,7},{7,6},{8,9},{9,8},{10,11... | collective-permute-start | bytes 147464 | tf_op jit(solution)/shard_map/ppermute | solution.py:263
  15.4 4.9 %collective-permute-start.6 = (f32[64,128]{1,0:T(8,128)S(1)}, f32[64,128]{1,0:T(8,128)S(1)}, u32[]{:S(2)}, u32[]{:S(2)}) collective-permute-start(f32[64,128]{1,0:T(8,128)S(1)} %get-tuple-element.21), channel_id=1, source_target_pairs={{0,4},{1,5},{2,6},{3,7},{4,0},{5,1},{6,2},{7,3},{8,12},{9,13},{10,... | collective-permute-start | bytes 98312 | tf_op jit(solution)/shard_map/ppermute | solution.py:279

commit v13 on v9

--- a/solution.py
+++ b/solution.py
@@ -228,7 +228,7 @@
     rank = factor_three.shape[1]
     owned = rows // blocks
     half = owned // 2
-    chunk = min(16, half)
+    chunk = min(8, half)
     count = blocks // 4
     f32 = functools.partial(pltpu.VMEM, dtype=jnp.float32)
     packed = f32((rank // 2, 2 * rank))

time: 22.8 us -> 22.8 us (level)
  no operation moved by 1% of the time
where the time goes in v13:
time: 22.8 us; the launch traced here: 22.7 us
  Pallas kernels  9.79 us (43%)
  starting transfers between devices  9.23 us (40%)
  waiting for transfers between devices  3.59 us (16%)
    pallas_call x5, Pallas kernels, call(): pl.pallas_call(kernel, out_shape=out_shape, in_specs=specs or [WHOLE] * l...  9.79 us
    ppermute x3, starting transfers between devices, body(): lax.ppermute(value, 'gy', [(i, i - i % 4 + table[i % 4]) for i in range(b...  3.49 us
    ppermute x3, starting transfers between devices, body(): lax.ppermute(mine, 'gx', [(i, i ^ distance) for i in range(groups)])  3.08 us
    ppermute x1, starting transfers between devices, body(): lax.ppermute(value, 'gy', [(i, i ^ 4 * distance) for i in range(blocks)])  2.65 us
    ppermute x1, waiting for transfers between devices, body(): lax.ppermute(value, 'gy', [(i, i ^ 4 * distance) for i in range(blocks)])  2.23 us
    ppermute x3, waiting for transfers between devices, body(): lax.ppermute(value, 'gy', [(i, i - i % 4 + table[i % 4]) for i in range(b...  1.14 us
  transfers between devices with their start and end apart: 7, of which 4 were waited for; matrix products, arithmetic and copies ran while one was open for 0% of the time, Pallas kernels for 24%

profile of v13, /device:TPU:0, one launch (start us, length us, event | category | flops | bytes accessed | tf_op | source)
XLA Modules:
  0.0 22.7 jit_solution(4912656802411706589)
XLA Ops:
  0.0 0.0 copy-start.1
  0.0 0.0 copy-start
  0.0 2.4 %collective-permute-start.2 = (f32[16,128]{1,0:T(8,128)}, f32[16,128]{1,0:T(8,128)S(1)}, u32[]{:S(2)}, u32[]{:S(2)}) collective-permute-start(f32[16,128]{1,0:T(8,128)} %bitcast.2), channel_id=1, source_target_pairs={{0,24},{8,16},{16,8},{24,0},{1,25},{9,17},{17,9},{25,1},{2,26},{10... | collective-permute-start | bytes 24584 | tf_op jit(solution)/shard_map/ppermute | solution.py:245
  2.4 0.6 %collective-permute-start.1 = (f32[16,128]{1,0:T(8,128)}, f32[16,128]{1,0:T(8,128)S(1)}, u32[]{:S(2)}, u32[]{:S(2)}) collective-permute-start(f32[16,128]{1,0:T(8,128)} %bitcast.3), channel_id=1, source_target_pairs={{0,16},{8,24},{16,0},{24,8},{1,17},{9,25},{17,1},{25,9},{2,18},{10... | collective-permute-start | bytes 24584 | tf_op jit(solution)/shard_map/ppermute | solution.py:245
  3.0 0.0 collective-permute-start
  3.1 2.9 %shard_map.37.split_ref = bf16[12288,256]{1,0:T(8,128)(2,1)S(1)} custom-call(f32[512,32,128]{2,1,0:T(8,128)} %bitcast.6), custom_call_target="tpu_custom_call" | custom-call | flops 1000000000 | bytes 20971520 | tf_op jit(solution)/shard_map/pallas_call | solution.py:214
  6.0 0.0 collective-permute-done.2.refs_3_
  6.0 0.2 collective-permute-done.1.refs_2_
  6.3 0.0 collective-permute-done.refs_1_
  6.3 0.0 copy-done.1
  6.3 0.0 copy-done
  6.3 2.0 %shard_map.38 = (f32[96,128]{1,0:T(8,128)S(1)}, f32[96,128]{1,0:T(8,128)S(1)}, f32[96,128]{1,0:T(8,128)S(1)}, f32[32,128]{1,0:T(8,128)S(1)}, bf16[256,128]{1,0:T(8,128)(2,1)S(1)}) custom-call(bf16[12288,256]{1,0:T(8,128)(2,1)S(1)} %shard_map.37.split_ref, f32[32,64]{1,0:T(8,128)S(1)} %copy-done, f32[16,128]{1,0:T(8,128)S(1)} %bitcast.5, ...), custom_call_target="tpu_custom_call" | custom-call | flops 2000000000 | bytes 12918784 | tf_op jit(solution)/shard_map/pallas_call | solution.py:214
  8.3 2.5 %collective-permute-start.3 = (f32[96,128]{1,0:T(8,128)S(1)}, f32[96,128]{1,0:T(8,128)S(1)}, u32[]{:S(2)}, u32[]{:S(2)}) collective-permute-start(f32[96,128]{1,0:T(8,128)S(1)} %get-tuple-element.17), channel_id=1, source_target_pairs={{0,3},{1,2},{2,1},{3,0},{4,7},{5,6},{6,5},{7,4},{8,11},{9,10},{10,... | collective-permute-start | bytes 147464 | tf_op jit(solution)/shard_map/ppermute | solution.py:267
  10.9 0.5 %collective-permute-start.4 = (f32[96,128]{1,0:T(8,128)S(1)}, f32[96,128]{1,0:T(8,128)S(1)}, u32[]{:S(2)}, u32[]{:S(2)}) collective-permute-start(f32[96,128]{1,0:T(8,128)S(1)} %get-tuple-element.18), channel_id=1, source_target_pairs={{0,2},{1,3},{2,0},{3,1},{4,6},{5,7},{6,4},{7,5},{8,10},{9,11},{10,... | collective-permute-start | bytes 147464 | tf_op jit(solution)/shard_map/ppermute | solution.py:267
  11.3 0.5 %collective-permute-start.5 = (f32[96,128]{1,0:T(8,128)S(1)}, f32[96,128]{1,0:T(8,128)S(1)}, u32[]{:S(2)}, u32[]{:S(2)}) collective-permute-start(f32[96,128]{1,0:T(8,128)S(1)} %get-tuple-element.19), channel_id=1, source_target_pairs={{0,1},{1,0},{2,3},{3,2},{4,5},{5,4},{6,7},{7,6},{8,9},{9,8},{10,11... | collective-permute-start | bytes 147464 | tf_op jit(solution)/shard_map/ppermute | solution.py:267
  11.8 2.4 %shard_map.39 = (f32[96,128]{1,0:T(8,128)S(1)}, f32[32,128]{1,0:T(8,128)S(1)}) custom-call(f32[512,32,128]{2,1,0:T(8,128)} %bitcast.7, bf16[256,128]{1,0:T(8,128)(2,1)S(1)} %get-tuple-element.14.weight_ref, f32[32,64]{1,0:T(8,128)S(1)} %copy-done, f32[32,128]{1,0:T(8,128)S(1)} %get-tuple-element.15.gram_ref), custom_call_target="tpu_custom_call" | custom-call | flops 2000000000 | bytes 8609792 | tf_op jit(solution)/shard_map/pallas_call | solution.py:214
  14.3 0.0 collective-permute-done.3.refs_1_
  14.3 0.7 %collective-permute-done.4.refs_2_ = f32[96,128]{1,0:T(8,128)S(1)} collective-permute-done((f32[96,128]{1,0:T(8,128)S(1)}, f32[96,128]{1,0:T(8,128)S(1)}, u32[]{:S(2)}, u32[]{:S(2)}) %collective-permute-start.4) | collective-permute-done | bytes 49184 | tf_op jit(solution)/shard_map/ppermute | solution.py:267
  14.9 0.5 %collective-permute-done.5.refs_3_ = f32[96,128]{1,0:T(8,128)S(1)} collective-permute-done((f32[96,128]{1,0:T(8,128)S(1)}, f32[96,128]{1,0:T(8,128)S(1)}, u32[]{:S(2)}, u32[]{:S(2)}) %collective-permute-start.5) | collective-permute-done | bytes 49184 | tf_op jit(solution)/shard_map/ppermute | solution.py:267
  15.4 2.7 %collective-permute-start.6 = (f32[64,128]{1,0:T(8,128)S(1)}, f32[64,128]{1,0:T(8,128)S(1)}, u32[]{:S(2)}, u32[]{:S(2)}) collective-permute-start(f32[64,128]{1,0:T(8,128)S(1)} %get-tuple-element.21), channel_id=1, source_target_pairs={{0,4},{1,5},{2,6},{3,7},{4,0},{5,1},{6,2},{7,3},{8,12},{9,13},{10,... | collective-permute-start | bytes 98312 | tf_op jit(solution)/shard_map/ppermute | solution.py:283
  18.1 2.2 %collective-permute-done.6.refs_1_ = f32[64,128]{1,0:T(8,128)S(1)} collective-permute-done((f32[64,128]{1,0:T(8,128)S(1)}, f32[64,128]{1,0:T(8,128)S(1)}, u32[]{:S(2)}, u32[]{:S(2)}) %collective-permute-start.6) | collective-permute-done | bytes 32800 | tf_op jit(solution)/shard_map/ppermute | solution.py:283
  20.3 2.4 %shard_map.41 = f32[64,64]{1,0:T(8,128)} custom-call(f32[64,128]{1,0:T(8,128)S(1)} %get-tuple-element.20.refs_0_, f32[64,128]{1,0:T(8,128)S(1)} %collective-permute-done.6.refs_1_, f32[32,128]{1,0:T(8,128)S(1)} %get-tuple-element.22.refs_2_), custom_call_target="tpu_custom_call" | custom-call | flops 100000000 | bytes 98304 | tf_op jit(solution)/shard_map/pallas_call | solution.py:214
  (1 shorter events, 0.0 us)
Async XLA Ops:
  0.0 6.3 %copy-start.1 = (f32[128,16]{0,1:T(8,128)S(1)}, f32[128,16]{0,1:T(8,128)}, u32[]{:S(2)}) copy-start(f32[128,16]{0,1:T(8,128)} %param.4) | copy-start | bytes 24580
  0.0 6.3 %copy-start = (f32[32,64]{1,0:T(8,128)S(1)}, f32[32,64]{1,0:T(8,128)}, u32[]{:S(2)}) copy-start(f32[32,64]{1,0:T(8,128)} %three_ref.3) | copy-start | bytes 24580
  0.0 6.0 %collective-permute-start.2 = (f32[16,128]{1,0:T(8,128)}, f32[16,128]{1,0:T(8,128)S(1)}, u32[]{:S(2)}, u32[]{:S(2)}) collective-permute-start(f32[16,128]{1,0:T(8,128)} %bitcast.2), channel_id=1, source_target_pairs={{0,24},{8,16},{16,8},{24,0},{1,25},{9,17},{17,9},{25,1},{2,26},{10... | collective-permute-start | bytes 24584 | tf_op jit(solution)/shard_map/ppermute | solution.py:245
  2.4 3.9 %collective-permute-start.1 = (f32[16,128]{1,0:T(8,128)}, f32[16,128]{1,0:T(8,128)S(1)}, u32[]{:S(2)}, u32[]{:S(2)}) collective-permute-start(f32[16,128]{1,0:T(8,128)} %bitcast.3), channel_id=1, source_target_pairs={{0,16},{8,24},{16,0},{24,8},{1,17},{9,25},{17,1},{25,9},{2,18},{10... | collective-permute-start | bytes 24584 | tf_op jit(solution)/shard_map/ppermute | solution.py:245
  3.0 3.2 %collective-permute-start = (f32[16,128]{1,0:T(8,128)}, f32[16,128]{1,0:T(8,128)S(1)}, u32[]{:S(2)}, u32[]{:S(2)}) collective-permute-start(f32[16,128]{1,0:T(8,128)} %bitcast.4), channel_id=1, source_target_pairs={{0,8},{8,0},{16,24},{24,16},{1,9},{9,1},{17,25},{25,17},{2,10},{10... | collective-permute-start | bytes 24584 | tf_op jit(solution)/shard_map/ppermute | solution.py:245
  8.3 5.9 %collective-permute-start.3 = (f32[96,128]{1,0:T(8,128)S(1)}, f32[96,128]{1,0:T(8,128)S(1)}, u32[]{:S(2)}, u32[]{:S(2)}) collective-permute-start(f32[96,128]{1,0:T(8,128)S(1)} %get-tuple-element.17), channel_id=1, source_target_pairs={{0,3},{1,2},{2,1},{3,0},{4,7},{5,6},{6,5},{7,4},{8,11},{9,10},{10,... | collective-permute-start | bytes 147464 | tf_op jit(solution)/shard_map/ppermute | solution.py:267
  10.9 4.1 %collective-permute-start.4 = (f32[96,128]{1,0:T(8,128)S(1)}, f32[96,128]{1,0:T(8,128)S(1)}, u32[]{:S(2)}, u32[]{:S(2)}) collective-permute-start(f32[96,128]{1,0:T(8,128)S(1)} %get-tuple-element.18), channel_id=1, source_target_pairs={{0,2},{1,3},{2,0},{3,1},{4,6},{5,7},{6,4},{7,5},{8,10},{9,11},{10,... | collective-permute-start | bytes 147464 | tf_op jit(solution)/shard_map/ppermute | solution.py:267
  11.3 4.1 %collective-permute-start.5 = (f32[96,128]{1,0:T(8,128)S(1)}, f32[96,128]{1,0:T(8,128)S(1)}, u32[]{:S(2)}, u32[]{:S(2)}) collective-permute-start(f32[96,128]{1,0:T(8,128)S(1)} %get-tuple-element.19), channel_id=1, source_target_pairs={{0,1},{1,0},{2,3},{3,2},{4,5},{5,4},{6,7},{7,6},{8,9},{9,8},{10,11... | collective-permute-start | bytes 147464 | tf_op jit(solution)/shard_map/ppermute | solution.py:267
  15.4 4.9 %collective-permute-start.6 = (f32[64,128]{1,0:T(8,128)S(1)}, f32[64,128]{1,0:T(8,128)S(1)}, u32[]{:S(2)}, u32[]{:S(2)}) collective-permute-start(f32[64,128]{1,0:T(8,128)S(1)} %get-tuple-element.21), channel_id=1, source_target_pairs={{0,4},{1,5},{2,6},{3,7},{4,0},{5,1},{6,2},{7,3},{8,12},{9,13},{10,... | collective-permute-start | bytes 98312 | tf_op jit(solution)/shard_map/ppermute | solution.py:283

commit v14 on v9

--- a/solution.py
+++ b/solution.py
@@ -16,6 +16,15 @@
     return lax.dot_general(
         left, right, ((dims[:1], dims[1:]), ((), ())), precision=HIGHEST, preferred_element_type=jnp.float32
     )
+
+
+def narrow_dot(left, right, dims):
+    return lax.dot_general(left, right, ((dims[:1], dims[1:]), ((), ())), preferred_element_type=jnp.float32)
+
+
+def parted(values):
+    high = values.astype(jnp.bfloat16).astype(jnp.float32)
+    return high, values - high
 
 
 def pack(values):
@@ -95,13 +104,17 @@
     for distance, ref in enumerate(shares):
         two_ref[pl.ds(pl.multiple_of((me ^ distance) * share, share), share), :] = ref[...]
     two = two_ref[...]
-    gram = pack(dot_of(two, two, (1, 1)))
+    high, low = parted(two)
+    stacked = jnp.concatenate([high, low], axis=0)
+    both = stacked.T.astype(jnp.bfloat16)
+    weight_ref[...] = jnp.concatenate([both, both], axis=0)
+    product = narrow_dot(stacked.astype(jnp.bfloat16), both, (1, 0))
+    rank = two.shape[0]
+    product = product[:rank] + product[rank:]
+    gram = pack((product + pltpu.roll(product, rank, 1))[:, :rank])
     gram_ref[...] = gram
     for out_ref in outs:
         out_ref[count * (sum_ref.shape[0] // 2) :, :] = gram
-    high = two.astype(jnp.bfloat16).astype(jnp.float32)
-    both = jnp.concatenate([high, two - high], axis=0).T.astype(jnp.bfloat16)
-    weight_ref[...] = jnp.concatenate([both, both], axis=0)
 
     def take(start):
         return split_ref[start * depth : (start + chunk) * depth, :]
@@ -203,9 +216,21 @@
             column = [lane(bands[h], base + q) for q in range(8)]
             for q in range(8):
                 bands[h] = follow(bands[h], column, q)
-    lower = jnp.concatenate(bands, axis=0)
-    solved = dot_of(right, lower, (1, 1))
-    out_ref[...] = dot_of(solved, lower, (1, 0))[:, :order]
+    left = lane_ids < order
+    lower = jnp.where(left, jnp.concatenate(bands, axis=0), 0.0)
+    lower_high, lower_low = parted(lower)
+    right_high, right_low = parted(right)
+    doubled = lower_high + pltpu.roll(lower_high, order, 1)
+    factors = jnp.concatenate([doubled, lower_low], axis=1).astype(jnp.bfloat16)
+    terms = jnp.concatenate([right_high + pltpu.roll(right_low, order, 1), right_high], axis=1).astype(jnp.bfloat16)
+    solved = narrow_dot(terms, jnp.concatenate([factors, factors], axis=0), (1, 1))
+    solved_high, solved_low = parted(solved)
+    inside = lax.broadcasted_iota(jnp.int32, solved.shape, 1) < order
+    terms = jnp.concatenate(
+        [jnp.where(inside, solved_high, solved_low), jnp.where(inside, solved_high, 0.0)], axis=1
+    ).astype(jnp.bfloat16)
+    factors = jnp.concatenate([lower_high, lower_high, lower_low, lower_low], axis=0).astype(jnp.bfloat16)
+    out_ref[...] = narrow_dot(terms, factors, (1, 0))[:, :order]
 
 
 def call(kernel, out_shape, args, flops, limit, scratch=(), specs=None):

time: 22.8 us -> 22.8 us (level)
  no operation moved by 1% of the time
where the time goes in v14:
time: 22.8 us; the launch traced here: 22.6 us
  Pallas kernels  9.84 us (43%)
  starting transfers between devices  9.24 us (41%)
  waiting for transfers between devices  3.5 us (15%)
    pallas_call x5, Pallas kernels, call(): pl.pallas_call(kernel, out_shape=out_shape, in_specs=specs or [WHOLE] * l...  9.84 us
    ppermute x3, starting transfers between devices, body(): lax.ppermute(value, 'gy', [(i, i - i % 4 + table[i % 4]) for i in range(b...  3.5 us
    ppermute x3, starting transfers between devices, body(): lax.ppermute(mine, 'gx', [(i, i ^ distance) for i in range(groups)])  3.08 us
    ppermute x1, starting transfers between devices, body(): lax.ppermute(value, 'gy', [(i, i ^ 4 * distance) for i in range(blocks)])  2.65 us
    ppermute x1, waiting for transfers between devices, body(): lax.ppermute(value, 'gy', [(i, i ^ 4 * distance) for i in range(blocks)])  2.22 us
    ppermute x3, waiting for transfers between devices, body(): lax.ppermute(value, 'gy', [(i, i - i % 4 + table[i % 4]) for i in range(b...  1.05 us
  transfers between devices with their start and end apart: 7, of which 4 were waited for; matrix products, arithmetic and copies ran while one was open for 0% of the time, Pallas kernels for 24%

profile of v14, /device:TPU:0, one launch (start us, length us, event | category | flops | bytes accessed | tf_op | source)
XLA Modules:
  0.0 22.6 jit_solution(15815835060243996324)
XLA Ops:
  0.0 0.0 copy-start.1
  0.0 0.0 copy-start
  0.0 2.4 %collective-permute-start.2 = (f32[16,128]{1,0:T(8,128)}, f32[16,128]{1,0:T(8,128)S(1)}, u32[]{:S(2)}, u32[]{:S(2)}) collective-permute-start(f32[16,128]{1,0:T(8,128)} %bitcast.2), channel_id=1, source_target_pairs={{0,24},{8,16},{16,8},{24,0},{1,25},{9,17},{17,9},{25,1},{2,26},{10... | collective-permute-start | bytes 24584 | tf_op jit(solution)/shard_map/ppermute | solution.py:270
  2.4 0.6 %collective-permute-start.1 = (f32[16,128]{1,0:T(8,128)}, f32[16,128]{1,0:T(8,128)S(1)}, u32[]{:S(2)}, u32[]{:S(2)}) collective-permute-start(f32[16,128]{1,0:T(8,128)} %bitcast.3), channel_id=1, source_target_pairs={{0,16},{8,24},{16,0},{24,8},{1,17},{9,25},{17,1},{25,9},{2,18},{10... | collective-permute-start | bytes 24584 | tf_op jit(solution)/shard_map/ppermute | solution.py:270
  3.0 0.0 collective-permute-start
  3.1 2.9 %shard_map.37.split_ref = bf16[12288,256]{1,0:T(8,128)(2,1)S(1)} custom-call(f32[512,32,128]{2,1,0:T(8,128)} %bitcast.6), custom_call_target="tpu_custom_call" | custom-call | flops 1000000000 | bytes 20971520 | tf_op jit(solution)/shard_map/pallas_call | solution.py:239
  6.0 0.0 collective-permute-done.2.refs_3_
  6.0 0.2 collective-permute-done.1.refs_2_
  6.3 0.0 collective-permute-done.refs_1_
  6.3 0.0 copy-done.1
  6.3 0.0 copy-done
  6.3 2.0 %shard_map.38 = (f32[96,128]{1,0:T(8,128)S(1)}, f32[96,128]{1,0:T(8,128)S(1)}, f32[96,128]{1,0:T(8,128)S(1)}, f32[32,128]{1,0:T(8,128)S(1)}, bf16[256,128]{1,0:T(8,128)(2,1)S(1)}) custom-call(bf16[12288,256]{1,0:T(8,128)(2,1)S(1)} %shard_map.37.split_ref, f32[32,64]{1,0:T(8,128)S(1)} %copy-done, f32[16,128]{1,0:T(8,128)S(1)} %bitcast.5, ...), custom_call_target="tpu_custom_call" | custom-call | flops 2000000000 | bytes 12918784 | tf_op jit(solution)/shard_map/pallas_call | solution.py:239
  8.3 2.5 %collective-permute-start.3 = (f32[96,128]{1,0:T(8,128)S(1)}, f32[96,128]{1,0:T(8,128)S(1)}, u32[]{:S(2)}, u32[]{:S(2)}) collective-permute-start(f32[96,128]{1,0:T(8,128)S(1)} %get-tuple-element.17), channel_id=1, source_target_pairs={{0,3},{1,2},{2,1},{3,0},{4,7},{5,6},{6,5},{7,4},{8,11},{9,10},{10,... | collective-permute-start | bytes 147464 | tf_op jit(solution)/shard_map/ppermute | solution.py:292
  10.8 0.5 %collective-permute-start.4 = (f32[96,128]{1,0:T(8,128)S(1)}, f32[96,128]{1,0:T(8,128)S(1)}, u32[]{:S(2)}, u32[]{:S(2)}) collective-permute-start(f32[96,128]{1,0:T(8,128)S(1)} %get-tuple-element.18), channel_id=1, source_target_pairs={{0,2},{1,3},{2,0},{3,1},{4,6},{5,7},{6,4},{7,5},{8,10},{9,11},{10,... | collective-permute-start | bytes 147464 | tf_op jit(solution)/shard_map/ppermute | solution.py:292
  11.3 0.5 %collective-permute-start.5 = (f32[96,128]{1,0:T(8,128)S(1)}, f32[96,128]{1,0:T(8,128)S(1)}, u32[]{:S(2)}, u32[]{:S(2)}) collective-permute-start(f32[96,128]{1,0:T(8,128)S(1)} %get-tuple-element.19), channel_id=1, source_target_pairs={{0,1},{1,0},{2,3},{3,2},{4,5},{5,4},{6,7},{7,6},{8,9},{9,8},{10,11... | collective-permute-start | bytes 147464 | tf_op jit(solution)/shard_map/ppermute | solution.py:292
  11.8 2.5 %shard_map.39 = (f32[96,128]{1,0:T(8,128)S(1)}, f32[32,128]{1,0:T(8,128)S(1)}) custom-call(f32[512,32,128]{2,1,0:T(8,128)} %bitcast.7, bf16[256,128]{1,0:T(8,128)(2,1)S(1)} %get-tuple-element.14.weight_ref, f32[32,64]{1,0:T(8,128)S(1)} %copy-done, f32[32,128]{1,0:T(8,128)S(1)} %get-tuple-element.15.gram_ref), custom_call_target="tpu_custom_call" | custom-call | flops 2000000000 | bytes 8609792 | tf_op jit(solution)/shard_map/pallas_call | solution.py:239
  14.3 0.0 collective-permute-done.3.refs_1_
  14.3 0.6 %collective-permute-done.4.refs_2_ = f32[96,128]{1,0:T(8,128)S(1)} collective-permute-done((f32[96,128]{1,0:T(8,128)S(1)}, f32[96,128]{1,0:T(8,128)S(1)}, u32[]{:S(2)}, u32[]{:S(2)}) %collective-permute-start.4) | collective-permute-done | bytes 49184 | tf_op jit(solution)/shard_map/ppermute | solution.py:292
  14.9 0.5 %collective-permute-done.5.refs_3_ = f32[96,128]{1,0:T(8,128)S(1)} collective-permute-done((f32[96,128]{1,0:T(8,128)S(1)}, f32[96,128]{1,0:T(8,128)S(1)}, u32[]{:S(2)}, u32[]{:S(2)}) %collective-permute-start.5) | collective-permute-done | bytes 49184 | tf_op jit(solution)/shard_map/ppermute | solution.py:292
  15.4 2.7 %collective-permute-start.6 = (f32[64,128]{1,0:T(8,128)S(1)}, f32[64,128]{1,0:T(8,128)S(1)}, u32[]{:S(2)}, u32[]{:S(2)}) collective-permute-start(f32[64,128]{1,0:T(8,128)S(1)} %get-tuple-element.21), channel_id=1, source_target_pairs={{0,4},{1,5},{2,6},{3,7},{4,0},{5,1},{6,2},{7,3},{8,12},{9,13},{10,... | collective-permute-start | bytes 98312 | tf_op jit(solution)/shard_map/ppermute | solution.py:308
  18.0 2.2 %collective-permute-done.6.refs_1_ = f32[64,128]{1,0:T(8,128)S(1)} collective-permute-done((f32[64,128]{1,0:T(8,128)S(1)}, f32[64,128]{1,0:T(8,128)S(1)}, u32[]{:S(2)}, u32[]{:S(2)}) %collective-permute-start.6) | collective-permute-done | bytes 32800 | tf_op jit(solution)/shard_map/ppermute | solution.py:308
  20.3 2.4 %shard_map.41 = f32[64,64]{1,0:T(8,128)} custom-call(f32[64,128]{1,0:T(8,128)S(1)} %get-tuple-element.20.refs_0_, f32[64,128]{1,0:T(8,128)S(1)} %collective-permute-done.6.refs_1_, f32[32,128]{1,0:T(8,128)S(1)} %get-tuple-element.22.refs_2_), custom_call_target="tpu_custom_call" | custom-call | flops 100000000 | bytes 98304 | tf_op jit(solution)/shard_map/pallas_call | solution.py:239
  (1 shorter events, 0.0 us)
Async XLA Ops:
  0.0 6.3 %copy-start.1 = (f32[128,16]{0,1:T(8,128)S(1)}, f32[128,16]{0,1:T(8,128)}, u32[]{:S(2)}) copy-start(f32[128,16]{0,1:T(8,128)} %param.4) | copy-start | bytes 24580
  0.0 6.3 %copy-start = (f32[32,64]{1,0:T(8,128)S(1)}, f32[32,64]{1,0:T(8,128)}, u32[]{:S(2)}) copy-start(f32[32,64]{1,0:T(8,128)} %three_ref.3) | copy-start | bytes 24580
  0.0 6.0 %collective-permute-start.2 = (f32[16,128]{1,0:T(8,128)}, f32[16,128]{1,0:T(8,128)S(1)}, u32[]{:S(2)}, u32[]{:S(2)}) collective-permute-start(f32[16,128]{1,0:T(8,128)} %bitcast.2), channel_id=1, source_target_pairs={{0,24},{8,16},{16,8},{24,0},{1,25},{9,17},{17,9},{25,1},{2,26},{10... | collective-permute-start | bytes 24584 | tf_op jit(solution)/shard_map/ppermute | solution.py:270
  2.4 3.9 %collective-permute-start.1 = (f32[16,128]{1,0:T(8,128)}, f32[16,128]{1,0:T(8,128)S(1)}, u32[]{:S(2)}, u32[]{:S(2)}) collective-permute-start(f32[16,128]{1,0:T(8,128)} %bitcast.3), channel_id=1, source_target_pairs={{0,16},{8,24},{16,0},{24,8},{1,17},{9,25},{17,1},{25,9},{2,18},{10... | collective-permute-start | bytes 24584 | tf_op jit(solution)/shard_map/ppermute | solution.py:270
  3.0 3.2 %collective-permute-start = (f32[16,128]{1,0:T(8,128)}, f32[16,128]{1,0:T(8,128)S(1)}, u32[]{:S(2)}, u32[]{:S(2)}) collective-permute-start(f32[16,128]{1,0:T(8,128)} %bitcast.4), channel_id=1, source_target_pairs={{0,8},{8,0},{16,24},{24,16},{1,9},{9,1},{17,25},{25,17},{2,10},{10... | collective-permute-start | bytes 24584 | tf_op jit(solution)/shard_map/ppermute | solution.py:270
  8.3 6.0 %collective-permute-start.3 = (f32[96,128]{1,0:T(8,128)S(1)}, f32[96,128]{1,0:T(8,128)S(1)}, u32[]{:S(2)}, u32[]{:S(2)}) collective-permute-start(f32[96,128]{1,0:T(8,128)S(1)} %get-tuple-element.17), channel_id=1, source_target_pairs={{0,3},{1,2},{2,1},{3,0},{4,7},{5,6},{6,5},{7,4},{8,11},{9,10},{10,... | collective-permute-start | bytes 147464 | tf_op jit(solution)/shard_map/ppermute | solution.py:292
  10.8 4.1 %collective-permute-start.4 = (f32[96,128]{1,0:T(8,128)S(1)}, f32[96,128]{1,0:T(8,128)S(1)}, u32[]{:S(2)}, u32[]{:S(2)}) collective-permute-start(f32[96,128]{1,0:T(8,128)S(1)} %get-tuple-element.18), channel_id=1, source_target_pairs={{0,2},{1,3},{2,0},{3,1},{4,6},{5,7},{6,4},{7,5},{8,10},{9,11},{10,... | collective-permute-start | bytes 147464 | tf_op jit(solution)/shard_map/ppermute | solution.py:292
  11.3 4.1 %collective-permute-start.5 = (f32[96,128]{1,0:T(8,128)S(1)}, f32[96,128]{1,0:T(8,128)S(1)}, u32[]{:S(2)}, u32[]{:S(2)}) collective-permute-start(f32[96,128]{1,0:T(8,128)S(1)} %get-tuple-element.19), channel_id=1, source_target_pairs={{0,1},{1,0},{2,3},{3,2},{4,5},{5,4},{6,7},{7,6},{8,9},{9,8},{10,11... | collective-permute-start | bytes 147464 | tf_op jit(solution)/shard_map/ppermute | solution.py:292
  15.4 4.9 %collective-permute-start.6 = (f32[64,128]{1,0:T(8,128)S(1)}, f32[64,128]{1,0:T(8,128)S(1)}, u32[]{:S(2)}, u32[]{:S(2)}) collective-permute-start(f32[64,128]{1,0:T(8,128)S(1)} %get-tuple-element.21), channel_id=1, source_target_pairs={{0,4},{1,5},{2,6},{3,7},{4,0},{5,1},{6,2},{7,3},{8,12},{9,13},{10,... | collective-permute-start | bytes 98312 | tf_op jit(solution)/shard_map/ppermute | solution.py:308

commit v15 on v9

--- a/solution.py
+++ b/solution.py
@@ -16,6 +16,15 @@
     return lax.dot_general(
         left, right, ((dims[:1], dims[1:]), ((), ())), precision=HIGHEST, preferred_element_type=jnp.float32
     )
+
+
+def narrow_dot(left, right, dims):
+    return lax.dot_general(left, right, ((dims[:1], dims[1:]), ((), ())), preferred_element_type=jnp.float32)
+
+
+def parted(values):
+    high = values.astype(jnp.bfloat16).astype(jnp.float32)
+    return high, values - high
 
 
 def pack(values):
@@ -95,13 +104,17 @@
     for distance, ref in enumerate(shares):
         two_ref[pl.ds(pl.multiple_of((me ^ distance) * share, share), share), :] = ref[...]
     two = two_ref[...]
-    gram = pack(dot_of(two, two, (1, 1)))
+    high, low = parted(two)
+    stacked = jnp.concatenate([high, low], axis=0)
+    both = stacked.T.astype(jnp.bfloat16)
+    weight_ref[...] = jnp.concatenate([both, both], axis=0)
+    product = narrow_dot(stacked.astype(jnp.bfloat16), both, (1, 0))
+    rank = two.shape[0]
+    product = product[:rank] + product[rank:]
+    gram = pack((product + pltpu.roll(product, rank, 1))[:, :rank])
     gram_ref[...] = gram
     for out_ref in outs:
         out_ref[count * (sum_ref.shape[0] // 2) :, :] = gram
-    high = two.astype(jnp.bfloat16).astype(jnp.float32)
-    both = jnp.concatenate([high, two - high], axis=0).T.astype(jnp.bfloat16)
-    weight_ref[...] = jnp.concatenate([both, both], axis=0)
 
     def take(start):
         return split_ref[start * depth : (start + chunk) * depth, :]
@@ -164,15 +177,14 @@
 
     for own in range(len(bands)):
         base = 8 * own
-        spot = 72 * own
+        spot = 64 * own
         for p in range(8):
             spread_ref[spot + 8 * p : spot + 8 * p + 8, :] = lane(bands[own], base + p)
-        spread_ref[spot + 64 : spot + 72, :] = bands[own]
 
         def spread(place):
             return jnp.broadcast_to(spread_ref[place : place + 1, :], tile)
 
-        line = [spread(spot + 64 + q) for q in range(8)]
+        line = [jnp.broadcast_to(bands[own][q : q + 1], tile) for q in range(8)]
         entry = [[spread(spot + 8 * p + q) if p >= q else None for p in range(8)] for q in range(8)]
         inverse, done = [None] * 8, None
 
@@ -284,7 +296,7 @@
         for distance, value in enumerate(sent, 1)
     ]
     return call(
-        solve_kernel, jax.ShapeDtypeStruct((owned, rank), jnp.float32), (kept, *parts, three_gram), 10**8, 12, [f32((9 * rank, 2 * rank))]
+        solve_kernel, jax.ShapeDtypeStruct((owned, rank), jnp.float32), (kept, *parts, three_gram), 10**8, 12, [f32((8 * rank, 2 * rank))]
     )
 
 

time: 22.8 us -> 22.8 us (level)
  no operation moved by 1% of the time
where the time goes in v15:
time: 22.8 us; the launch traced here: 22.6 us
  Pallas kernels  9.86 us (43%)
  starting transfers between devices  9.24 us (41%)
  waiting for transfers between devices  3.5 us (15%)
    pallas_call x5, Pallas kernels, call(): pl.pallas_call(kernel, out_shape=out_shape, in_specs=specs or [WHOLE] * l...  9.86 us
    ppermute x3, starting transfers between devices, body(): lax.ppermute(value, 'gy', [(i, i - i % 4 + table[i % 4]) for i in range(b...  3.5 us
    ppermute x3, starting transfers between devices, body(): lax.ppermute(mine, 'gx', [(i, i ^ distance) for i in range(groups)])  3.08 us
    ppermute x1, starting transfers between devices, body(): lax.ppermute(value, 'gy', [(i, i ^ 4 * distance) for i in range(blocks)])  2.65 us
    ppermute x1, waiting for transfers between devices, body(): lax.ppermute(value, 'gy', [(i, i ^ 4 * distance) for i in range(blocks)])  2.22 us
    ppermute x3, waiting for transfers between devices, body(): lax.ppermute(value, 'gy', [(i, i - i % 4 + table[i % 4]) for i in range(b...  1.05 us
  transfers between devices with their start and end apart: 7, of which 4 were waited for; matrix products, arithmetic and copies ran while one was open for 0% of the time, Pallas kernels for 24%

profile of v15, /device:TPU:0, one launch (start us, length us, event | category | flops | bytes accessed | tf_op | source)
XLA Modules:
  0.0 22.6 jit_solution(3709234526084297623)
XLA Ops:
  0.0 0.0 copy-start.1
  0.0 0.0 copy-start
  0.0 2.4 %collective-permute-start.2 = (f32[16,128]{1,0:T(8,128)}, f32[16,128]{1,0:T(8,128)S(1)}, u32[]{:S(2)}, u32[]{:S(2)}) collective-permute-start(f32[16,128]{1,0:T(8,128)} %bitcast.2), channel_id=1, source_target_pairs={{0,24},{8,16},{16,8},{24,0},{1,25},{9,17},{17,9},{25,1},{2,26},{10... | collective-permute-start | bytes 24584 | tf_op jit(solution)/shard_map/ppermute | solution.py:257
  2.4 0.6 %collective-permute-start.1 = (f32[16,128]{1,0:T(8,128)}, f32[16,128]{1,0:T(8,128)S(1)}, u32[]{:S(2)}, u32[]{:S(2)}) collective-permute-start(f32[16,128]{1,0:T(8,128)} %bitcast.3), channel_id=1, source_target_pairs={{0,16},{8,24},{16,0},{24,8},{1,17},{9,25},{17,1},{25,9},{2,18},{10... | collective-permute-start | bytes 24584 | tf_op jit(solution)/shard_map/ppermute | solution.py:257
  3.0 0.0 collective-permute-start
  3.1 2.9 %shard_map.37.split_ref = bf16[12288,256]{1,0:T(8,128)(2,1)S(1)} custom-call(f32[512,32,128]{2,1,0:T(8,128)} %bitcast.6), custom_call_target="tpu_custom_call" | custom-call | flops 1000000000 | bytes 20971520 | tf_op jit(solution)/shard_map/pallas_call | solution.py:226
  6.0 0.0 collective-permute-done.2.refs_3_
  6.0 0.2 collective-permute-done.1.refs_2_
  6.3 0.0 collective-permute-done.refs_1_
  6.3 0.0 copy-done.1
  6.3 0.0 copy-done
  6.3 2.0 %shard_map.38 = (f32[96,128]{1,0:T(8,128)S(1)}, f32[96,128]{1,0:T(8,128)S(1)}, f32[96,128]{1,0:T(8,128)S(1)}, f32[32,128]{1,0:T(8,128)S(1)}, bf16[256,128]{1,0:T(8,128)(2,1)S(1)}) custom-call(bf16[12288,256]{1,0:T(8,128)(2,1)S(1)} %shard_map.37.split_ref, f32[32,64]{1,0:T(8,128)S(1)} %copy-done, f32[16,128]{1,0:T(8,128)S(1)} %bitcast.5, ...), custom_call_target="tpu_custom_call" | custom-call | flops 2000000000 | bytes 12918784 | tf_op jit(solution)/shard_map/pallas_call | solution.py:226
  8.3 2.5 %collective-permute-start.3 = (f32[96,128]{1,0:T(8,128)S(1)}, f32[96,128]{1,0:T(8,128)S(1)}, u32[]{:S(2)}, u32[]{:S(2)}) collective-permute-start(f32[96,128]{1,0:T(8,128)S(1)} %get-tuple-element.17), channel_id=1, source_target_pairs={{0,3},{1,2},{2,1},{3,0},{4,7},{5,6},{6,5},{7,4},{8,11},{9,10},{10,... | collective-permute-start | bytes 147464 | tf_op jit(solution)/shard_map/ppermute | solution.py:279
  10.8 0.5 %collective-permute-start.4 = (f32[96,128]{1,0:T(8,128)S(1)}, f32[96,128]{1,0:T(8,128)S(1)}, u32[]{:S(2)}, u32[]{:S(2)}) collective-permute-start(f32[96,128]{1,0:T(8,128)S(1)} %get-tuple-element.18), channel_id=1, source_target_pairs={{0,2},{1,3},{2,0},{3,1},{4,6},{5,7},{6,4},{7,5},{8,10},{9,11},{10,... | collective-permute-start | bytes 147464 | tf_op jit(solution)/shard_map/ppermute | solution.py:279
  11.3 0.5 %collective-permute-start.5 = (f32[96,128]{1,0:T(8,128)S(1)}, f32[96,128]{1,0:T(8,128)S(1)}, u32[]{:S(2)}, u32[]{:S(2)}) collective-permute-start(f32[96,128]{1,0:T(8,128)S(1)} %get-tuple-element.19), channel_id=1, source_target_pairs={{0,1},{1,0},{2,3},{3,2},{4,5},{5,4},{6,7},{7,6},{8,9},{9,8},{10,11... | collective-permute-start | bytes 147464 | tf_op jit(solution)/shard_map/ppermute | solution.py:279
  11.8 2.5 %shard_map.39 = (f32[96,128]{1,0:T(8,128)S(1)}, f32[32,128]{1,0:T(8,128)S(1)}) custom-call(f32[512,32,128]{2,1,0:T(8,128)} %bitcast.7, bf16[256,128]{1,0:T(8,128)(2,1)S(1)} %get-tuple-element.14.weight_ref, f32[32,64]{1,0:T(8,128)S(1)} %copy-done, f32[32,128]{1,0:T(8,128)S(1)} %get-tuple-element.15.gram_ref), custom_call_target="tpu_custom_call" | custom-call | flops 2000000000 | bytes 8609792 | tf_op jit(solution)/shard_map/pallas_call | solution.py:226
  14.3 0.0 collective-permute-done.3.refs_1_
  14.3 0.6 %collective-permute-done.4.refs_2_ = f32[96,128]{1,0:T(8,128)S(1)} collective-permute-done((f32[96,128]{1,0:T(8,128)S(1)}, f32[96,128]{1,0:T(8,128)S(1)}, u32[]{:S(2)}, u32[]{:S(2)}) %collective-permute-start.4) | collective-permute-done | bytes 49184 | tf_op jit(solution)/shard_map/ppermute | solution.py:279
  14.9 0.5 %collective-permute-done.5.refs_3_ = f32[96,128]{1,0:T(8,128)S(1)} collective-permute-done((f32[96,128]{1,0:T(8,128)S(1)}, f32[96,128]{1,0:T(8,128)S(1)}, u32[]{:S(2)}, u32[]{:S(2)}) %collective-permute-start.5) | collective-permute-done | bytes 49184 | tf_op jit(solution)/shard_map/ppermute | solution.py:279
  15.4 2.7 %collective-permute-start.6 = (f32[64,128]{1,0:T(8,128)S(1)}, f32[64,128]{1,0:T(8,128)S(1)}, u32[]{:S(2)}, u32[]{:S(2)}) collective-permute-start(f32[64,128]{1,0:T(8,128)S(1)} %get-tuple-element.21), channel_id=1, source_target_pairs={{0,4},{1,5},{2,6},{3,7},{4,0},{5,1},{6,2},{7,3},{8,12},{9,13},{10,... | collective-permute-start | bytes 98312 | tf_op jit(solution)/shard_map/ppermute | solution.py:295
  18.0 2.2 %collective-permute-done.6.refs_1_ = f32[64,128]{1,0:T(8,128)S(1)} collective-permute-done((f32[64,128]{1,0:T(8,128)S(1)}, f32[64,128]{1,0:T(8,128)S(1)}, u32[]{:S(2)}, u32[]{:S(2)}) %collective-permute-start.6) | collective-permute-done | bytes 32800 | tf_op jit(solution)/shard_map/ppermute | solution.py:295
  20.3 2.4 %shard_map.41 = f32[64,64]{1,0:T(8,128)} custom-call(f32[64,128]{1,0:T(8,128)S(1)} %get-tuple-element.20.refs_0_, f32[64,128]{1,0:T(8,128)S(1)} %collective-permute-done.6.refs_1_, f32[32,128]{1,0:T(8,128)S(1)} %get-tuple-element.22.refs_2_), custom_call_target="tpu_custom_call" | custom-call | flops 100000000 | bytes 98304 | tf_op jit(solution)/shard_map/pallas_call | solution.py:226
  (1 shorter events, 0.0 us)
Async XLA Ops:
  0.0 6.3 %copy-start.1 = (f32[128,16]{0,1:T(8,128)S(1)}, f32[128,16]{0,1:T(8,128)}, u32[]{:S(2)}) copy-start(f32[128,16]{0,1:T(8,128)} %param.4) | copy-start | bytes 24580
  0.0 6.3 %copy-start = (f32[32,64]{1,0:T(8,128)S(1)}, f32[32,64]{1,0:T(8,128)}, u32[]{:S(2)}) copy-start(f32[32,64]{1,0:T(8,128)} %three_ref.3) | copy-start | bytes 24580
  0.0 6.0 %collective-permute-start.2 = (f32[16,128]{1,0:T(8,128)}, f32[16,128]{1,0:T(8,128)S(1)}, u32[]{:S(2)}, u32[]{:S(2)}) collective-permute-start(f32[16,128]{1,0:T(8,128)} %bitcast.2), channel_id=1, source_target_pairs={{0,24},{8,16},{16,8},{24,0},{1,25},{9,17},{17,9},{25,1},{2,26},{10... | collective-permute-start | bytes 24584 | tf_op jit(solution)/shard_map/ppermute | solution.py:257
  2.4 3.9 %collective-permute-start.1 = (f32[16,128]{1,0:T(8,128)}, f32[16,128]{1,0:T(8,128)S(1)}, u32[]{:S(2)}, u32[]{:S(2)}) collective-permute-start(f32[16,128]{1,0:T(8,128)} %bitcast.3), channel_id=1, source_target_pairs={{0,16},{8,24},{16,0},{24,8},{1,17},{9,25},{17,1},{25,9},{2,18},{10... | collective-permute-start | bytes 24584 | tf_op jit(solution)/shard_map/ppermute | solution.py:257
  3.0 3.2 %collective-permute-start = (f32[16,128]{1,0:T(8,128)}, f32[16,128]{1,0:T(8,128)S(1)}, u32[]{:S(2)}, u32[]{:S(2)}) collective-permute-start(f32[16,128]{1,0:T(8,128)} %bitcast.4), channel_id=1, source_target_pairs={{0,8},{8,0},{16,24},{24,16},{1,9},{9,1},{17,25},{25,17},{2,10},{10... | collective-permute-start | bytes 24584 | tf_op jit(solution)/shard_map/ppermute | solution.py:257
  8.3 6.0 %collective-permute-start.3 = (f32[96,128]{1,0:T(8,128)S(1)}, f32[96,128]{1,0:T(8,128)S(1)}, u32[]{:S(2)}, u32[]{:S(2)}) collective-permute-start(f32[96,128]{1,0:T(8,128)S(1)} %get-tuple-element.17), channel_id=1, source_target_pairs={{0,3},{1,2},{2,1},{3,0},{4,7},{5,6},{6,5},{7,4},{8,11},{9,10},{10,... | collective-permute-start | bytes 147464 | tf_op jit(solution)/shard_map/ppermute | solution.py:279
  10.8 4.1 %collective-permute-start.4 = (f32[96,128]{1,0:T(8,128)S(1)}, f32[96,128]{1,0:T(8,128)S(1)}, u32[]{:S(2)}, u32[]{:S(2)}) collective-permute-start(f32[96,128]{1,0:T(8,128)S(1)} %get-tuple-element.18), channel_id=1, source_target_pairs={{0,2},{1,3},{2,0},{3,1},{4,6},{5,7},{6,4},{7,5},{8,10},{9,11},{10,... | collective-permute-start | bytes 147464 | tf_op jit(solution)/shard_map/ppermute | solution.py:279
  11.3 4.1 %collective-permute-start.5 = (f32[96,128]{1,0:T(8,128)S(1)}, f32[96,128]{1,0:T(8,128)S(1)}, u32[]{:S(2)}, u32[]{:S(2)}) collective-permute-start(f32[96,128]{1,0:T(8,128)S(1)} %get-tuple-element.19), channel_id=1, source_target_pairs={{0,1},{1,0},{2,3},{3,2},{4,5},{5,4},{6,7},{7,6},{8,9},{9,8},{10,11... | collective-permute-start | bytes 147464 | tf_op jit(solution)/shard_map/ppermute | solution.py:279
  15.4 4.9 %collective-permute-start.6 = (f32[64,128]{1,0:T(8,128)S(1)}, f32[64,128]{1,0:T(8,128)S(1)}, u32[]{:S(2)}, u32[]{:S(2)}) collective-permute-start(f32[64,128]{1,0:T(8,128)S(1)} %get-tuple-element.21), channel_id=1, source_target_pairs={{0,4},{1,5},{2,6},{3,7},{4,0},{5,1},{6,2},{7,3},{8,12},{9,13},{10,... | collective-permute-start | bytes 98312 | tf_op jit(solution)/shard_map/ppermute | solution.py:295
